TPU v7x, 256 devices: a whole 4x4x8 slice. The times are simulated.
256 devices in a mesh: lat: 16 (over z, x_lo), lon: 16 (over y, x_hi, core).
Axes of the slice: x: 4 (x_hi: 2, x_lo: 2; x = x_hi * 2 + x_lo), y: 4, z: 8, core: 2. Of those that a mesh axis runs over, the one named last changes fastest.
Arguments:
- state: bfloat16 [2, 96, 384, 192], P(None, 'lat', 'lon'), may hold values from -6 to 6
- out_cot: bfloat16 [2, 96, 384, 192], P(None, 'lat', 'lon'), may hold values from -6 to 6
- qkv_weight: bfloat16 [2, 192, 576], replicated, may hold values from -0.4375 to 0.4375
- proj_weight: bfloat16 [2, 192, 192], replicated, may hold values from -0.4375 to 0.4375
- fc1_weight: bfloat16 [2, 192, 768], replicated, may hold values from -0.4375 to 0.4375
- fc2_weight: bfloat16 [2, 768, 192], replicated, may hold values from -0.21875 to 0.21875
- norm_gain: float32 [2, 2, 192], replicated, may hold values from 0.5 to 1.5
- bias_table: float32 [2, 16, 1, 6, 3312], P(None, 'lat'), may hold values from -3 to 303
Outputs:
- state_grad: float32 [2, 96, 384, 192], P(None, 'lat', 'lon')
- qkv_grad: float32 [2, 192, 576], P(None, 'lat', 'lon')
- proj_grad: float32 [2, 192, 192], P(None, 'lat', 'lon')
- fc1_grad: float32 [2, 192, 768], P(None, 'lat', 'lon')
- fc2_grad: float32 [2, 768, 192], P(None, 'lat', 'lon')
- norm_gain_grad: float32 [2, 2, 192], replicated
- bias_table_grad: float32 [2, 16, 1, 6, 3312], P(None, 'lat', None, None, 'lon')
All inputs are finite; a program needn't handle non-finite values.
Results may differ from a plain program's by a relative error of at most 0.028.
Values may be sent and summed in bfloat16 or wider, within the bound.
A program may use at most 128 MiB of HBM per device.

v0:
```python
import jax
import jax.numpy as jnp
from jax import lax
from jax.sharding import Mesh
from jax.sharding import PartitionSpec as P

WZ = 2
WH = 6
WW = 12
LAT = ("lat_0", "lat_1")
LON = ("lon_0", "lon_1", "lon_2")
LAT_LON = ("lat_0", "lat_1", "lon_0", "lon_1", "lon_2")


def from_behind(value, axis, steps):
    count = lax.axis_size(axis)
    pairs = [(source, (source + steps) % count) for source in range(count)]
    return lax.ppermute(value, axis, pairs)


def as_sent(array):

    def short(part):
        return part.astype(jnp.bfloat16) if part.dtype == jnp.float32 else part

    return jax.tree.map(short, array)


def split_up(array, dim, count):
    dims = array.shape
    parts = array.reshape(*dims[:dim], count, dims[dim] // count, *dims[dim + 1 :])
    return jnp.moveaxis(parts, dim, 0)


def sent_and_summed(array, axis, dim):
    count = lax.axis_size(axis)
    parts = lax.all_to_all(split_up(array, dim, count), axis, 0, 0, tiled=True)
    return jnp.sum(parts.astype(jnp.float32), axis=0)


def by_axis(array, axes):
    for axis in axes:
        array = lax.psum(array, axis)
    return array


def position_index():
    tokens = jnp.arange(WZ * WH * WW, dtype=jnp.int32)
    level_in = tokens // (WH * WW)
    row_in = tokens // WW % WH
    column_in = tokens % WW
    level_part = (level_in[:, None] * WZ + level_in[None, :]) * (WH * WH * (2 * WW - 1))
    row_part = (row_in[:, None] * WH + row_in[None, :]) * (2 * WW - 1)
    return level_part + row_part + column_in[:, None] - column_in[None, :] + WW - 1


def shifted_labels(lat_windows, level_windows, lat_start, lat_total):
    tokens = jnp.arange(WZ * WH * WW, dtype=jnp.int32)
    level_in = tokens // (WH * WW)
    row_in = tokens // WW % WH
    global_level = (
        jnp.arange(level_windows, dtype=jnp.int32)[None, :, None] * WZ + level_in[None, None, :]
    )
    global_row = (
        lat_start
        + jnp.arange(lat_windows, dtype=jnp.int32)[:, None, None] * WH
        + row_in[None, None, :]
    )
    level_mark = (global_level >= level_windows * WZ - 1).astype(jnp.int32)
    row_mark = (global_row >= lat_total - WH // 2).astype(jnp.int32)
    return 2 * level_mark + row_mark


def to_windows(brick):
    levels, rows, columns, model_width = brick.shape
    shaped = brick.reshape(levels // WZ, WZ, rows // WH, WH, columns // WW, WW, model_width)
    shaped = shaped.transpose(2, 0, 4, 1, 3, 5, 6)
    return shaped.reshape(rows // WH, levels // WZ, columns // WW, WZ * WH * WW, model_width)


def from_windows(windows):
    lat_windows, level_windows, lon_windows, window_size, model_width = windows.shape
    shaped = windows.reshape(lat_windows, level_windows, lon_windows, WZ, WH, WW, model_width)
    shaped = shaped.transpose(1, 3, 0, 4, 2, 5, 6)
    return shaped.reshape(level_windows * WZ, lat_windows * WH, lon_windows * WW, model_width)


def layer_norm(values, gain):
    average = jnp.mean(values, -1, keepdims=True)
    centred = values - average
    variance = jnp.mean(centred * centred, -1, keepdims=True)
    return centred * lax.rsqrt(variance + 1e-05) * gain


def rounded(values):
    return lax.optimization_barrier(values.astype(jnp.bfloat16)).astype(jnp.float32)


def run_block(values, gain_pair, table_part, offsets, labels, weights):
    w_qkv, w_proj, w_fc1, w_fc2 = weights
    head_count = table_part.shape[2]
    model_width = values.shape[-1]
    head_size = model_width // head_count
    normed = layer_norm(values, gain_pair[0]).astype(jnp.bfloat16)
    qkv_out = jnp.dot(normed, w_qkv, preferred_element_type=jnp.float32) + offsets[0]
    projected = rounded(qkv_out).reshape(values.shape[:-1] + (3, head_count, head_size))
    queries = projected[..., 0, :, :]
    key_vectors = projected[..., 1, :, :]
    value_vectors = projected[..., 2, :, :]
    scores = jnp.einsum("abcqhd,abckhd->abchqk", queries, key_vectors) * head_size ** (-0.5)
    bias_full = jnp.take(table_part, position_index(), axis=3)
    allowed = (labels[:, :, :, None] == labels[:, :, None, :])[:, :, None, None]
    scores = jnp.where(allowed, scores + bias_full[:, :, None], -1e30)
    attention = rounded(jax.nn.softmax(scores, axis=-1))
    attended = jnp.einsum("abchqk,abckhd->abcqhd", attention, value_vectors).reshape(values.shape)
    joined = attended.astype(jnp.bfloat16)
    middle = values + jnp.dot(joined, w_proj, preferred_element_type=jnp.float32) + offsets[1]
    normed_two = layer_norm(middle, gain_pair[1]).astype(jnp.bfloat16)
    expanded = jnp.dot(normed_two, w_fc1, preferred_element_type=jnp.float32) + offsets[2]
    hidden = jax.nn.gelu(expanded, approximate=False).astype(jnp.bfloat16)
    result = middle + jnp.dot(hidden, w_fc2, preferred_element_type=jnp.float32) + offsets[3]
    return (result, (normed, joined, normed_two, hidden))


def open_block(values, gain_pair, table_part, labels, weights):
    lead = values.shape[:-1]
    model_width = values.shape[-1]
    offsets = (
        jnp.zeros(lead + (3 * model_width,), jnp.float32),
        jnp.zeros(lead + (model_width,), jnp.float32),
        jnp.zeros(lead + (weights[2].shape[1],), jnp.float32),
        jnp.zeros(lead + (model_width,), jnp.float32),
    )

    def forward(inputs, gains_in, table_in, offsets_in):
        return run_block(inputs, gains_in, table_in, offsets_in, labels, weights)

    return jax.vjp(forward, values, gain_pair, table_part, offsets, has_aux=True)


def close_block(pullback, stored, cotangent):
    value_grad, gain_grad, table_grad, output_grads = pullback(cotangent)
    weight_grads = tuple(
        (
            lax.dot_general(
                inputs_act.reshape(-1, inputs_act.shape[-1]),
                grad_out.reshape(-1, grad_out.shape[-1]).astype(jnp.bfloat16),
                (((0,), (0,)), ((), ())),
                preferred_element_type=jnp.float32,
            )
            for inputs_act, grad_out in zip(stored, output_grads)
        )
    )
    return (value_grad, weight_grads, gain_grad, table_grad)


def body(state, out_cot, qkv_weight, proj_weight, fc1_weight, fc2_weight, norm_gain, bias_table):
    matrices = (qkv_weight, proj_weight, fc1_weight, fc2_weight)
    first_weights = tuple((w[0] for w in matrices))
    second_weights = tuple((w[1] for w in matrices))
    half_lat = WH // 2
    half_lon = WW // 2
    lat_rows = state.shape[1]
    lat_windows = lat_rows // WH
    level_windows = state.shape[0] // WZ
    windows_in = to_windows(state.astype(jnp.float32))
    unmasked = jnp.zeros((lat_windows, level_windows, WZ * WH * WW), jnp.int32)
    first_out, first_pull, first_inputs = open_block(
        windows_in, norm_gain[0], bias_table[0], unmasked, first_weights
    )
    state_one = from_windows(first_out).astype(jnp.bfloat16)
    paired = jnp.stack((state_one, out_cot))
    arrived = from_behind(paired[:, :, :half_lat], LAT, -1)
    paired = jnp.concatenate((paired[:, :, half_lat:], arrived), 2)
    arrived = from_behind(paired[:, :, :, :half_lon], LON, -1)
    paired = jnp.roll(jnp.concatenate((paired[:, :, :, half_lon:], arrived), 3), -(WZ // 2), 1)
    rolled = paired[0]
    cot_rolled = paired[1]
    lat_start = lax.axis_index(LAT) * lat_rows
    lat_total = lat_rows * lax.axis_size(LAT)
    shifted = shifted_labels(lat_windows, level_windows, lat_start, lat_total)
    both_windows = to_windows(jnp.concatenate((rolled, cot_rolled), 3).astype(jnp.float32))
    model_width = state.shape[-1]
    second_out, second_pull, second_inputs = open_block(
        both_windows[..., :model_width], norm_gain[1], bias_table[1], shifted, second_weights
    )
    rolled_grad, second_grads, second_gains, second_table = close_block(
        second_pull, second_inputs, both_windows[..., model_width:]
    )
    returned = jnp.roll(from_windows(rolled_grad), WZ // 2, 0)
    arrived = from_behind(as_sent(returned[:, :, -half_lon:]), LON, 1)
    returned = jnp.concatenate((arrived, returned[:, :, :-half_lon]), 2)
    arrived = from_behind(as_sent(returned[:, -half_lat:]), LAT, 1)
    returned = jnp.concatenate((arrived, returned[:, :-half_lat]), 1)
    state_grad, first_grads, first_gains, first_table = close_block(
        first_pull, first_inputs, to_windows(returned)
    )
    stacked = tuple((jnp.stack((left, right)) for left, right in zip(first_grads, second_grads)))
    partial_sums = (
        lax.psum_scatter(
            stacked[0].astype(jnp.bfloat16), LON, scatter_dimension=2, tiled=True
        ).astype(jnp.float32),
        lax.psum_scatter(
            stacked[1].astype(jnp.bfloat16), LON, scatter_dimension=2, tiled=True
        ).astype(jnp.float32),
        lax.psum_scatter(
            stacked[2].astype(jnp.bfloat16), LON, scatter_dimension=2, tiled=True
        ).astype(jnp.float32),
        lax.psum_scatter(
            stacked[3].astype(jnp.bfloat16), LON, scatter_dimension=2, tiled=True
        ).astype(jnp.float32),
    )
    summed = (
        sent_and_summed(partial_sums[0].astype(jnp.bfloat16), LAT, 1),
        sent_and_summed(partial_sums[1].astype(jnp.bfloat16), LAT, 1),
        sent_and_summed(partial_sums[2].astype(jnp.bfloat16), LAT, 1),
        sent_and_summed(partial_sums[3].astype(jnp.bfloat16), LAT, 1),
    )
    table_grad = sent_and_summed(
        jnp.stack((first_table, second_table)).astype(jnp.bfloat16), LON, 4
    )
    gain_grad = by_axis(jnp.stack((first_gains, second_gains)), LAT_LON)
    return (
        from_windows(state_grad),
        summed[0],
        summed[1],
        summed[2],
        summed[3],
        gain_grad,
        table_grad,
    )


def solution(mesh):
    split = Mesh(mesh.devices.reshape(8, 2, 4, 2, 2), ("lat_0", "lat_1", "lon_0", "lon_1", "lon_2"))
    placed = (
        P(None, LAT, LON, None),
        P(None, LAT, LON, None),
        P(),
        P(),
        P(),
        P(),
        P(),
        P(None, LAT, None, None, None),
    )
    return jax.shard_map(
        body,
        mesh=split,
        in_specs=placed,
        out_specs=(
            P(None, LAT, LON, None),
            P(None, LAT, LON),
            P(None, LAT, LON),
            P(None, LAT, LON),
            P(None, LAT, LON),
            P(),
            P(None, LAT, None, None, LON),
        ),
        check_vma=False,
    )
```

profile of v0, /device:TPU:2, one launch (start us, length us, event | category | flops | bytes accessed | tf_op | source)
XLA Modules:
  0.0 600.1 jit_solution(2246142359874101578)
XLA Ops:
  20.8 38.8 %gather_fusion = f32[20736,6]{1,0:T(8,128)} fusion(f32[6,3312]{0,1:T(8,128)S(1)} %bitcast.496, s32[21504]{0:T(1024)S(1)} %pad_clamp_fusion), kind=kCustom, calls=%fused_computation.clone | custom fusion | bytes 1078272 | tf_op jit(solution)/shard_map/jvp(jit(_take))/gather | solution.py:111
  59.6 11.6 %copy.428 = f32[144,144,6]{0,1,2:T(8,128)S(1)} copy(f32[144,144,6]{2,1,0:T(8,128)} %bitcast.498) | data formatting | bytes 995328 | tf_op jit(solution)/shard_map/jvp(jit(_take))/gather | solution.py:111
  71.2 38.7 %gather_fusion.1 = f32[20736,6]{1,0:T(8,128)} fusion(f32[6,3312]{0,1:T(8,128)S(1)} %bitcast.495, s32[21504]{0:T(1024)S(1)} %pad_clamp_fusion), kind=kCustom, calls=%fused_computation.1.clone | custom fusion | bytes 1078272 | tf_op jit(solution)/shard_map/jvp(jit(_take))/gather | solution.py:111
  109.9 11.6 %copy.443 = f32[144,144,6]{0,1,2:T(8,128)S(1)} copy(f32[144,144,6]{2,1,0:T(8,128)} %bitcast.497) | data formatting | bytes 995328 | tf_op jit(solution)/shard_map/jvp(jit(_take))/gather | solution.py:111
  156.9 3.4 fusion.193
  183.8 5.4 collective-permute-done.2
  193.1 5.9 collective-permute-done.3
  222.9 3.1 copy.483
  244.3 11.2 %copy.516 = f32[144,144,6]{2,1,0:T(8,128)} copy(f32[144,144,6]{0,1,2:T(8,128)} %bitcast.515) | data formatting | bytes 995328 | tf_op jit(solution)/shard_map/transpose(jvp())/broadcast_in_dim | solution.py:113
  255.5 112.8 %scatter_custom_fusion.1 = f32[6,3312]{0,1:T(8,128)S(1)} fusion(s32[20736]{0:T(1024)} %reshape.1243, f32[20736,6]{1,0:T(8,128)} %bitcast.500, f32[]{:T(128)} %constant.73.clone.1), kind=kCustom, calls=%fused_computation.152 | custom fusion | flops 124416 | bytes 80000 | tf_op jit(solution)/shard_map/transpose(jvp(jit(_take)))/scatter-add | solution.py:111
  369.0 10.4 %copy.515 = f32[144,144,6]{2,1,0:T(8,128)} copy(f32[144,144,6]{0,1,2:T(8,128)S(1)} %bitcast.514) | data formatting | bytes 995328 | tf_op jit(solution)/shard_map/transpose(jvp())/broadcast_in_dim | solution.py:113
  379.4 113.0 %scatter_custom_fusion = f32[6,3312]{0,1:T(8,128)S(1)} fusion(s32[20736]{0:T(1024)} %reshape.1243, f32[20736,6]{1,0:T(8,128)} %bitcast.499, f32[]{:T(128)} %constant.73.clone.1), kind=kCustom, calls=%fused_computation.154 | custom fusion | flops 124416 | bytes 80000 | tf_op jit(solution)/shard_map/transpose(jvp(jit(_take)))/scatter-add | solution.py:111
  493.9 3.5 all-to-all-start.4
  497.5 16.5 %psum.35 = f32[2,2,192]{2,1,0:T(2,128)S(1)} all-reduce(f32[2,2,192]{2,1,0:T(2,128)S(1)} %pad_maximum_fusion.9), channel_id=1, replica_groups=mesh['lat_0'=8,'lat_1'=2,'lon_0'=4,'lon_1'=2,'lon_2'=2] {'lat_0'}, use_global_device_ids=true, to_apply=%region_34.36 | all-reduce | flops 768 | bytes 6144 | tf_op jit(solution)/shard_map/psum | solution.py:43
  513.9 4.9 psum.36
  518.9 10.8 %psum.37 = f32[2,2,192]{2,1,0:T(2,128)S(1)} all-reduce(f32[2,2,192]{2,1,0:T(2,128)S(1)} %psum.36), channel_id=1, replica_groups=mesh['lat_0'=8,'lat_1'=2,'lon_0'=4,'lon_1'=2,'lon_2'=2] {'lon_0'}, use_global_device_ids=true, to_apply=%region_36.38 | all-reduce | flops 768 | bytes 6144 | tf_op jit(solution)/shard_map/psum | solution.py:43
  529.7 6.4 %psum.38 = f32[2,2,192]{2,1,0:T(2,128)S(1)} all-reduce(f32[2,2,192]{2,1,0:T(2,128)S(1)} %psum.37), channel_id=1, replica_groups=mesh['lat_0'=8,'lat_1'=2,'lon_0'=4,'lon_1'=2,'lon_2'=2] {'lon_1'}, use_global_device_ids=true, to_apply=%region_37.39 | all-reduce | flops 768 | bytes 6144 | tf_op jit(solution)/shard_map/psum | solution.py:43
  542.3 5.2 all-to-all-start.1
  554.8 5.4 all-to-all-start
  561.5 6.1 %all-to-all-done = bf16[16,2,432]{2,1,0:T(2,128)(2,1)S(1)} async-done(((bf16[16,2,432]{2,1,0:T(2,128)(2,1)}), bf16[16,2,432]{2,1,0:T(2,128)(2,1)S(1)}, u32[]{:S(2)}, u32[]{:S(2)}) %all-to-all-start) | async-done | bytes 27680 | tf_op jit(solution)/shard_map/all_to_all | solution.py:37
  567.6 4.7 all-to-all-start.2
  573.2 6.7 %all-to-all-done.2 = bf16[16,2,576]{2,1,0:T(2,128)(2,1)S(1)} async-done(((bf16[16,2,576]{2,1,0:T(2,128)(2,1)}), bf16[16,2,576]{2,1,0:T(2,128)(2,1)S(1)}, u32[]{:S(2)}, u32[]{:S(2)}) %all-to-all-start.2) | async-done | bytes 36896 | tf_op jit(solution)/shard_map/all_to_all | solution.py:37
  579.9 4.7 all-to-all-start.3
  585.5 6.7 %all-to-all-done.3 = bf16[16,2,576]{2,1,0:T(2,128)(2,1)S(1)} async-done(((bf16[16,2,576]{2,1,0:T(2,128)(2,1)}), bf16[16,2,576]{2,1,0:T(2,128)(2,1)S(1)}, u32[]{:S(2)}, u32[]{:S(2)}) %all-to-all-start.3) | async-done | bytes 36896 | tf_op jit(solution)/shard_map/all_to_all | solution.py:37
  (366 shorter events, 134.7 us)
Async XLA Ops:
  7.2 532.6 %all-reduce.17.cloned.1.call-start = ((), (), s32[]{:S(2)}) async-start(), calls=%async_computation.5 | async-start | bytes 4325376
  9.6 7.2 %copy-start.74 = (f32[1,1,192]{2,1,0:T(1,128)}, f32[1,1,192]{2,1,0:T(1,128)S(1)}, u32[]{:S(2)}) copy-start(f32[1,1,192]{2,1,0:T(1,128)S(1)} %get-tuple-element.97) | copy-start | bytes 2308
  9.6 117.8 %copy-start.70 = (f32[1,1,192]{2,1,0:T(1,128)}, f32[1,1,192]{2,1,0:T(1,128)S(1)}, u32[]{:S(2)}) copy-start(f32[1,1,192]{2,1,0:T(1,128)S(1)} %get-tuple-element.96) | copy-start | bytes 2308
  130.9 15.6 %copy-start.8 = (bf16[2,144,768]{2,1,0:T(8,128)(2,1)}, bf16[2,144,768]{2,1,0:T(8,128)(2,1)S(1)}, u32[]{:S(2)}) copy-start(bf16[2,144,768]{2,1,0:T(8,128)(2,1)S(1)} %get-tuple-element.77) | copy-start | bytes 1327108
  130.9 6.1 %copy-start.23 = (bf16[1,1,2,2,6,12,192]{6,3,5,2,4,0,1:T(2,128)(2,1)S(1)}, bf16[1,1,2,2,6,12,192]{6,3,5,2,4,0,1:T(2,128)(2,1)}, u32[]{:S(2)}) copy-start(bf16[1,1,2,2,6,12,192]{6,3,5,2,4,0,1:T(2,128)(2,1)} %copy-done.22) | copy-start | bytes 331780
  130.9 10.0 %copy-start.34 = (s32[144,144,1]{1,0,2:T(8,128)S(1)}, s32[144,144,1]{1,0,2:T(8,128)}, u32[]{:S(2)}) copy-start(s32[144,144,1]{1,0,2:T(8,128)} %get-tuple-element.93) | copy-start | bytes 248836
  132.6 14.8 %collective-permute-start = (bf16[2,2,3,24,192]{4,1,3,2,0:T(2,128)(2,1)}, bf16[2,2,3,24,192]{4,1,3,2,0:T(2,128)(2,1)}, u32[]{:S(2)}, u32[]{:S(2)}) collective-permute-start(bf16[2,2,3,24,192]{4,1,3,2,0:T(2,128)(2,1)} %get-tuple-element.84), channel_id=1, source_target_pairs={{0,240},{16,0},{32,16},{48,32},{64,48},{80,64},{96,80},{112,96},{1... | collective-permute-start | bytes 331784 | tf_op jit(solution)/shard_map/ppermute | solution.py:18
  148.3 4.6 collective-permute-start.1
  164.6 5.8 copy-start.55
  181.6 10.7 %copy-start.32 = (bf16[1,1,2,144,192]{4,3,2,1,0:T(8,128)(2,1)S(1)}, bf16[1,1,2,144,192]{4,3,2,1,0:T(8,128)(2,1)}, u32[]{:S(2)}) copy-start(bf16[1,1,2,144,192]{4,3,2,1,0:T(8,128)(2,1)} %get-tuple-element.75) | copy-start | bytes 331780
  182.0 7.1 %collective-permute-start.2 = (bf16[2,6,6,192]{3,0,2,1:T(2,128)(2,1)S(1)}, bf16[2,6,6,192]{3,0,2,1:T(2,128)(2,1)S(1)}, u32[]{:S(2)}, u32[]{:S(2)}) collective-permute-start(bf16[2,6,6,192]{3,0,2,1:T(2,128)(2,1)S(1)} %fusion.149), channel_id=1, source_target_pairs={{0,1},{1,2},{2,3},{3,4},{4,5},{5,6},{6,7},{7,8},{8,9},{9,10},{10,1... | collective-permute-start | bytes 82952 | tf_op jit(solution)/shard_map/ppermute | solution.py:18
  183.7 16.4 %copy-start.27 = (f32[2,144,768]{2,1,0:T(8,128)S(1)}, f32[2,144,768]{2,1,0:T(8,128)}, u32[]{:S(2)}) copy-start(f32[2,144,768]{2,1,0:T(8,128)} %copy-done.26) | copy-start | bytes 2654212
  183.7 16.4 %copy-start.28 = (f32[2,144,768]{2,1,0:T(8,128)S(1)}, f32[2,144,768]{2,1,0:T(8,128)}, u32[]{:S(2)}) copy-start(f32[2,144,768]{2,1,0:T(8,128)} %get-tuple-element.78) | copy-start | bytes 2654212
  183.8 16.4 %copy-start.50 = (bf16[2,768,192]{1,2,0:T(8,128)(2,1)S(1)}, bf16[2,768,192]{1,2,0:T(8,128)(2,1)}, u32[]{:S(2)}) copy-start(bf16[2,768,192]{1,2,0:T(8,128)(2,1)} %param.15) | copy-start | bytes 1769476
  189.5 9.5 %collective-permute-start.3 = (bf16[2,3,24,192]{3,0,2,1:T(2,128)(2,1)S(1)}, bf16[2,3,24,192]{3,0,2,1:T(2,128)(2,1)S(1)}, u32[]{:S(2)}, u32[]{:S(2)}) collective-permute-start(bf16[2,3,24,192]{3,0,2,1:T(2,128)(2,1)S(1)} %slice.349), channel_id=1, source_target_pairs={{0,16},{16,32},{32,48},{48,64},{64,80},{80,96},{96,112},{112,128},... | collective-permute-start | bytes 165896 | tf_op jit(solution)/shard_map/ppermute | solution.py:18
  379.4 118.0 %copy-start.79 = (f32[192]{0:T(256)S(1)}, f32[192]{0:T(256)}, u32[]{:S(2)}) copy-start(f32[192]{0:T(256)} %get-tuple-element.67) | copy-start | bytes 2308
  379.4 118.0 %copy-start.80 = (f32[192]{0:T(256)S(1)}, f32[192]{0:T(256)}, u32[]{:S(2)}) copy-start(f32[192]{0:T(256)} %get-tuple-element.61) | copy-start | bytes 2308
  379.4 118.0 %copy-start.81 = (f32[192]{0:T(256)S(1)}, f32[192]{0:T(256)}, u32[]{:S(2)}) copy-start(f32[192]{0:T(256)} %get-tuple-element.63) | copy-start | bytes 2308
  379.4 118.0 %copy-start.82 = (f32[192]{0:T(256)S(1)}, f32[192]{0:T(256)}, u32[]{:S(2)}) copy-start(f32[192]{0:T(256)} %get-tuple-element.65) | copy-start | bytes 2308
  493.9 45.3 %all-to-all-start.4 = ((bf16[16,2,1,1,6,207]{5,1,4,3,2,0:T(2,128)(2,1)}), bf16[16,2,1,1,6,207]{5,1,4,3,2,0:T(2,128)(2,1)S(1)}, u32[]{:S(2)}, u32[]{:S(2)}) async-start(bf16[16,2,1,1,6,207]{5,1,4,3,2,0:T(2,128)(2,1)} %copy.494), calls=%async_computation.4 | async-start | bytes 196608 | tf_op jit(solution)/shard_map/all_to_all | solution.py:37
  542.3 12.4 %all-to-all-start.1 = ((bf16[16,2,144]{2,1,0:T(2,128)(2,1)}), bf16[16,2,144]{2,1,0:T(2,128)(2,1)S(1)}, u32[]{:S(2)}, u32[]{:S(2)}) async-start(bf16[16,2,144]{2,1,0:T(2,128)(2,1)} %reshape.1310), calls=%async_computation.1 | async-start | bytes 32768 | tf_op jit(solution)/shard_map/all_to_all | solution.py:37
  554.8 12.8 %all-to-all-start = ((bf16[16,2,432]{2,1,0:T(2,128)(2,1)}), bf16[16,2,432]{2,1,0:T(2,128)(2,1)S(1)}, u32[]{:S(2)}, u32[]{:S(2)}) async-start(bf16[16,2,432]{2,1,0:T(2,128)(2,1)} %reshape.1308), calls=%async_computation | async-start | bytes 65536 | tf_op jit(solution)/shard_map/all_to_all | solution.py:37
  567.6 12.3 %all-to-all-start.2 = ((bf16[16,2,576]{2,1,0:T(2,128)(2,1)}), bf16[16,2,576]{2,1,0:T(2,128)(2,1)S(1)}, u32[]{:S(2)}, u32[]{:S(2)}) async-start(bf16[16,2,576]{2,1,0:T(2,128)(2,1)} %reshape.1312), calls=%async_computation.2 | async-start | bytes 81920 | tf_op jit(solution)/shard_map/all_to_all | solution.py:37
  579.9 12.3 %all-to-all-start.3 = ((bf16[16,2,576]{2,1,0:T(2,128)(2,1)}), bf16[16,2,576]{2,1,0:T(2,128)(2,1)S(1)}, u32[]{:S(2)}, u32[]{:S(2)}) async-start(bf16[16,2,576]{2,1,0:T(2,128)(2,1)} %reshape.1314), calls=%async_computation.3 | async-start | bytes 81920 | tf_op jit(solution)/shard_map/all_to_all | solution.py:37
  (69 other events, 158.3 us)
Sparse Core Ops, SparseCore 0:
  238.0 147.6 all-reduce.16
where the time goes:
time: 606 us; the launch traced here: 600 us
  other arithmetic  265 us (44%)
  local copies, waits for them, and re-layouts  175 us (29%)
  blocking collectives  41.7 us (7%)
  matrix products  35.7 us (6%)
  waiting for transfers between devices  34.3 us (6%)
  starting transfers between devices  31.3 us (5%)
  between operations  17.7 us (3%)
    scatter-add x2, other arithmetic, run_block(): bias_full = jnp.take(table_part, position_index(), axis=3)  226 us
    gather x4, local copies, waits for them, and re-layouts, run_block(): bias_full = jnp.take(table_part, position_index(), axis=3)  101 us
    psum x5, blocking collectives, by_axis(): array = lax.psum(array, axis)  41.7 us
    all_to_all x5, starting transfers between devices, sent_and_summed(): parts = lax.all_to_all(split_up(array, dim, count), axis, 0, 0, tiled=True)  23.6 us
    all_to_all x5, waiting for transfers between devices, sent_and_summed(): parts = lax.all_to_all(split_up(array, dim, count), axis, 0, 0, tiled=True)  22.2 us
    broadcast_in_dim x2, local copies, waits for them, and re-layouts, run_block(): scores = jnp.where(allowed, scores + bias_full[:, :, None], -1e+30)  21.6 us
    unnamed x185, local copies, waits for them, and re-layouts  16 us
  transfers between devices with their start and end apart: 10, of which 7 were waited for; matrix products, arithmetic and copies ran while one was open for 46% of the time, Pallas kernels for 0%

commit v1 on v0

v1 whole, which is shorter than its diff:
```python
import functools

import jax
import jax.numpy as jnp
import ml_dtypes
import numpy as np
from jax import lax
from jax.experimental import pallas as pl
from jax.experimental.pallas import tpu as pltpu
from jax.sharding import Mesh
from jax.sharding import PartitionSpec as P

WZ = 2
WH = 6
WW = 12
LAT = ("lat_0", "lat_1")
LON = ("lon_0", "lon_1", "lon_2")
LAT_LON = ("lat_0", "lat_1", "lon_0", "lon_1", "lon_2")
BF = jnp.bfloat16
F32 = jnp.float32
HEADS = 6
DIM = 192
HEAD = 32
WIN = 144
TOK = 288
HID = 768
POS = 3312
SCALE = HEAD**-0.5


def token_order():
    order = np.zeros((TOK, TOK), np.float32)
    row = 0
    for n in range(2):
        for ih in range(2):
            for w in range(WW):
                for z in range(2):
                    for il in range(3):
                        source = (z * 6 + ih * 3 + il) * 24 + n * WW + w
                        order[row, source] = 1
                        row += 1
    return order.astype(ml_dtypes.bfloat16)


def lane_order():
    order = np.zeros((276, 512), np.float32)
    for a in range(12):
        for d in range(23):
            order[a * 23 + d, (a // 6) * 256 + d * 6 + a % 6] = 1
    return order.astype(ml_dtypes.bfloat16)


def table_offsets(flip):
    offsets = {}
    for b in range(12):
        for a in range(12):
            hk, zk, lk = b // 6, b % 6 // 3, b % 3
            hq, zq, lq = a // 6, a % 6 // 3, a % 3
            if flip:
                hk, zk, hq, zq = 1 - hk, 1 - zk, 1 - hq, 1 - zq
            offsets[b, a] = (zq * 2 + zk) * 828 + ((hq * 3 + lq) * 6 + hk * 3 + lk) * 23
    return offsets


def nn(a, b):
    return lax.dot_general(a, b, (((1,), (0,)), ((), ())), preferred_element_type=F32)


def nt(a, b):
    return lax.dot_general(a, b, (((1,), (1,)), ((), ())), preferred_element_type=F32)


def tn(a, b):
    return lax.dot_general(a, b, (((0,), (0,)), ((), ())), preferred_element_type=F32)


def two_pieces(x):
    high = x.astype(BF)
    return high, (x - high.astype(F32)).astype(BF)


def three_pieces(x):
    high = x.astype(BF)
    rest = x - high.astype(F32)
    middle = rest.astype(BF)
    return high, middle, (rest - middle.astype(F32)).astype(BF)


def expand_bias(table, lanes, flip, bias_ref):
    offsets = table_offsets(flip)
    rows = []
    for b in range(12):
        rows.append(
            jnp.concatenate(
                [table[:, offsets[b, a] : offsets[b, a] + 23] for a in range(12)], axis=1
            )
        )
    stacked = jnp.concatenate(rows, axis=0)
    high, middle, low = three_pieces(stacked)
    spread = nn(high, lanes) + nn(middle, lanes) + nn(low, lanes)
    for b in range(12):
        block = spread[b * 8 : b * 8 + 8]
        for w in range(WW):
            start = (11 - w) * 6
            both = jnp.concatenate(
                (block[:, start : start + 72], block[:, 256 + start : 256 + start + 72]), axis=1
            )
            row = (b // 6) * 72 + w * 6 + b % 6
            right = jnp.concatenate((both[:, 128:], jnp.zeros((8, 112), F32)), axis=1)
            bias_ref[0, pl.ds(row, 8, stride=WIN), :] = both[:, :128]
            bias_ref[1, pl.ds(row, 8, stride=WIN), :] = right


def reduce_bias(grad_ref, lanes, flip):
    offsets = table_offsets(flip)
    rows = []
    for b in range(12):
        left = jnp.zeros((8, 256), F32)
        right = jnp.zeros((8, 256), F32)
        for w in range(WW):
            start = (11 - w) * 6
            row = (b // 6) * 72 + w * 6 + b % 6
            both = jnp.concatenate(
                (
                    grad_ref[0, pl.ds(row, 8, stride=WIN), :],
                    grad_ref[1, pl.ds(row, 8, stride=WIN), :][:, :16],
                ),
                axis=1,
            )
            left = left + jnp.pad(both[:, :72], ((0, 0), (start, 184 - start)))
            right = right + jnp.pad(both[:, 72:], ((0, 0), (start, 184 - start)))
        rows.append(jnp.concatenate((left, right), axis=1))
    stacked = jnp.concatenate(rows, axis=0)
    high, low = two_pieces(stacked)
    packed = nt(high, lanes) + nt(low, lanes)
    places = sorted((start, b, a) for (b, a), start in offsets.items())
    return jnp.concatenate(
        [packed[b * 8 : b * 8 + 8, a * 23 : a * 23 + 23] for _, b, a in places], axis=1
    )


def normed(u):
    mean = jnp.mean(u, -1, keepdims=True)
    centred = u - mean
    scale = lax.rsqrt(jnp.mean(centred * centred, -1, keepdims=True) + 1e-05)
    return centred * scale, scale


def normed_back(grad, unit, scale):
    mean = jnp.mean(grad, -1, keepdims=True)
    product = jnp.mean(grad * unit, -1, keepdims=True)
    return scale * (grad - mean - unit * product)


def head_masks():
    lane = lax.broadcasted_iota(jnp.int32, (1, DIM), 1) // HEAD
    return [(lane == h).astype(F32) for h in range(HEADS)]


def by_head(x, masks):
    return jnp.concatenate([x * m.astype(BF) for m in masks], axis=0)


def from_heads(x, masks):
    total = x[:WIN] * masks[0]
    for h in range(1, HEADS):
        total = total + x[h * WIN : h * WIN + WIN] * masks[h]
    return total


def forward(u, gains, w_qkv, w_proj, w_fc1, w_fc2, bias_ref, allowed, prob_ref):
    masks = head_masks()
    unit, _ = normed(u)
    n1 = (unit * gains[0:1]).astype(BF)
    q, k, v = (
        nn(n1, w_qkv[:, i * DIM : i * DIM + DIM]) for i in range(3)
    )
    joined = []
    for n in range(2):
        part = slice(n * WIN, n * WIN + WIN)
        scores = nt(by_head(k[part].astype(BF), masks), q[part].astype(BF))
        v_t = jnp.transpose(v[part]).astype(BF)
        out_t = []
        for h in range(HEADS):
            rows = slice(h * WIN, h * WIN + WIN)
            bias = jnp.concatenate((bias_ref[0, rows, :], bias_ref[1, rows, :16]), axis=1)
            s = scores[rows] * SCALE + bias
            if allowed is not None:
                s = jnp.where(allowed, s, -1e30)
            e = jnp.exp(s - jnp.max(s, 0, keepdims=True))
            p = (e * (1.0 / jnp.sum(e, 0, keepdims=True))).astype(BF)
            prob_ref[n, rows, :] = p
            out_t.append(nn(v_t[h * HEAD : h * HEAD + HEAD], p))
        joined.append(jnp.transpose(jnp.concatenate(out_t, axis=0)))
    o = jnp.concatenate(joined, axis=0).astype(BF)
    m = u + nn(o, w_proj)
    unit2, _ = normed(m)
    n2 = (unit2 * gains[1:2]).astype(BF)
    e = nn(n2, w_fc1)
    cdf = 0.5 * (1.0 + lax.erf(e * (0.5**0.5)))
    g = (e * cdf).astype(BF)
    slope = cdf + e * jnp.exp(e * e * -0.5) * 0.3989422804014327
    return q.astype(BF), k.astype(BF), v.astype(BF), o, m, g, slope.astype(BF)


def backward(u, q, k, v, o, m, g, slope, cot, gains, w_qkv, w_proj, w_fc1, w_fc2, prob_ref, grad_ref, outs):
    qkv_ref, proj_ref, fc1_ref, fc2_ref, gain_ref = outs
    masks = head_masks()
    unit, scale = normed(u)
    n1 = (unit * gains[0:1]).astype(BF)
    unit2, scale2 = normed(m)
    n2 = (unit2 * gains[1:2]).astype(BF)
    y2 = cot.astype(BF)
    fc2_ref[...] = tn(y2, g).astype(fc2_ref.dtype)
    dg = nt(y2, w_fc2).astype(BF).astype(F32)
    y1 = (dg * slope.astype(F32)).astype(BF)
    fc1_ref[...] = tn(y1, n2).astype(fc1_ref.dtype)
    dn2 = nt(y1, w_fc1).astype(BF).astype(F32)
    gain_ref[1:2, :] = jnp.sum(dn2 * unit2, 0, keepdims=True)
    dm = cot + normed_back(dn2 * gains[1:2], unit2, scale2)
    yp = dm.astype(BF)
    proj_ref[...] = tn(yp, o).astype(proj_ref.dtype)
    do = nt(yp, w_proj).astype(BF)
    dqs, dks, dvs = [], [], []
    for n in range(2):
        part = slice(n * WIN, n * WIN + WIN)
        do_n, q_n, k_n, v_n = do[part], q[part], k[part], v[part]
        dp = nt(by_head(v_n, masks), do_n)
        dvs.append(from_heads(nn(prob_ref[n], do_n), masks))
        k_t = jnp.transpose(k_n.astype(F32)).astype(BF)
        ds_all, dq_t = [], []
        for h in range(HEADS):
            rows = slice(h * WIN, h * WIN + WIN)
            p = prob_ref[n, rows, :].astype(F32)
            dp_h = dp[rows].astype(BF).astype(F32)
            ds = p * (dp_h - jnp.sum(p * dp_h, 0, keepdims=True))
            if n == 0:
                grad_ref[0, rows, :] = ds[:, :128]
                grad_ref[1, rows, :16] = ds[:, 128:]
            else:
                grad_ref[0, rows, :] += ds[:, :128]
                grad_ref[1, rows, :16] += ds[:, 128:]
            ds = (ds * SCALE).astype(BF)
            ds_all.append(ds)
            dq_t.append(nn(k_t[h * HEAD : h * HEAD + HEAD], ds))
        dqs.append(jnp.transpose(jnp.concatenate(dq_t, axis=0)))
        dks.append(from_heads(nn(jnp.concatenate(ds_all, axis=0), q_n), masks))
    dn1 = jnp.zeros((TOK, DIM), F32)
    for i, parts in enumerate((dqs, dks, dvs)):
        d = jnp.concatenate(parts, axis=0).astype(BF)
        qkv_ref[i * DIM : i * DIM + DIM, :] = tn(d, n1).astype(qkv_ref.dtype)
        dn1 = dn1 + nt(d, w_qkv[:, i * DIM : i * DIM + DIM])
    dn1 = dn1.astype(BF).astype(F32)
    gain_ref[0:1, :] = jnp.sum(dn1 * unit, 0, keepdims=True)
    return dm + normed_back(dn1 * gains[0:1], unit, scale)


def flat_rows(ref):
    return jnp.concatenate([ref[z, i].astype(F32) for z in range(2) for i in range(6)], axis=0)


def first_kernel(state, cot, order, lanes, table, gains, w_qkv, w_proj, w_fc1, w_fc2,
                 out_ref, cot_ref, x_ref, q_ref, k_ref, v_ref, o_ref, m_ref, g_ref, slope_ref, prob_ref, bias_ref):
    perm = order[...]
    x = nn(perm, flat_rows(state).astype(BF))
    cot_ref[...] = nn(perm, flat_rows(cot).astype(BF)).astype(BF)
    x_ref[...] = x.astype(BF)
    expand_bias(table[...], lanes[...], False, bias_ref)
    q, k, v, o, m, g, slope = forward(
        x, gains[0], w_qkv[0], w_proj[0], w_fc1[0], w_fc2[0], bias_ref, None, prob_ref
    )
    out_ref[...] = (m + nn(g, w_fc2[0])).astype(BF)
    for ref, value in ((q_ref, q), (k_ref, k), (v_ref, v), (o_ref, o), (m_ref, m), (g_ref, g), (slope_ref, slope)):
        ref[...] = value


def second_kernel(last, u_ref, cot_ref, lanes, table, gains, w_qkv, w_proj, w_fc1, w_fc2,
                  du_ref, qkv_ref, proj_ref, fc1_ref, fc2_ref, gain_ref, table_ref, bias_ref, prob_ref, grad_ref):
    expand_bias(table[...], lanes[...], True, bias_ref)
    row = lax.broadcasted_iota(jnp.int32, (WIN, WIN), 0)
    lane = lax.broadcasted_iota(jnp.int32, (WIN, WIN), 1)
    same_z = (row % 6 // 3) == (lane % 6 // 3)
    same_h = (row // 72) == (lane // 72)
    allowed = same_z & (same_h | (jnp.full((WIN, WIN), last[0], jnp.int32) == 0))
    u = u_ref[...].astype(F32)
    weights = (w_qkv[0], w_proj[0], w_fc1[0], w_fc2[0])
    saved = forward(u, gains[0], *weights, bias_ref, allowed, prob_ref)
    grad_ref[...] = jnp.zeros_like(grad_ref)
    du_ref[...] = backward(
        u, *saved, cot_ref[...].astype(F32), gains[0], *weights, prob_ref, grad_ref,
        (qkv_ref, proj_ref, fc1_ref, fc2_ref, gain_ref),
    )
    table_ref[...] = reduce_bias(grad_ref, lanes[...], True)


def third_kernel(x_ref, q_ref, k_ref, v_ref, o_ref, m_ref, g_ref, slope_ref, prob_ref, cot_ref, order, lanes,
                 gains, w_qkv, w_proj, w_fc1, w_fc2,
                 du_ref, qkv_ref, proj_ref, fc1_ref, fc2_ref, gain_ref, table_ref, grad_ref):
    weights = (w_qkv[0], w_proj[0], w_fc1[0], w_fc2[0])
    grad_ref[...] = jnp.zeros_like(grad_ref)
    du = backward(
        x_ref[...].astype(F32), q_ref[...], k_ref[...], v_ref[...], o_ref[...], m_ref[...], g_ref[...],
        slope_ref[...], cot_ref[...], gains[0], *weights, prob_ref, grad_ref,
        (qkv_ref, proj_ref, fc1_ref, fc2_ref, gain_ref),
    )
    high, low = two_pieces(du)
    flat = tn(order[...], high) + tn(order[...], low)
    for z in range(2):
        for i in range(6):
            start = (z * 6 + i) * 24
            du_ref[z, i] = flat[start : start + 24]
    table_ref[...] = reduce_bias(grad_ref, lanes[...], False)


def whole(shape):
    return pl.BlockSpec(shape, lambda i: (0,) * len(shape))


def of_block(block, shape):
    return pl.BlockSpec((1,) + shape, lambda i: (block,) + (0,) * len(shape))


def weight_specs(block):
    return [
        of_block(block, (2, DIM)),
        of_block(block, (DIM, 3 * DIM)),
        of_block(block, (DIM, DIM)),
        of_block(block, (DIM, HID)),
        of_block(block, (HID, DIM)),
    ]


PARAMS = pltpu.CompilerParams(vmem_limit_bytes=48 * 1024 * 1024)
GRADS = (
    ((3 * DIM, DIM), BF),
    ((DIM, DIM), BF),
    ((HID, DIM), BF),
    ((DIM, HID), BF),
    ((2, DIM), F32),
    ((8, POS), F32),
)


def call(kernel, in_specs, outs, scratch, args):
    return pl.pallas_call(
        kernel,
        grid=(1,),
        in_specs=in_specs,
        out_specs=[whole(s) for s, _ in outs],
        out_shape=[jax.ShapeDtypeStruct(s, d) for s, d in outs],
        scratch_shapes=scratch,
        compiler_params=PARAMS,
    )(*args)


def first(state, cot, table, weights):
    full = (2, 6, 24, DIM)
    return call(
        first_kernel,
        [whole(full), whole(full), whole((TOK, TOK)), whole((276, 512)), whole((8, POS))] + weight_specs(0),
        [((TOK, DIM), BF)] * 6 + [((TOK, DIM), BF), ((TOK, DIM), F32), ((TOK, HID), BF), ((TOK, HID), BF),
         ((2, HEADS * WIN, WIN), BF)],
        [pltpu.VMEM((2, 8 * WIN, 128), F32)],
        (state, cot, token_order(), lane_order(), table) + weights,
    )


def second(last, u, cot, table, weights):
    return call(
        second_kernel,
        [pl.BlockSpec(memory_space=pltpu.SMEM), whole((TOK, DIM)), whole((TOK, DIM)), whole((276, 512)),
         whole((8, POS))] + weight_specs(1),
        [((TOK, DIM), F32)] + list(GRADS),
        [pltpu.VMEM((2, 8 * WIN, 128), F32), pltpu.VMEM((2, HEADS * WIN, WIN), BF), pltpu.VMEM((2, 8 * WIN, 128), F32)],
        (last, u, cot, lane_order(), table) + weights,
    )


def third(saved, cot, weights):
    return call(
        third_kernel,
        [whole((TOK, DIM))] * 6 + [whole((TOK, HID))] * 2 + [whole((2, HEADS * WIN, WIN)), whole((TOK, DIM)),
         whole((TOK, TOK)), whole((276, 512))] + weight_specs(0),
        [((2, 6, 24, DIM), F32)] + list(GRADS),
        [pltpu.VMEM((2, 8 * WIN, 128), F32)],
        tuple(saved) + (cot, token_order(), lane_order()) + weights,
    )


def from_behind(value, axis, steps):
    count = lax.axis_size(axis)
    pairs = [(source, (source + steps) % count) for source in range(count)]
    return lax.ppermute(value, axis, pairs)


def sent_and_summed(array, axis, dim):
    count = lax.axis_size(axis)
    dims = array.shape
    parts = array.reshape(*dims[:dim], count, dims[dim] // count, *dims[dim + 1 :])
    parts = lax.all_to_all(jnp.moveaxis(parts, dim, 0), axis, 0, 0, tiled=True)
    return jnp.sum(parts.astype(F32), axis=0)


def body(state, out_cot, qkv_weight, proj_weight, fc1_weight, fc2_weight, norm_gain, bias_table):
    weights = (norm_gain, qkv_weight, proj_weight, fc1_weight, fc2_weight)
    tables = jnp.pad(bias_table[:, 0, 0], ((0, 0), (0, 2), (0, 0)))
    one, cot, *saved = first(state, out_cot, tables[0], weights)
    paired = jnp.stack((one, cot)).reshape(2, 2, 2, 72, DIM)
    arrived = from_behind(paired[:, :, 0], LAT, -1)
    paired = jnp.stack((arrived, paired[:, :, 1]), 2)
    arrived = from_behind(paired[:, 0, :, :36], LON, -1)
    following = jnp.stack((paired[:, 1, :, :36], arrived), 1)
    paired = jnp.concatenate((paired[:, :, :, 36:], following), 3).reshape(2, TOK, DIM)
    last = (lax.axis_index(LAT) == lax.axis_size(LAT) - 1).astype(jnp.int32).reshape(1)
    du, *second_grads = second(last, paired[0], paired[1], tables[1], weights)
    du = du.reshape(2, 2, 72, DIM)
    arrived = from_behind(du[1, :, 36:].astype(BF), LON, 1).astype(F32)
    before = jnp.stack((arrived, du[0, :, 36:]))
    du = jnp.concatenate((before, du[:, :, :36]), 2)
    arrived = from_behind(du[:, 0].astype(BF), LAT, 1).astype(F32)
    du = jnp.stack((arrived, du[:, 1]), 1).reshape(TOK, DIM)
    state_grad, *first_grads = third(saved[:], du, weights)
    summed = []
    for i in range(4):
        both = jnp.stack((first_grads[i], second_grads[i]))
        both = lax.psum_scatter(both, LON, scatter_dimension=1, tiled=True)
        summed.append(jnp.swapaxes(sent_and_summed(both, LAT, 2), 1, 2))
    gain_grad = lax.psum(jnp.stack((first_grads[4], second_grads[4])), LAT_LON)
    table_grad = jnp.stack((first_grads[5], second_grads[5]))[:, None, None, :6].astype(BF)
    table_grad = sent_and_summed(table_grad, LON, 4)
    return (state_grad, *summed, gain_grad, table_grad)


def solution(mesh):
    split = Mesh(mesh.devices.reshape(8, 2, 4, 2, 2), ("lat_0", "lat_1", "lon_0", "lon_1", "lon_2"))
    placed = (
        P(None, LAT, LON, None),
        P(None, LAT, LON, None),
        P(),
        P(),
        P(),
        P(),
        P(),
        P(None, LAT, None, None, None),
    )
    return jax.shard_map(
        body,
        mesh=split,
        in_specs=placed,
        out_specs=(
            P(None, LAT, LON, None),
            P(None, LAT, LON),
            P(None, LAT, LON),
            P(None, LAT, LON),
            P(None, LAT, LON),
            P(),
            P(None, LAT, None, None, LON),
        ),
        check_vma=False,
    )
```

time: 606 us -> 343 us (0.57)
  other arithmetic: 265 us -> 5.89 us
  local copies, waits for them, and re-layouts: 175 us -> 37.4 us
  waiting for transfers between devices: 34.3 us -> 153 us
  blocking collectives: 41.7 us -> 79 us
  matrix products: 35.7 us -> 0 us
  Pallas kernels: 0 us -> 15.5 us
    scatter-add x2 -> x0, other arithmetic: 226 us -> none  [run_block(): bias_full = jnp.take(table_part, position_index(), axis=3)]
    unnamed x2 -> x3, waiting for transfers between devices: 0.02 us -> 114 us
    gather x4 -> x0, local copies, waits for them, and re-layouts: 101 us -> none  [run_block(): bias_full = jnp.take(table_part, position_index(), axis=3)]
    psum x5 -> x1, blocking collectives: 41.7 us -> 79 us  [body(): gain_grad = lax.psum(jnp.stack((first_grads[4], second_grads[4])), LAT_LON)]
    dot_general x33 -> x0, matrix products: 30.3 us -> none  [the longest x6 8.91 us: run_block(): jnp.einsum('abchqk,abckhd->abcqhd', attention, value_vectors)]
    broadcast_in_dim x3 -> x0, local copies, waits for them, and re-layouts: 21.7 us -> none  [the longest x2 21.6 us: run_block(): scores = jnp.where(allowed, scores + bias_full[:, :, None], -1e+30)]
    pallas_call x0 -> x3, Pallas kernels: none -> 15.5 us  [call(): pl.pallas_call(kernel, grid=(1,), in_specs=in_specs, out_specs=[whole(s)...]
    unnamed x185 -> x111, local copies, waits for them, and re-layouts: 16 us -> 27 us
  transfers between devices with their start and end apart: 10 -> 11, of which waited for: 7 -> 9; matrix products, arithmetic and copies ran while one was open for 46% -> 4% of each run, Pallas kernels for 0% -> 0%
where the time goes in v1:
time: 343 us; the launch traced here: 342 us
  waiting for transfers between devices  153 us (45%)
  blocking collectives  79 us (23%)
  local copies, waits for them, and re-layouts  37.4 us (11%)
  starting transfers between devices  35.4 us (10%)
  between operations  15.8 us (5%)
  Pallas kernels  15.5 us (5%)
  other arithmetic  5.89 us (2%)
    unnamed x3, waiting for transfers between devices  114 us
    psum x1, blocking collectives, body(): gain_grad = lax.psum(jnp.stack((first_grads[4], second_grads[4])), LAT_LON)  79 us
    all_to_all x5, starting transfers between devices, sent_and_summed(): parts = lax.all_to_all(jnp.moveaxis(parts, dim, 0), axis, 0, 0, tiled=True)  27.9 us
    unnamed x111, local copies, waits for them, and re-layouts  27 us
    all_to_all x5, waiting for transfers between devices, sent_and_summed(): parts = lax.all_to_all(jnp.moveaxis(parts, dim, 0), axis, 0, 0, tiled=True)  24.1 us
    pallas_call x3, Pallas kernels, call(): pl.pallas_call(kernel, grid=(1,), in_specs=in_specs, out_specs=[whole(s)...  15.5 us
    ppermute x4, waiting for transfers between devices, from_behind(): return lax.ppermute(value, axis, pairs)  15.4 us
    ppermute x4, starting transfers between devices, from_behind(): return lax.ppermute(value, axis, pairs)  7.37 us
  transfers between devices with their start and end apart: 11, of which 9 were waited for; matrix products, arithmetic and copies ran while one was open for 4% of the time, Pallas kernels for 0%

profile of v1, /device:TPU:2, one launch (start us, length us, event | category | flops | bytes accessed | tf_op | source)
XLA Modules:
  0.0 342.4 jit_solution(96020305658630664)
XLA Ops:
  13.1 3.0 shard_map.180
  20.4 2.3 collective-permute-start
  22.7 4.2 %collective-permute-done = bf16[2,2,72,192]{3,2,0,1:T(8,128)(2,1)S(1)} collective-permute-done((bf16[2,2,72,192]{3,2,0,1:T(8,128)(2,1)S(1)}, bf16[2,2,72,192]{3,2,0,1:T(8,128)(2,1)S(1)}, u32[]{:S(2)}, u32[]{:S(2)}) %collective-permute-start) | collective-permute-done | bytes 110624 | tf_op jit(solution)/shard_map/ppermute | solution.py:393
  27.7 3.1 collective-permute-start.1
  30.8 2.4 collective-permute-done.1
  35.2 6.5 %shard_map.181 = (f32[288,192]{1,0:T(8,128)S(1)}, bf16[576,192]{1,0:T(8,128)(2,1)S(1)}, bf16[192,192]{1,0:T(8,128)(2,1)S(1)}, bf16[768,192]{1,0:T(8,128)(2,1)S(1...) custom-call(s32[1]{0:T(128)} %bitcast.2.last, bf16[288,192]{1,0:T(8,128)(2,1)S(1)} %bitcast.94, ...), custom_call_target="tpu_custom_call" | custom-call | tf_op jit(solution)/shard_map/pallas_call | solution.py:345
  43.7 7.0 %collective-permute-done.2 = bf16[2,36,192]{2,1,0:T(8,128)(2,1)S(1)} collective-permute-done((bf16[2,36,192]{2,1,0:T(8,128)(2,1)S(1)}, bf16[2,36,192]{2,1,0:T(8,128)(2,1)S(1)}, u32[]{:S(2)}, u32[]{:S(2)}) %collective-permute-start.2) | collective-permute-done | bytes 27680 | tf_op jit(solution)/shard_map/ppermute | solution.py:393
  51.6 1.9 collective-permute-start.3
  53.5 1.3 dynamic-slice
  57.0 1.8 collective-permute-done.3
  60.8 6.0 %shard_map.182 = (f32[2,6,24,192]{3,2,1,0:T(8,128)}, bf16[576,192]{1,0:T(8,128)(2,1)S(1)}, bf16[192,192]{1,0:T(8,128)(2,1)S(1)}, bf16[768,192]{1,0:T(8,128)(2,1)...) custom-call(bf16[288,192]{1,0:T(8,128)(2,1)S(1)} %copy-done.23, ...), custom_call_target="tpu_custom_call" | custom-call | tf_op jit(solution)/shard_map/pallas_call | solution.py:345
  72.4 1.4 copy.80
  75.0 1.4 copy.87
  78.3 3.5 %all-to-all-start.4 = ((bf16[16,2,1,1,6,207]{5,1,4,3,2,0:T(2,128)(2,1)}), bf16[16,2,1,1,6,207]{5,1,4,3,2,0:T(2,128)(2,1)S(1)}, u32[]{:S(2)}, u32[]{:S(2)}) async-start(bf16[16,2,1,1,6,207]{5,1,4,3,2,0:T(2,128)(2,1)} %copy.90), calls=%async_computation.5 | async-start | bytes 196608 | tf_op jit(solution)/shard_map/all_to_all | solution.py:400
  82.6 79.0 %psum.7 = f32[2,2,192]{2,1,0:T(2,128)} all-reduce(f32[2,2,192]{2,1,0:T(2,128)S(1)} %pad_maximum_fusion.7), channel_id=1, replica_groups=mesh['lat_0'=8,'lat_1'=2,'lon_0'=4,'lon_1'=2,'lon_2'=2] {'lat_0','lat_1'..., use_global_device_ids=true, to_apply=%region_8.9 | all-reduce | flops 768 | bytes 6144 | tf_op jit(solution)/shard_map/psum | solution.py:428
  163.3 6.4 %all-to-all-start.2 = ((bf16[16,2,576]{2,1,0:T(2,128)(2,1)}), bf16[16,2,576]{2,1,0:T(2,128)(2,1)S(1)}, u32[]{:S(2)}, u32[]{:S(2)}) async-start(bf16[16,2,576]{2,1,0:T(2,128)(2,1)} %reshape.76), calls=%async_computation.3 | async-start | bytes 81920 | tf_op jit(solution)/shard_map/all_to_all | solution.py:400
  170.4 6.8 %all-to-all-done.2 = bf16[16,2,576]{2,1,0:T(2,128)(2,1)S(1)} async-done(((bf16[16,2,576]{2,1,0:T(2,128)(2,1)}), bf16[16,2,576]{2,1,0:T(2,128)(2,1)S(1)}, u32[]{:S(2)}, u32[]{:S(2)}) %all-to-all-start.2) | async-done | bytes 36896 | tf_op jit(solution)/shard_map/all_to_all | solution.py:400
  178.1 113.8 %all-reduce.7.cloned.1.call-done = (bf16[2,576,192]{2,0,1:T(2,128)(2,1)}, bf16[2,192,192]{2,0,1:T(2,128)(2,1)}, bf16[2,192,768]{2,0,1:T(2,128)(2,1)}) async-done(((bf16[2,576,192]{2,0,1:T(2,128)(2,1)}, bf16[2,192,192]{2,0,1:T(2,128)(2,1)}, bf16[2,192,768]{2,0,1:T(2,128)(2,1)}), (bf16[2,576,192]{2,0,1:T(2,128)(2,1)}, bf16[2,192,192]{2,0,1:T(2,128)(2,1)}, ...) | async-done | bytes 1179664
  294.5 8.5 %all-to-all-start.1 = ((bf16[16,2,144]{2,1,0:T(2,128)(2,1)}), bf16[16,2,144]{2,1,0:T(2,128)(2,1)S(1)}, u32[]{:S(2)}, u32[]{:S(2)}) async-start(bf16[16,2,144]{2,1,0:T(2,128)(2,1)} %reshape.74), calls=%async_computation.1 | async-start | bytes 32768 | tf_op jit(solution)/shard_map/all_to_all | solution.py:400
  305.7 4.5 %all-to-all-done.1 = bf16[16,2,144]{2,1,0:T(2,128)(2,1)S(1)} async-done(((bf16[16,2,144]{2,1,0:T(2,128)(2,1)}), bf16[16,2,144]{2,1,0:T(2,128)(2,1)S(1)}, u32[]{:S(2)}, u32[]{:S(2)}) %all-to-all-start.1) | async-done | bytes 9248 | tf_op jit(solution)/shard_map/all_to_all | solution.py:400
  310.2 4.7 %all-to-all-start = ((bf16[16,2,432]{2,1,0:T(2,128)(2,1)}), bf16[16,2,432]{2,1,0:T(2,128)(2,1)S(1)}, u32[]{:S(2)}, u32[]{:S(2)}) async-start(bf16[16,2,432]{2,1,0:T(2,128)(2,1)} %reshape.72), calls=%async_computation | async-start | bytes 65536 | tf_op jit(solution)/shard_map/all_to_all | solution.py:400
  316.3 6.1 %all-to-all-done = bf16[16,2,432]{2,1,0:T(2,128)(2,1)S(1)} async-done(((bf16[16,2,432]{2,1,0:T(2,128)(2,1)}), bf16[16,2,432]{2,1,0:T(2,128)(2,1)S(1)}, u32[]{:S(2)}, u32[]{:S(2)}) %all-to-all-start) | async-done | bytes 27680 | tf_op jit(solution)/shard_map/all_to_all | solution.py:400
  322.4 4.7 %all-to-all-start.3 = ((bf16[16,2,576]{2,1,0:T(2,128)(2,1)}), bf16[16,2,576]{2,1,0:T(2,128)(2,1)S(1)}, u32[]{:S(2)}, u32[]{:S(2)}) async-start(bf16[16,2,576]{2,1,0:T(2,128)(2,1)} %reshape.78), calls=%async_computation.4 | async-start | bytes 81920 | tf_op jit(solution)/shard_map/all_to_all | solution.py:400
  328.0 6.7 %all-to-all-done.3 = bf16[16,2,576]{2,1,0:T(2,128)(2,1)S(1)} async-done(((bf16[16,2,576]{2,1,0:T(2,128)(2,1)}), bf16[16,2,576]{2,1,0:T(2,128)(2,1)S(1)}, u32[]{:S(2)}, u32[]{:S(2)}) %all-to-all-start.3) | async-done | bytes 36896 | tf_op jit(solution)/shard_map/all_to_all | solution.py:400
  (158 shorter events, 39.4 us)
Async XLA Ops:
  7.2 1.9 copy-start.47
  7.2 154.4 %reduce-scatter.2.cloned.1.call-start = ((), (), s32[]{:S(2)}) async-start(), calls=%async_computation.6 | async-start | bytes 835584 | tf_op jit(solution)/shard_map/reduce_scatter | solution.py:426
  9.0 1.1 copy-start
  9.0 1.3 copy-start.1
  9.0 1.3 copy-start.2
  9.0 1.3 copy-start.38
  19.7 7.2 %copy-start.10 = (f32[288,192]{1,0:T(8,128)}, f32[288,192]{1,0:T(8,128)S(1)}, u32[]{:S(2)}) copy-start(f32[288,192]{1,0:T(8,128)S(1)} %get-tuple-element.37.m_ref) | copy-start | bytes 663556
  20.4 6.5 %collective-permute-start = (bf16[2,2,72,192]{3,2,0,1:T(8,128)(2,1)S(1)}, bf16[2,2,72,192]{3,2,0,1:T(8,128)(2,1)S(1)}, u32[]{:S(2)}, u32[]{:S(2)}) collective-permute-start(bf16[2,2,72,192]{3,2,0,1:T(8,128)(2,1)S(1)} %fusion.5), channel_id=1, source_target_pairs={{0,240},{16,0},{32,16},{48,32},{64,48},{80,64},{96,80},{112,96},{1... | collective-permute-start | bytes 331784 | tf_op jit(solution)/shard_map/ppermute | solution.py:393
  27.7 5.5 %collective-permute-start.1 = (bf16[2,2,36,192]{3,2,1,0:T(8,128)(2,1)}, bf16[2,2,36,192]{3,2,1,0:T(8,128)(2,1)}, u32[]{:S(2)}, u32[]{:S(2)}) collective-permute-start(bf16[2,2,36,192]{3,2,1,0:T(8,128)(2,1)} %get-tuple-element.84), channel_id=1, source_target_pairs={{0,15},{1,0},{2,1},{3,2},{4,3},{5,4},{6,5},{7,6},{8,7},{9,8},{10,9... | collective-permute-start | bytes 165896 | tf_op jit(solution)/shard_map/ppermute | solution.py:393
  43.6 7.2 %copy-start.12 = (bf16[192,768]{1,0:T(8,128)(2,1)}, bf16[192,768]{1,0:T(8,128)(2,1)S(1)}, u32[]{:S(2)}) copy-start(bf16[192,768]{1,0:T(8,128)(2,1)S(1)} %get-tuple-element.52) | copy-start | bytes 884740
  43.6 7.2 %copy-start.8 = (bf16[768,192]{1,0:T(8,128)(2,1)}, bf16[768,192]{1,0:T(8,128)(2,1)S(1)}, u32[]{:S(2)}) copy-start(bf16[768,192]{1,0:T(8,128)(2,1)S(1)} %get-tuple-element.50) | copy-start | bytes 884740
  43.6 7.2 %collective-permute-start.2 = (bf16[2,36,192]{2,1,0:T(8,128)(2,1)S(1)}, bf16[2,36,192]{2,1,0:T(8,128)(2,1)S(1)}, u32[]{:S(2)}, u32[]{:S(2)}) collective-permute-start(bf16[2,36,192]{2,1,0:T(8,128)(2,1)S(1)} %fusion.9), channel_id=1, source_target_pairs={{0,1},{1,2},{2,3},{3,4},{4,5},{5,6},{6,7},{7,8},{8,9},{9,10},{10,1... | collective-permute-start | bytes 82952 | tf_op jit(solution)/shard_map/ppermute | solution.py:393
  51.6 7.2 %collective-permute-start.3 = (bf16[2,72,192]{2,1,0:T(8,128)(2,1)}, bf16[2,72,192]{2,1,0:T(8,128)(2,1)}, u32[]{:S(2)}, u32[]{:S(2)}) collective-permute-start(bf16[2,72,192]{2,1,0:T(8,128)(2,1)} %fusion.8), channel_id=1, source_target_pairs={{0,16},{16,32},{32,48},{48,64},{64,80},{80,96},{96,112},{112,128},... | collective-permute-start | bytes 165896 | tf_op jit(solution)/shard_map/ppermute | solution.py:393
  56.0 3.8 %copy-start.29 = (bf16[288,192]{1,0:T(8,128)(2,1)S(1)}, bf16[288,192]{1,0:T(8,128)(2,1)}, u32[]{:S(2)}) copy-start(bf16[288,192]{1,0:T(8,128)(2,1)} %copy-done.28) | copy-start | bytes 331780
  56.0 3.8 %copy-start.31 = (bf16[288,192]{1,0:T(8,128)(2,1)S(1)}, bf16[288,192]{1,0:T(8,128)(2,1)}, u32[]{:S(2)}) copy-start(bf16[288,192]{1,0:T(8,128)(2,1)} %copy-done.30) | copy-start | bytes 331780
  60.8 9.3 %copy-start.9 = (bf16[768,192]{1,0:T(8,128)(2,1)S(1)}, bf16[768,192]{1,0:T(8,128)(2,1)}, u32[]{:S(2)}) copy-start(bf16[768,192]{1,0:T(8,128)(2,1)} %copy-done.8) | copy-start | bytes 884740
  71.2 1.1 copy-start.19
  71.2 220.7 %all-reduce.7.cloned.1.call-start = ((), (), s32[]{:S(2)}) async-start(), calls=%async_computation.7 | async-start | bytes 2752512
  72.4 1.4 copy-start.37
  78.3 85.0 %all-to-all-start.4 = ((bf16[16,2,1,1,6,207]{5,1,4,3,2,0:T(2,128)(2,1)}), bf16[16,2,1,1,6,207]{5,1,4,3,2,0:T(2,128)(2,1)S(1)}, u32[]{:S(2)}, u32[]{:S(2)}) async-start(bf16[16,2,1,1,6,207]{5,1,4,3,2,0:T(2,128)(2,1)} %copy.90), calls=%async_computation.5 | async-start | bytes 196608 | tf_op jit(solution)/shard_map/all_to_all | solution.py:400
  163.3 14.0 %all-to-all-start.2 = ((bf16[16,2,576]{2,1,0:T(2,128)(2,1)}), bf16[16,2,576]{2,1,0:T(2,128)(2,1)S(1)}, u32[]{:S(2)}, u32[]{:S(2)}) async-start(bf16[16,2,576]{2,1,0:T(2,128)(2,1)} %reshape.76), calls=%async_computation.3 | async-start | bytes 81920 | tf_op jit(solution)/shard_map/all_to_all | solution.py:400
  294.5 15.7 %all-to-all-start.1 = ((bf16[16,2,144]{2,1,0:T(2,128)(2,1)}), bf16[16,2,144]{2,1,0:T(2,128)(2,1)S(1)}, u32[]{:S(2)}, u32[]{:S(2)}) async-start(bf16[16,2,144]{2,1,0:T(2,128)(2,1)} %reshape.74), calls=%async_computation.1 | async-start | bytes 32768 | tf_op jit(solution)/shard_map/all_to_all | solution.py:400
  310.2 12.2 %all-to-all-start = ((bf16[16,2,432]{2,1,0:T(2,128)(2,1)}), bf16[16,2,432]{2,1,0:T(2,128)(2,1)S(1)}, u32[]{:S(2)}, u32[]{:S(2)}) async-start(bf16[16,2,432]{2,1,0:T(2,128)(2,1)} %reshape.72), calls=%async_computation | async-start | bytes 65536 | tf_op jit(solution)/shard_map/all_to_all | solution.py:400
  322.4 12.3 %all-to-all-start.3 = ((bf16[16,2,576]{2,1,0:T(2,128)(2,1)}), bf16[16,2,576]{2,1,0:T(2,128)(2,1)S(1)}, u32[]{:S(2)}, u32[]{:S(2)}) async-start(bf16[16,2,576]{2,1,0:T(2,128)(2,1)} %reshape.78), calls=%async_computation.4 | async-start | bytes 81920 | tf_op jit(solution)/shard_map/all_to_all | solution.py:400
  (35 other events, 28.8 us)
Sparse Core Ops, SparseCore 0:
  71.3 70.4 reduce-scatter.1
  144.9 146.9 all-reduce.6

commit v2 on v1

--- a/solution.py
+++ b/solution.py
@@ -137,6 +137,36 @@
     return jnp.concatenate(
         [packed[b * 8 : b * 8 + 8, a * 23 : a * 23 + 23] for _, b, a in places], axis=1
     )
+
+
+def pack_chunks(qkv, proj, fc1, fc2, table, out_ref):
+    table = jnp.concatenate((table, jnp.zeros((8, 256), F32)), axis=1)
+    for b in range(16):
+        rows = jnp.concatenate(
+            [qkv[36 * b : 36 * b + 36], proj[12 * b : 12 * b + 12], fc1[48 * b : 48 * b + 48]]
+            + [part[12 * b : 12 * b + 12] for part in fc2],
+            axis=0,
+        )
+        right = rows[:, 128:]
+        own = table[:, 207 * b : 207 * b + 207]
+        own = jnp.concatenate((own, jnp.zeros((8, 49), F32)), axis=1)
+        chunk = jnp.concatenate(
+            (
+                rows[:, :128],
+                jnp.concatenate((right[:72], right[72:]), axis=1),
+                own[:, :128],
+                own[:, 128:],
+                jnp.zeros((8, 128), F32),
+            ),
+            axis=0,
+        )
+        y, x, core = b // 4, b // 2 % 2, b % 2
+        out_ref[core * 8 + y * 2 + x] = chunk.astype(BF)
+
+
+def unpack_chunk(chunk):
+    right = jnp.concatenate((chunk[144:216, :64], chunk[144:216, 64:]), axis=0)
+    return jnp.concatenate((chunk[:144], right), axis=1)
 
 
 def normed(u):
@@ -203,23 +233,23 @@
     return q.astype(BF), k.astype(BF), v.astype(BF), o, m, g, slope.astype(BF)
 
 
-def backward(u, q, k, v, o, m, g, slope, cot, gains, w_qkv, w_proj, w_fc1, w_fc2, prob_ref, grad_ref, outs):
-    qkv_ref, proj_ref, fc1_ref, fc2_ref, gain_ref = outs
+def backward(u, q, k, v, o, m, g, slope, cot, gains, w_qkv, w_proj, w_fc1, w_fc2, lanes, flip, prob_ref, grad_ref, gain_ref, chunk_ref):
+    grad_ref[...] = jnp.zeros_like(grad_ref)
     masks = head_masks()
     unit, scale = normed(u)
     n1 = (unit * gains[0:1]).astype(BF)
     unit2, scale2 = normed(m)
     n2 = (unit2 * gains[1:2]).astype(BF)
     y2 = cot.astype(BF)
-    fc2_ref[...] = tn(y2, g).astype(fc2_ref.dtype)
+    fc2 = [tn(y2, g[:, DIM * i : DIM * i + DIM]) for i in range(4)]
     dg = nt(y2, w_fc2).astype(BF).astype(F32)
     y1 = (dg * slope.astype(F32)).astype(BF)
-    fc1_ref[...] = tn(y1, n2).astype(fc1_ref.dtype)
+    fc1 = tn(y1, n2)
     dn2 = nt(y1, w_fc1).astype(BF).astype(F32)
     gain_ref[1:2, :] = jnp.sum(dn2 * unit2, 0, keepdims=True)
     dm = cot + normed_back(dn2 * gains[1:2], unit2, scale2)
     yp = dm.astype(BF)
-    proj_ref[...] = tn(yp, o).astype(proj_ref.dtype)
+    proj = tn(yp, o)
     do = nt(yp, w_proj).astype(BF)
     dqs, dks, dvs = [], [], []
     for n in range(2):
@@ -246,13 +276,61 @@
         dqs.append(jnp.transpose(jnp.concatenate(dq_t, axis=0)))
         dks.append(from_heads(nn(jnp.concatenate(ds_all, axis=0), q_n), masks))
     dn1 = jnp.zeros((TOK, DIM), F32)
+    qkv = []
     for i, parts in enumerate((dqs, dks, dvs)):
         d = jnp.concatenate(parts, axis=0).astype(BF)
-        qkv_ref[i * DIM : i * DIM + DIM, :] = tn(d, n1).astype(qkv_ref.dtype)
+        qkv.append(tn(d, n1))
         dn1 = dn1 + nt(d, w_qkv[:, i * DIM : i * DIM + DIM])
     dn1 = dn1.astype(BF).astype(F32)
     gain_ref[0:1, :] = jnp.sum(dn1 * unit, 0, keepdims=True)
+    table = reduce_bias(grad_ref, lanes, flip)
+    pack_chunks(jnp.concatenate(qkv, axis=0), proj, fc1, fc2, table, chunk_ref)
     return dm + normed_back(dn1 * gains[0:1], unit, scale)
+
+
+def quarters(x):
+    return {
+        (n, ih, half): x[n * WIN + ih * 72 + half * 36 :][:36]
+        for n in range(2)
+        for ih in range(2)
+        for half in range(2)
+    }
+
+
+def padded(pieces, rows):
+    have = sum(p.shape[0] for p in pieces)
+    return jnp.concatenate(list(pieces) + [jnp.zeros((rows - have, DIM), F32)], axis=0).astype(BF)
+
+
+OWN = ((0, 1, 1), (1, 1, 0), (1, 1, 1))
+BY_LAT = ((0, 0, 1), (1, 0, 0), (1, 0, 1))
+BY_LON = ((0, 1, 0),)
+BY_BOTH = ((0, 0, 0),)
+
+
+def shifted(have):
+    order = []
+    for n in range(2):
+        for ih in range(2):
+            order += [(n, ih, 1), ((n + 1) % 2, ih, 0)]
+    return jnp.concatenate([have[key] for key in order], axis=0)
+
+
+def unshifted(x):
+    have = {}
+    row = 0
+    for n in range(2):
+        for ih in range(2):
+            for key in ((n, ih, 1), ((n + 1) % 2, ih, 0)):
+                have[key] = x[row : row + 36]
+                row += 36
+    return have
+
+
+def whole_block(have):
+    return jnp.concatenate(
+        [have[n, ih, half] for n in range(2) for ih in range(2) for half in range(2)], axis=0
+    )
 
 
 def flat_rows(ref):
@@ -260,48 +338,65 @@
 
 
 def first_kernel(state, cot, order, lanes, table, gains, w_qkv, w_proj, w_fc1, w_fc2,
-                 out_ref, cot_ref, x_ref, q_ref, k_ref, v_ref, o_ref, m_ref, g_ref, slope_ref, prob_ref, bias_ref):
+                 own_ref, lat_ref, lon_ref, both_ref,
+                 x_ref, q_ref, k_ref, v_ref, o_ref, m_ref, g_ref, slope_ref, prob_ref, bias_ref):
     perm = order[...]
     x = nn(perm, flat_rows(state).astype(BF))
-    cot_ref[...] = nn(perm, flat_rows(cot).astype(BF)).astype(BF)
+    cot_rows = nn(perm, flat_rows(cot).astype(BF))
     x_ref[...] = x.astype(BF)
     expand_bias(table[...], lanes[...], False, bias_ref)
     q, k, v, o, m, g, slope = forward(
         x, gains[0], w_qkv[0], w_proj[0], w_fc1[0], w_fc2[0], bias_ref, None, prob_ref
     )
-    out_ref[...] = (m + nn(g, w_fc2[0])).astype(BF)
+    out = quarters(m + nn(g, w_fc2[0]))
+    given = quarters(cot_rows)
+    for ref, keys in ((own_ref, OWN), (lat_ref, BY_LAT), (lon_ref, BY_LON), (both_ref, BY_BOTH)):
+        ref[...] = padded([out[key] for key in keys] + [given[key] for key in keys], ref.shape[0])
     for ref, value in ((q_ref, q), (k_ref, k), (v_ref, v), (o_ref, o), (m_ref, m), (g_ref, g), (slope_ref, slope)):
         ref[...] = value
 
 
-def second_kernel(last, u_ref, cot_ref, lanes, table, gains, w_qkv, w_proj, w_fc1, w_fc2,
-                  du_ref, qkv_ref, proj_ref, fc1_ref, fc2_ref, gain_ref, table_ref, bias_ref, prob_ref, grad_ref):
+def second_kernel(last, own_ref, lat_ref, lon_ref, both_ref, lanes, table, gains, w_qkv, w_proj, w_fc1, w_fc2,
+                  mine_ref, to_lat_ref, to_lon_ref, to_both_ref, gain_ref, chunk_ref,
+                  bias_ref, prob_ref, grad_ref):
     expand_bias(table[...], lanes[...], True, bias_ref)
     row = lax.broadcasted_iota(jnp.int32, (WIN, WIN), 0)
     lane = lax.broadcasted_iota(jnp.int32, (WIN, WIN), 1)
     same_z = (row % 6 // 3) == (lane % 6 // 3)
     same_h = (row // 72) == (lane // 72)
     allowed = same_z & (same_h | (jnp.full((WIN, WIN), last[0], jnp.int32) == 0))
-    u = u_ref[...].astype(F32)
+    out, given = {}, {}
+    for ref, keys in ((own_ref, OWN), (lat_ref, BY_LAT), (lon_ref, BY_LON), (both_ref, BY_BOTH)):
+        rows = ref[...].astype(F32)
+        for i, key in enumerate(keys):
+            out[key] = rows[36 * i : 36 * i + 36]
+            given[key] = rows[36 * (i + len(keys)) :][:36]
+    u = shifted(out)
     weights = (w_qkv[0], w_proj[0], w_fc1[0], w_fc2[0])
     saved = forward(u, gains[0], *weights, bias_ref, allowed, prob_ref)
-    grad_ref[...] = jnp.zeros_like(grad_ref)
-    du_ref[...] = backward(
-        u, *saved, cot_ref[...].astype(F32), gains[0], *weights, prob_ref, grad_ref,
-        (qkv_ref, proj_ref, fc1_ref, fc2_ref, gain_ref),
-    )
-    table_ref[...] = reduce_bias(grad_ref, lanes[...], True)
-
-
-def third_kernel(x_ref, q_ref, k_ref, v_ref, o_ref, m_ref, g_ref, slope_ref, prob_ref, cot_ref, order, lanes,
+    du = backward(
+        u, *saved, shifted(given), gains[0], *weights, lanes[...], True, prob_ref, grad_ref, gain_ref, chunk_ref
+    )
+    have = unshifted(du)
+    mine_ref[...] = jnp.concatenate([have[key] for key in OWN] + [jnp.zeros((4, DIM), F32)], axis=0)
+    for ref, keys in ((to_lat_ref, BY_LAT), (to_lon_ref, BY_LON), (to_both_ref, BY_BOTH)):
+        ref[...] = padded([have[key] for key in keys], ref.shape[0])
+
+
+def third_kernel(x_ref, q_ref, k_ref, v_ref, o_ref, m_ref, g_ref, slope_ref, prob_ref,
+                 mine_ref, lat_ref, lon_ref, both_ref, order, lanes,
                  gains, w_qkv, w_proj, w_fc1, w_fc2,
-                 du_ref, qkv_ref, proj_ref, fc1_ref, fc2_ref, gain_ref, table_ref, grad_ref):
+                 du_ref, gain_ref, chunk_ref, grad_ref):
     weights = (w_qkv[0], w_proj[0], w_fc1[0], w_fc2[0])
-    grad_ref[...] = jnp.zeros_like(grad_ref)
+    have = {}
+    for ref, keys in ((mine_ref, OWN), (lat_ref, BY_LAT), (lon_ref, BY_LON), (both_ref, BY_BOTH)):
+        rows = ref[...].astype(F32)
+        for i, key in enumerate(keys):
+            have[key] = rows[36 * i : 36 * i + 36]
     du = backward(
         x_ref[...].astype(F32), q_ref[...], k_ref[...], v_ref[...], o_ref[...], m_ref[...], g_ref[...],
-        slope_ref[...], cot_ref[...], gains[0], *weights, prob_ref, grad_ref,
-        (qkv_ref, proj_ref, fc1_ref, fc2_ref, gain_ref),
+        slope_ref[...], whole_block(have), gains[0], *weights, lanes[...], False, prob_ref, grad_ref,
+        gain_ref, chunk_ref,
     )
     high, low = two_pieces(du)
     flat = tn(order[...], high) + tn(order[...], low)
@@ -309,7 +404,224 @@
         for i in range(6):
             start = (z * 6 + i) * 24
             du_ref[z, i] = flat[start : start + 24]
-    table_ref[...] = reduce_bias(grad_ref, lanes[...], False)
+
+
+MESH = pl.DeviceIdType.MESH
+
+
+def ring(names):
+    sizes = [lax.axis_size(name) for name in names]
+    me = 0
+    for name, size in zip(names, sizes):
+        me = me * size + lax.axis_index(name)
+    total = 1
+    for size in sizes:
+        total *= size
+
+    def at(index):
+        where = {}
+        for name, size in reversed(list(zip(names, sizes))):
+            where[name] = lax.rem(index, size)
+            index = index // size
+        return where
+
+    return me, total, at
+
+
+def greet(devices):
+    barrier = pltpu.get_barrier_semaphore()
+    for device in devices:
+        pl.semaphore_signal(barrier, inc=1, device_id=device, device_id_type=MESH)
+    pl.semaphore_wait(barrier, len(devices))
+
+
+def halo_kernel(step, lat_in, lon_in, both_in, lat_out, lon_out, both_out, send_sem, recv_sem):
+    lat_me, lat_count, lat_at = ring(LAT)
+    lon_me, lon_count, lon_at = ring(LON)
+
+    def neighbours(way):
+        lat = lat_at(lax.rem(lat_me + way + lat_count, lat_count))
+        lon = lon_at(lax.rem(lon_me + way + lon_count, lon_count))
+        return lat, lon, {**lat, **lon}
+
+    greet(neighbours(-step))
+    copies = []
+    targets = neighbours(step)
+    for i, (source, target) in enumerate(((lat_in, lat_out), (lon_in, lon_out), (both_in, both_out))):
+        copy = pltpu.make_async_remote_copy(
+            src_ref=source, dst_ref=target, send_sem=send_sem.at[i], recv_sem=recv_sem.at[i],
+            device_id=targets[i], device_id_type=MESH,
+        )
+        copy.start()
+        copies.append(copy)
+    for copy in copies:
+        copy.wait()
+
+
+def halo(arrays, step, collective_id):
+    vmem = pl.BlockSpec(memory_space=pltpu.VMEM)
+    return pl.pallas_call(
+        functools.partial(halo_kernel, step),
+        in_specs=[vmem] * 3,
+        out_specs=[vmem] * 3,
+        out_shape=[jax.ShapeDtypeStruct(a.shape, a.dtype) for a in arrays],
+        scratch_shapes=[pltpu.SemaphoreType.DMA((3,)), pltpu.SemaphoreType.DMA((3,))],
+        compiler_params=pltpu.CompilerParams(collective_id=collective_id, has_side_effects=True),
+    )(*arrays)
+
+
+def reduce_kernel(first_w, second_w, first_g, second_g,
+                  qkv_ref, proj_ref, fc1_ref, fc2_ref, gain_ref, table_ref,
+                  got_a, sum_a, got_b, sum_b, got_c, sent_d, got_d,
+                  gain_s, gain_a, gain_b, gain_c, gain_d,
+                  send_a, recv_a, send_b, recv_b, send_c, recv_c, send_d, recv_d):
+    core = lax.axis_index("lon_2")
+    side = lax.axis_index("lon_1")
+    y, y_count = lax.axis_index("lon_0"), lax.axis_size("lon_0")
+    lat_me, lat_count, lat_at = ring(LAT)
+    core_peer = {"lon_2": 1 - core}
+    side_peer = {"lon_1": 1 - side}
+
+    def y_peer(o):
+        return lax.rem(y + o, y_count)
+
+    def lat_peer(o):
+        return lax.rem(lat_me + o, lat_count)
+
+    greet(
+        [core_peer, side_peer]
+        + [{"lon_0": y_peer(o)} for o in range(1, y_count)]
+        + [lat_at(lat_peer(o)) for o in range(1, lat_count)]
+    )
+
+    def send(source, target, sems, i, device):
+        copy = pltpu.make_async_remote_copy(
+            src_ref=source, dst_ref=target, send_sem=sems[0].at[i], recv_sem=sems[1].at[i],
+            device_id=device, device_id_type=MESH,
+        )
+        copy.start()
+        return copy
+
+    parts = (second_w, first_w)
+    flights_a = [
+        send(w.at[pl.ds((1 - core) * 8, 8)], got_a.at[i], (send_a, recv_a), i, core_peer)
+        for i, w in enumerate(parts)
+    ]
+    pad = jnp.zeros((2, 64), F32)
+    gain_s[0] = jnp.concatenate(
+        (
+            jnp.concatenate((first_g[...], pad), axis=1),
+            jnp.concatenate((second_g[...], pad), axis=1),
+            jnp.zeros((4, 256), F32),
+        ),
+        axis=0,
+    )
+    flights_a.append(send(gain_s.at[0], gain_a, (send_a, recv_a), 2, core_peer))
+    flights_b = []
+    for i, w in enumerate(parts):
+        flights_a[i].wait()
+        sum_a[i] = (w[pl.ds(core * 8, 8)].astype(F32) + got_a[i].astype(F32)).astype(BF)
+        for o in range(1, y_count):
+            flights_b.append(
+                send(sum_a.at[i, pl.ds(y_peer(o) * 2, 2)], got_b.at[i, y], (send_b, recv_b),
+                     i * (y_count - 1) + o - 1, {"lon_0": y_peer(o)})
+            )
+        got_b[i, pl.ds(y, 1)] = sum_a[i, pl.ds(y * 2, 2)][None]
+    flights_a[2].wait()
+    gain_s[1] = gain_s[0] + gain_a[...]
+    for o in range(1, y_count):
+        flights_b.append(
+            send(gain_s.at[1], gain_b.at[y], (send_b, recv_b), 2 * (y_count - 1) + o - 1, {"lon_0": y_peer(o)})
+        )
+    gain_b[pl.ds(y, 1)] = gain_s[pl.ds(1, 1)]
+    flights_c = []
+    for i in range(3):
+        for flight in flights_b[i * (y_count - 1) : (i + 1) * (y_count - 1)]:
+            flight.wait()
+        if i < 2:
+            total = got_b[i, 0].astype(F32)
+            for o in range(1, y_count):
+                total = total + got_b[i, o].astype(F32)
+            sum_b[i] = total.astype(BF)
+            flights_c.append(send(sum_b.at[i, 1 - side], got_c.at[i], (send_c, recv_c), i, side_peer))
+        else:
+            total = gain_b[0]
+            for o in range(1, y_count):
+                total = total + gain_b[o]
+            gain_s[2] = total
+            flights_c.append(send(gain_s.at[2], gain_c, (send_c, recv_c), 2, side_peer))
+    rows = [None, None]
+    for i in range(2):
+        flights_c[i].wait()
+        chunk = sum_b[i, pl.ds(side, 1)][0].astype(F32) + got_c[i].astype(F32)
+        table_ref[1 - i] = jnp.concatenate((chunk[216:224], chunk[224:232]), axis=1)[:6, :207]
+        rows[1 - i] = unpack_chunk(chunk)
+    across = jnp.concatenate([jnp.transpose(x[:96]) for x in rows], axis=1)
+    for a in range(16):
+        down, right = 96 + 12 * (a // 4), 48 * (a % 4)
+        piece = jnp.concatenate(
+            [across[12 * a : 12 * a + 12]]
+            + [x[down : down + 12, right : right + 48] for x in rows]
+            + [jnp.zeros((12, 96), F32)],
+            axis=1,
+        )
+        sent_d[a] = jnp.concatenate((piece, jnp.zeros((4, 384), F32)), axis=0).astype(BF)
+    flights_d = [
+        send(sent_d.at[lat_peer(o)], got_d.at[lat_me], (send_d, recv_d), o - 1, lat_at(lat_peer(o)))
+        for o in range(1, lat_count)
+    ]
+    flights_c[2].wait()
+    gain_s[3] = gain_s[2] + gain_c[...]
+    flights_d += [
+        send(gain_s.at[3], gain_d.at[lat_me], (send_d, recv_d), lat_count - 2 + o, lat_at(lat_peer(o)))
+        for o in range(1, lat_count)
+    ]
+    got_d[pl.ds(lat_me, 1)] = sent_d[pl.ds(lat_me, 1)]
+    gain_d[pl.ds(lat_me, 1)] = gain_s[pl.ds(3, 1)]
+    for flight in flights_d:
+        flight.wait()
+    total = jnp.sum(got_d[...].astype(F32), axis=0)
+    turned = jnp.transpose(total[:, 192:288])
+    for i in range(2):
+        qkv_ref[i] = total[:12, 96 * i : 96 * i + 36]
+        proj_ref[i] = total[:12, 96 * i + 36 : 96 * i + 48]
+        fc1_ref[i] = total[:12, 96 * i + 48 : 96 * i + 96]
+        fc2_ref[i] = turned[48 * i : 48 * i + 48, :12]
+    gains = gain_d[0]
+    for o in range(1, lat_count):
+        gains = gains + gain_d[o]
+    for i in range(2):
+        gain_ref[i] = gains[2 * i : 2 * i + 2, :DIM]
+
+
+def reduce_all(first_w, second_w, first_g, second_g):
+    vmem = pl.BlockSpec(memory_space=pltpu.VMEM)
+    dma = pltpu.SemaphoreType.DMA
+    shapes = ((2, 12, 36), (2, 12, 12), (2, 12, 48), (2, 48, 12), (2, 2, DIM), (2, 6, 207))
+    return pl.pallas_call(
+        reduce_kernel,
+        in_specs=[vmem] * 4,
+        out_specs=[vmem] * 6,
+        out_shape=[jax.ShapeDtypeStruct(s, F32) for s in shapes],
+        scratch_shapes=[
+            pltpu.VMEM((2, 8, 240, 128), BF),
+            pltpu.VMEM((2, 8, 240, 128), BF),
+            pltpu.VMEM((2, 4, 2, 240, 128), BF),
+            pltpu.VMEM((2, 2, 240, 128), BF),
+            pltpu.VMEM((2, 240, 128), BF),
+            pltpu.VMEM((16, 16, 384), BF),
+            pltpu.VMEM((16, 16, 384), BF),
+            pltpu.VMEM((4, 8, 256), F32),
+            pltpu.VMEM((8, 256), F32),
+            pltpu.VMEM((4, 8, 256), F32),
+            pltpu.VMEM((8, 256), F32),
+            pltpu.VMEM((16, 8, 256), F32),
+            dma((3,)), dma((3,)), dma((9,)), dma((9,)), dma((3,)), dma((3,)), dma((30,)), dma((30,)),
+        ],
+        compiler_params=pltpu.CompilerParams(
+            collective_id=2, has_side_effects=True, vmem_limit_bytes=48 * 1024 * 1024
+        ),
+    )(first_w, second_w, first_g, second_g)
 
 
 def whole(shape):
@@ -331,14 +643,8 @@
 
 
 PARAMS = pltpu.CompilerParams(vmem_limit_bytes=48 * 1024 * 1024)
-GRADS = (
-    ((3 * DIM, DIM), BF),
-    ((DIM, DIM), BF),
-    ((HID, DIM), BF),
-    ((DIM, HID), BF),
-    ((2, DIM), F32),
-    ((8, POS), F32),
-)
+GRADS = [((2, DIM), F32), ((16, 240, 128), BF)]
+SENT = [((112, DIM), BF), ((48, DIM), BF), ((48, DIM), BF)]
 
 
 def call(kernel, in_specs, outs, scratch, args):
@@ -358,77 +664,48 @@
     return call(
         first_kernel,
         [whole(full), whole(full), whole((TOK, TOK)), whole((276, 512)), whole((8, POS))] + weight_specs(0),
-        [((TOK, DIM), BF)] * 6 + [((TOK, DIM), BF), ((TOK, DIM), F32), ((TOK, HID), BF), ((TOK, HID), BF),
-         ((2, HEADS * WIN, WIN), BF)],
+        [((224, DIM), BF), ((224, DIM), BF), ((80, DIM), BF), ((80, DIM), BF)] + [((TOK, DIM), BF)] * 5
+        + [((TOK, DIM), F32), ((TOK, HID), BF), ((TOK, HID), BF), ((2, HEADS * WIN, WIN), BF)],
         [pltpu.VMEM((2, 8 * WIN, 128), F32)],
         (state, cot, token_order(), lane_order(), table) + weights,
     )
 
 
-def second(last, u, cot, table, weights):
+def second(last, pieces, table, weights):
     return call(
         second_kernel,
-        [pl.BlockSpec(memory_space=pltpu.SMEM), whole((TOK, DIM)), whole((TOK, DIM)), whole((276, 512)),
-         whole((8, POS))] + weight_specs(1),
-        [((TOK, DIM), F32)] + list(GRADS),
-        [pltpu.VMEM((2, 8 * WIN, 128), F32), pltpu.VMEM((2, HEADS * WIN, WIN), BF), pltpu.VMEM((2, 8 * WIN, 128), F32)],
-        (last, u, cot, lane_order(), table) + weights,
-    )
-
-
-def third(saved, cot, weights):
+        [pl.BlockSpec(memory_space=pltpu.SMEM)] + [whole(p.shape) for p in pieces]
+        + [whole((276, 512)), whole((8, POS))] + weight_specs(1),
+        [((112, DIM), F32)] + SENT + GRADS,
+        [pltpu.VMEM((2, 8 * WIN, 128), F32), pltpu.VMEM((2, HEADS * WIN, WIN), BF),
+         pltpu.VMEM((2, 8 * WIN, 128), F32)],
+        (last, *pieces, lane_order(), table) + weights,
+    )
+
+
+def third(saved, pieces, weights):
     return call(
         third_kernel,
-        [whole((TOK, DIM))] * 6 + [whole((TOK, HID))] * 2 + [whole((2, HEADS * WIN, WIN)), whole((TOK, DIM)),
-         whole((TOK, TOK)), whole((276, 512))] + weight_specs(0),
-        [((2, 6, 24, DIM), F32)] + list(GRADS),
+        [whole(a.shape) for a in (*saved, *pieces)] + [whole((TOK, TOK)), whole((276, 512))] + weight_specs(0),
+        [((2, 6, 24, DIM), F32)] + GRADS,
         [pltpu.VMEM((2, 8 * WIN, 128), F32)],
-        tuple(saved) + (cot, token_order(), lane_order()) + weights,
-    )
-
-
-def from_behind(value, axis, steps):
-    count = lax.axis_size(axis)
-    pairs = [(source, (source + steps) % count) for source in range(count)]
-    return lax.ppermute(value, axis, pairs)
-
-
-def sent_and_summed(array, axis, dim):
-    count = lax.axis_size(axis)
-    dims = array.shape
-    parts = array.reshape(*dims[:dim], count, dims[dim] // count, *dims[dim + 1 :])
-    parts = lax.all_to_all(jnp.moveaxis(parts, dim, 0), axis, 0, 0, tiled=True)
-    return jnp.sum(parts.astype(F32), axis=0)
+        (*saved, *pieces, token_order(), lane_order()) + weights,
+    )
 
 
 def body(state, out_cot, qkv_weight, proj_weight, fc1_weight, fc2_weight, norm_gain, bias_table):
     weights = (norm_gain, qkv_weight, proj_weight, fc1_weight, fc2_weight)
     tables = jnp.pad(bias_table[:, 0, 0], ((0, 0), (0, 2), (0, 0)))
-    one, cot, *saved = first(state, out_cot, tables[0], weights)
-    paired = jnp.stack((one, cot)).reshape(2, 2, 2, 72, DIM)
-    arrived = from_behind(paired[:, :, 0], LAT, -1)
-    paired = jnp.stack((arrived, paired[:, :, 1]), 2)
-    arrived = from_behind(paired[:, 0, :, :36], LON, -1)
-    following = jnp.stack((paired[:, 1, :, :36], arrived), 1)
-    paired = jnp.concatenate((paired[:, :, :, 36:], following), 3).reshape(2, TOK, DIM)
+    own, *leaving, = first(state, out_cot, tables[0], weights)
+    leaving, saved = leaving[:3], leaving[3:]
+    arrived = halo(leaving, -1, 0)
     last = (lax.axis_index(LAT) == lax.axis_size(LAT) - 1).astype(jnp.int32).reshape(1)
-    du, *second_grads = second(last, paired[0], paired[1], tables[1], weights)
-    du = du.reshape(2, 2, 72, DIM)
-    arrived = from_behind(du[1, :, 36:].astype(BF), LON, 1).astype(F32)
-    before = jnp.stack((arrived, du[0, :, 36:]))
-    du = jnp.concatenate((before, du[:, :, :36]), 2)
-    arrived = from_behind(du[:, 0].astype(BF), LAT, 1).astype(F32)
-    du = jnp.stack((arrived, du[:, 1]), 1).reshape(TOK, DIM)
-    state_grad, *first_grads = third(saved[:], du, weights)
-    summed = []
-    for i in range(4):
-        both = jnp.stack((first_grads[i], second_grads[i]))
-        both = lax.psum_scatter(both, LON, scatter_dimension=1, tiled=True)
-        summed.append(jnp.swapaxes(sent_and_summed(both, LAT, 2), 1, 2))
-    gain_grad = lax.psum(jnp.stack((first_grads[4], second_grads[4])), LAT_LON)
-    table_grad = jnp.stack((first_grads[5], second_grads[5]))[:, None, None, :6].astype(BF)
-    table_grad = sent_and_summed(table_grad, LON, 4)
-    return (state_grad, *summed, gain_grad, table_grad)
+    mine, *leaving = second(last, (own, *arrived), tables[1], weights)
+    leaving, second_grads = leaving[:3], leaving[3:]
+    arrived = halo(leaving, 1, 1)
+    state_grad, *first_grads = third(saved, (mine, *arrived), weights)
+    *summed, table_grad = reduce_all(first_grads[1], second_grads[1], first_grads[0], second_grads[0])
+    return (state_grad, *summed, table_grad[:, None, None])
 
 
 def solution(mesh):

time: 343 us -> 114 us (0.33)
  the two profiles are of different devices: /device:TPU:2 before, /device:TPU:20 now
where the time goes in v2:
time: 114 us; the launch traced here: 113 us
  Pallas kernels  74.3 us (65%)
  local copies, waits for them, and re-layouts  38.3 us (34%)
    unnamed x104, local copies, waits for them, and re-layouts  37.6 us
    pallas_call x1, Pallas kernels, reduce_all(): pl.pallas_call(reduce_kernel, in_specs=[vmem] * 4, out_specs=[vmem] * 6,...  37.5 us
    pallas_call x2, Pallas kernels, halo(): pl.pallas_call(functools.partial(halo_kernel, step), in_specs=[vmem] * 3,...  21.3 us
    pallas_call x3, Pallas kernels, call(): pl.pallas_call(kernel, grid=(1,), in_specs=in_specs, out_specs=[whole(s)...  15.5 us

profile of v2, /device:TPU:20, one launch (start us, length us, event | category | flops | bytes accessed | tf_op | source)
XLA Modules:
  0.0 113.5 jit_solution(6664300770632891687)
XLA Ops:
  0.6 1.0 copy.39
  2.4 1.4 %copy.30.w_fc2 = bf16[2,768,192]{2,1,0:T(8,128)(2,1)S(1)} copy(bf16[2,768,192]{1,2,0:T(8,128)(2,1)} %param.18) | data formatting | bytes 1179648 | tf_op args[5]
  3.9 3.0 %shard_map.180 = (bf16[224,192]{1,0:T(8,128)(2,1)S(1)}, bf16[224,192]{1,0:T(8,128)(2,1)S(1)}, bf16[80,192]{1,0:T(8,128)(2,1)S(1)}, bf16[80,192]{1,0:T(8,128)(2,1...) custom-call(bf16[2,6,24,192]{3,2,1,0:T(8,128)(2,1)S(1)} %copy-done.1, ...), custom_call_target="tpu_custom_call" | custom-call | tf_op jit(solution)/shard_map/pallas_call | solution.py:651
  7.0 0.9 copy-done.5
  16.0 12.0 %shard_map.181 = (bf16[224,192]{1,0:T(8,128)(2,1)}, bf16[80,192]{1,0:T(8,128)(2,1)}, bf16[80,192]{1,0:T(8,128)(2,1)}) custom-call(bf16[224,192]{1,0:T(8,128)(2,1)} %copy-done.27, bf16[80,192]{1,0:T(8,128)(2,1)} %copy-done.35, bf16[80,192]{1,0:T(8,128)(2,1)} %copy-done.36), custom_call_target="tpu_custom_call" | custom-call | tf_op jit(solution)/shard_map/pallas_call | solution.py:463
  28.7 0.9 copy-done.12
  29.6 0.9 copy-done.31
  30.5 0.9 copy-done.32
  33.0 6.8 %shard_map.182 = (f32[112,192]{1,0:T(8,128)S(1)}, bf16[112,192]{1,0:T(8,128)(2,1)S(1)}, bf16[48,192]{1,0:T(8,128)(2,1)S(1)}, bf16[48,192]{1,0:T(8,128)(2,1)S(1)}...) custom-call(s32[1]{0:T(128)} %bitcast.2.last, bf16[224,192]{1,0:T(8,128)(2,1)S(1)} %copy-done.31, ...), custom_call_target="tpu_custom_call" | custom-call | tf_op jit(solution)/shard_map/pallas_call | solution.py:651
  42.8 9.2 %shard_map.183 = (bf16[112,192]{1,0:T(8,128)(2,1)}, bf16[48,192]{1,0:T(8,128)(2,1)}, bf16[48,192]{1,0:T(8,128)(2,1)}) custom-call(bf16[112,192]{1,0:T(8,128)(2,1)} %copy-done.34, bf16[48,192]{1,0:T(8,128)(2,1)} %copy-done.44, bf16[48,192]{1,0:T(8,128)(2,1)} %copy-done.45), custom_call_target="tpu_custom_call" | custom-call | tf_op jit(solution)/shard_map/pallas_call | solution.py:463
  52.7 1.2 %copy-done.6 = bf16[2,864,144]{2,1,0:T(8,128)(2,1)S(1)} copy-done((bf16[2,864,144]{2,1,0:T(8,128)(2,1)S(1)}, bf16[2,864,144]{2,1,0:T(8,128)(2,1)}, u32[]{:S(2)}) %copy-start.6) | copy-done | bytes 497688
  53.9 1.0 copy-done.9
  54.9 1.0 copy-done.11
  55.9 1.0 copy-done.14
  56.9 0.9 copy-done.18
  57.8 0.9 copy-done.20
  58.7 0.9 copy-done.22
  59.6 0.9 copy-done.24
  60.5 0.9 copy-done.26
  61.4 0.9 copy-done.29
  62.3 0.8 copy-done.33
  64.6 5.7 %shard_map.184 = (f32[2,6,24,192]{3,2,1,0:T(8,128)}, f32[2,192]{1,0:T(2,128)S(1)}, bf16[16,240,128]{2,1,0:T(8,128)(2,1)}) custom-call(bf16[288,192]{1,0:T(8,128)(2,1)S(1)} %copy-done.18, bf16[288,192]{1,0:T(8,128)(2,1)S(1)} %copy-done.20, bf16[288,192]{1,0:T(8,128)(2,1)S(1)} %copy-done.22, bf16[288,192]{1,0:T(8,128)(2,1)S(1)} %copy-done.24, ...), custom_call_target="tpu_custom_call" | custom-call | tf_op jit(solution)/shard_map/pallas_call | solution.py:651
  71.0 1.2 %copy-done.4 = bf16[16,240,128]{2,1,0:T(8,128)(2,1)S(1)} copy-done((bf16[16,240,128]{2,1,0:T(8,128)(2,1)S(1)}, bf16[16,240,128]{2,1,0:T(8,128)(2,1)}, u32[]{:S(2)}) %copy-start.4) | copy-done | bytes 983064
  72.2 37.5 %shard_map.185 = (f32[2,12,36]{2,1,0:T(8,128)S(1)}, f32[2,12,12]{2,1,0:T(8,128)S(1)}, f32[2,12,48]{2,1,0:T(8,128)S(1)}, f32[2,48,12]{2,1,0:T(8,128)S(1)}, f32[2,...) custom-call(bf16[16,240,128]{2,1,0:T(8,128)(2,1)S(1)} %copy-done.4, bf16[16,240,128]{2,1,0:T(8,128)(2,1)S(1)} %get-tuple-element.66.second_w, ...), custom_call_target="tpu_custom_call" | custom-call | tf_op jit(solution)/shard_map/pallas_call | solution.py:601
  (88 shorter events, 20.7 us)
Async XLA Ops:
  1.6 2.2 %copy-start.15 = (bf16[2,6,24,192]{3,2,1,0:T(8,128)(2,1)S(1)}, bf16[2,6,24,192]{3,2,1,0:T(8,128)(2,1)}, u32[]{:S(2)}) copy-start(bf16[2,6,24,192]{3,2,1,0:T(8,128)(2,1)} %state.1) | copy-start | bytes 331780
  1.7 2.2 %copy-start.16 = (bf16[2,6,24,192]{3,2,1,0:T(8,128)(2,1)S(1)}, bf16[2,6,24,192]{3,2,1,0:T(8,128)(2,1)}, u32[]{:S(2)}) copy-start(bf16[2,6,24,192]{3,2,1,0:T(8,128)(2,1)} %cot.1) | copy-start | bytes 331780
  1.7 2.2 %copy-start.3 = (bf16[2,192,192]{2,1,0:T(8,128)(2,1)S(1)}, bf16[2,192,192]{2,1,0:T(8,128)(2,1)}, u32[]{:S(2)}) copy-start(bf16[2,192,192]{2,1,0:T(8,128)(2,1)} %w_proj.5) | copy-start | bytes 442372
  1.7 2.2 %copy-start.7 = (bf16[288,288]{1,0:T(8,128)(2,1)S(1)}, bf16[288,288]{1,0:T(8,128)(2,1)}, u32[]{:S(2)}) copy-start(bf16[288,288]{1,0:T(8,128)(2,1)} %constant.23.clone.order) | copy-start | bytes 497668
  2.4 1.5 %copy-start = (bf16[2,192,768]{2,1,0:T(8,128)(2,1)S(1)}, bf16[2,192,768]{2,1,0:T(8,128)(2,1)}, u32[]{:S(2)}) copy-start(bf16[2,192,768]{2,1,0:T(8,128)(2,1)} %w_fc1.5) | copy-start | bytes 1769476
  2.4 1.5 %copy-start.1 = (bf16[2,192,576]{2,1,0:T(8,128)(2,1)S(1)}, bf16[2,192,576]{2,1,0:T(8,128)(2,1)}, u32[]{:S(2)}) copy-start(bf16[2,192,576]{2,1,0:T(8,128)(2,1)} %w_qkv.5) | copy-start | bytes 1327108
  2.4 1.5 %copy-start.2 = (bf16[276,512]{1,0:T(8,128)(2,1)S(1)}, bf16[276,512]{1,0:T(8,128)(2,1)}, u32[]{:S(2)}) copy-start(bf16[276,512]{1,0:T(8,128)(2,1)} %constant.24.clone.lanes) | copy-start | bytes 847876
  2.4 1.5 %copy-start.39 = (f32[2,2,192]{2,1,0:T(2,128)S(1)}, f32[2,2,192]{2,1,0:T(2,128)}, u32[]{:S(2)}) copy-start(f32[2,2,192]{2,1,0:T(2,128)} %gains.5) | copy-start | bytes 9220
  7.0 0.9 copy-start.5
  28.7 0.9 copy-start.12
  29.6 0.9 copy-start.31
  30.5 0.9 copy-start.32
  52.7 1.2 %copy-start.6 = (bf16[2,864,144]{2,1,0:T(8,128)(2,1)S(1)}, bf16[2,864,144]{2,1,0:T(8,128)(2,1)}, u32[]{:S(2)}) copy-start(bf16[2,864,144]{2,1,0:T(8,128)(2,1)} %copy-done.5) | copy-start | bytes 1492996
  53.9 1.0 copy-start.9
  54.9 1.0 copy-start.11
  55.9 1.0 copy-start.14
  56.9 0.9 copy-start.18
  57.8 0.9 copy-start.20
  58.7 0.9 copy-start.22
  59.6 0.9 copy-start.24
  60.5 0.9 copy-start.26
  61.4 0.9 copy-start.29
  62.3 0.8 copy-start.33
  71.0 1.2 %copy-start.4 = (bf16[16,240,128]{2,1,0:T(8,128)(2,1)S(1)}, bf16[16,240,128]{2,1,0:T(8,128)(2,1)}, u32[]{:S(2)}) copy-start(bf16[16,240,128]{2,1,0:T(8,128)(2,1)} %get-tuple-element.65.first_w) | copy-start | bytes 2949124
  (24 other events, 16.2 us)

commit v3 on v1

v3 whole, which is shorter than its diff:
```python
import jax
import jax.numpy as jnp
import ml_dtypes
import numpy as np
from jax import lax
from jax.experimental import pallas as pl
from jax.experimental.pallas import tpu as pltpu
from jax.sharding import Mesh
from jax.sharding import PartitionSpec as P

WZ = 2
WH = 6
WW = 12
LAT = ("lat_0", "lat_1")
LON = ("lon_0", "lon_1", "lon_2")
BF = jnp.bfloat16
F32 = jnp.float32
HEADS = 6
DIM = 192
HEAD = 32
WIN = 144
TOK = 288
HID = 768
POS = 3312
SCALE = HEAD**-0.5


def token_order():
    order = np.zeros((TOK, TOK), np.float32)
    row = 0
    for n in range(2):
        for ih in range(2):
            for w in range(WW):
                for z in range(2):
                    for il in range(3):
                        source = (z * 6 + ih * 3 + il) * 24 + n * WW + w
                        order[row, source] = 1
                        row += 1
    return order.astype(ml_dtypes.bfloat16)


def lane_order():
    order = np.zeros((276, 512), np.float32)
    for a in range(12):
        for d in range(23):
            order[a * 23 + d, (a // 6) * 256 + d * 6 + a % 6] = 1
    return order.astype(ml_dtypes.bfloat16)


def table_offsets(flip):
    offsets = {}
    for b in range(12):
        for a in range(12):
            hk, zk, lk = b // 6, b % 6 // 3, b % 3
            hq, zq, lq = a // 6, a % 6 // 3, a % 3
            if flip:
                hk, zk, hq, zq = 1 - hk, 1 - zk, 1 - hq, 1 - zq
            offsets[b, a] = (zq * 2 + zk) * 828 + ((hq * 3 + lq) * 6 + hk * 3 + lk) * 23
    return offsets


def nn(a, b):
    return lax.dot_general(a, b, (((1,), (0,)), ((), ())), preferred_element_type=F32)


def nt(a, b):
    return lax.dot_general(a, b, (((1,), (1,)), ((), ())), preferred_element_type=F32)


def tn(a, b):
    return lax.dot_general(a, b, (((0,), (0,)), ((), ())), preferred_element_type=F32)


def two_pieces(x):
    high = x.astype(BF)
    return high, (x - high.astype(F32)).astype(BF)


def three_pieces(x):
    high = x.astype(BF)
    rest = x - high.astype(F32)
    middle = rest.astype(BF)
    return high, middle, (rest - middle.astype(F32)).astype(BF)


def expand_bias(table, lanes, flip, bias_ref):
    offsets = table_offsets(flip)
    rows = []
    for b in range(12):
        rows.append(
            jnp.concatenate(
                [table[:, offsets[b, a] : offsets[b, a] + 23] for a in range(12)], axis=1
            )
        )
    stacked = jnp.concatenate(rows, axis=0)
    high, middle, low = three_pieces(stacked)
    spread = nn(high, lanes) + nn(middle, lanes) + nn(low, lanes)
    for b in range(12):
        block = spread[b * 8 : b * 8 + 8]
        for w in range(WW):
            start = (11 - w) * 6
            both = jnp.concatenate(
                (block[:, start : start + 72], block[:, 256 + start : 256 + start + 72]), axis=1
            )
            row = (b // 6) * 72 + w * 6 + b % 6
            right = jnp.concatenate((both[:, 128:], jnp.zeros((8, 112), F32)), axis=1)
            bias_ref[0, pl.ds(row, 8, stride=WIN), :] = both[:, :128]
            bias_ref[1, pl.ds(row, 8, stride=WIN), :] = right


def reduce_bias(grad_ref, lanes, flip):
    offsets = table_offsets(flip)
    rows = []
    for b in range(12):
        left = jnp.zeros((8, 256), F32)
        right = jnp.zeros((8, 256), F32)
        for w in range(WW):
            start = (11 - w) * 6
            row = (b // 6) * 72 + w * 6 + b % 6
            both = jnp.concatenate(
                (
                    grad_ref[0, pl.ds(row, 8, stride=WIN), :],
                    grad_ref[1, pl.ds(row, 8, stride=WIN), :][:, :16],
                ),
                axis=1,
            )
            left = left + jnp.pad(both[:, :72], ((0, 0), (start, 184 - start)))
            right = right + jnp.pad(both[:, 72:], ((0, 0), (start, 184 - start)))
        rows.append(jnp.concatenate((left, right), axis=1))
    stacked = jnp.concatenate(rows, axis=0)
    high, low = two_pieces(stacked)
    packed = nt(high, lanes) + nt(low, lanes)
    places = sorted((start, b, a) for (b, a), start in offsets.items())
    return jnp.concatenate(
        [packed[b * 8 : b * 8 + 8, a * 23 : a * 23 + 23] for _, b, a in places], axis=1
    )


def pack_chunks(qkv, proj, fc1, fc2, table, out_ref):
    table = jnp.concatenate((table, jnp.zeros((8, 256), F32)), axis=1)
    for b in range(16):
        rows = jnp.concatenate(
            [qkv[36 * b : 36 * b + 36], proj[12 * b : 12 * b + 12], fc1[48 * b : 48 * b + 48]]
            + [part[12 * b : 12 * b + 12] for part in fc2],
            axis=0,
        )
        right = rows[:, 128:]
        own = table[:, 207 * b : 207 * b + 207]
        own = jnp.concatenate((own, jnp.zeros((8, 49), F32)), axis=1)
        chunk = jnp.concatenate(
            (
                rows[:, :128],
                jnp.concatenate((right[:72], right[72:]), axis=1),
                own[:, :128],
                own[:, 128:],
                jnp.zeros((8, 128), F32),
            ),
            axis=0,
        )
        y, x, core = b // 4, b // 2 % 2, b % 2
        out_ref[core * 8 + y * 2 + x] = chunk.astype(BF)


def unpack_chunk(chunk):
    right = jnp.concatenate((chunk[144:216, :64], chunk[144:216, 64:]), axis=0)
    return jnp.concatenate((chunk[:144], right), axis=1)


def normed(u):
    mean = jnp.mean(u, -1, keepdims=True)
    centred = u - mean
    scale = lax.rsqrt(jnp.mean(centred * centred, -1, keepdims=True) + 1e-05)
    return centred * scale, scale


def normed_back(grad, unit, scale):
    mean = jnp.mean(grad, -1, keepdims=True)
    product = jnp.mean(grad * unit, -1, keepdims=True)
    return scale * (grad - mean - unit * product)


def head_masks():
    lane = lax.broadcasted_iota(jnp.int32, (1, DIM), 1) // HEAD
    return [(lane == h).astype(F32) for h in range(HEADS)]


def by_head(x, masks):
    return jnp.concatenate([x * m.astype(BF) for m in masks], axis=0)


def from_heads(x, masks):
    total = x[:WIN] * masks[0]
    for h in range(1, HEADS):
        total = total + x[h * WIN : h * WIN + WIN] * masks[h]
    return total


def forward(u, gains, w_qkv, w_proj, w_fc1, w_fc2, bias_ref, allowed, prob_ref):
    masks = head_masks()
    unit, _ = normed(u)
    n1 = (unit * gains[0:1]).astype(BF)
    q, k, v = (
        nn(n1, w_qkv[:, i * DIM : i * DIM + DIM]) for i in range(3)
    )
    joined = []
    for n in range(2):
        part = slice(n * WIN, n * WIN + WIN)
        scores = nt(by_head(k[part].astype(BF), masks), q[part].astype(BF))
        v_t = jnp.transpose(v[part]).astype(BF)
        out_t = []
        for h in range(HEADS):
            rows = slice(h * WIN, h * WIN + WIN)
            bias = jnp.concatenate((bias_ref[0, rows, :], bias_ref[1, rows, :16]), axis=1)
            s = scores[rows] * SCALE + bias
            if allowed is not None:
                s = jnp.where(allowed, s, -1e30)
            e = jnp.exp(s - jnp.max(s, 0, keepdims=True))
            p = (e * (1.0 / jnp.sum(e, 0, keepdims=True))).astype(BF)
            prob_ref[n, rows, :] = p
            out_t.append(nn(v_t[h * HEAD : h * HEAD + HEAD], p))
        joined.append(jnp.transpose(jnp.concatenate(out_t, axis=0)))
    o = jnp.concatenate(joined, axis=0).astype(BF)
    m = u + nn(o, w_proj)
    unit2, _ = normed(m)
    n2 = (unit2 * gains[1:2]).astype(BF)
    e = nn(n2, w_fc1)
    cdf = 0.5 * (1.0 + lax.erf(e * (0.5**0.5)))
    g = (e * cdf).astype(BF)
    slope = cdf + e * jnp.exp(e * e * -0.5) * 0.3989422804014327
    return q.astype(BF), k.astype(BF), v.astype(BF), o, m, g, slope.astype(BF)


def backward(u, q, k, v, o, m, g, slope, cot, gains, w_qkv, w_proj, w_fc1, w_fc2, lanes, flip, prob_ref, grad_ref, gain_ref, chunk_ref,
             meanwhile=None):
    grad_ref[...] = jnp.zeros_like(grad_ref)
    masks = head_masks()
    unit, scale = normed(u)
    n1 = (unit * gains[0:1]).astype(BF)
    unit2, scale2 = normed(m)
    n2 = (unit2 * gains[1:2]).astype(BF)
    y2 = cot.astype(BF)
    fc2 = [tn(y2, g[:, DIM * i : DIM * i + DIM]) for i in range(4)]
    dg = nn(y2, w_fc2).astype(BF).astype(F32)
    y1 = (dg * slope.astype(F32)).astype(BF)
    fc1 = tn(y1, n2)
    dn2 = nt(y1, w_fc1).astype(BF).astype(F32)
    gain_ref[1:2, :] = jnp.sum(dn2 * unit2, 0, keepdims=True)
    dm = cot + normed_back(dn2 * gains[1:2], unit2, scale2)
    yp = dm.astype(BF)
    proj = tn(yp, o)
    do = nt(yp, w_proj).astype(BF)
    if meanwhile is not None:
        meanwhile()
    dqs, dks, dvs = [], [], []
    for n in range(2):
        part = slice(n * WIN, n * WIN + WIN)
        do_n, q_n, k_n, v_n = do[part], q[part], k[part], v[part]
        dp = nt(by_head(v_n, masks), do_n)
        dvs.append(from_heads(nn(prob_ref[n], do_n), masks))
        k_t = jnp.transpose(k_n.astype(F32)).astype(BF)
        ds_all, dq_t = [], []
        for h in range(HEADS):
            rows = slice(h * WIN, h * WIN + WIN)
            p = prob_ref[n, rows, :].astype(F32)
            dp_h = dp[rows].astype(BF).astype(F32)
            ds = p * (dp_h - jnp.sum(p * dp_h, 0, keepdims=True))
            if n == 0:
                grad_ref[0, rows, :] = ds[:, :128]
                grad_ref[1, rows, :16] = ds[:, 128:]
            else:
                grad_ref[0, rows, :] += ds[:, :128]
                grad_ref[1, rows, :16] += ds[:, 128:]
            ds = (ds * SCALE).astype(BF)
            ds_all.append(ds)
            dq_t.append(nn(k_t[h * HEAD : h * HEAD + HEAD], ds))
        dqs.append(jnp.transpose(jnp.concatenate(dq_t, axis=0)))
        dks.append(from_heads(nn(jnp.concatenate(ds_all, axis=0), q_n), masks))
    dn1 = jnp.zeros((TOK, DIM), F32)
    qkv = []
    for i, parts in enumerate((dqs, dks, dvs)):
        d = jnp.concatenate(parts, axis=0).astype(BF)
        qkv.append(tn(d, n1))
        dn1 = dn1 + nt(d, w_qkv[:, i * DIM : i * DIM + DIM])
    dn1 = dn1.astype(BF).astype(F32)
    gain_ref[0:1, :] = jnp.sum(dn1 * unit, 0, keepdims=True)
    table = reduce_bias(grad_ref, lanes, flip)
    pack_chunks(jnp.concatenate(qkv, axis=0), proj, fc1, fc2, table, chunk_ref)
    return dm + normed_back(dn1 * gains[0:1], unit, scale)


def quarters(x):
    return {
        (n, ih, half): x[n * WIN + ih * 72 + half * 36 :][:36]
        for n in range(2)
        for ih in range(2)
        for half in range(2)
    }


def padded(pieces, rows):
    have = sum(p.shape[0] for p in pieces)
    return jnp.concatenate(list(pieces) + [jnp.zeros((rows - have, DIM), F32)], axis=0).astype(BF)


OWN = ((0, 1, 1), (1, 1, 0), (1, 1, 1))
BY_LAT = ((0, 0, 1), (1, 0, 0), (1, 0, 1))
BY_LON = ((0, 1, 0),)
BY_BOTH = ((0, 0, 0),)


def shifted(have):
    order = []
    for n in range(2):
        for ih in range(2):
            order += [(n, ih, 1), ((n + 1) % 2, ih, 0)]
    return jnp.concatenate([have[key] for key in order], axis=0)


def unshifted(x):
    have = {}
    row = 0
    for n in range(2):
        for ih in range(2):
            for key in ((n, ih, 1), ((n + 1) % 2, ih, 0)):
                have[key] = x[row : row + 36]
                row += 36
    return have


def whole_block(have):
    return jnp.concatenate(
        [have[n, ih, half] for n in range(2) for ih in range(2) for half in range(2)], axis=0
    )


def flat_rows(ref):
    return jnp.concatenate([ref[z, i].astype(F32) for z in range(2) for i in range(6)], axis=0)


MESH = pl.DeviceIdType.MESH


def ring(names):
    sizes = [lax.axis_size(name) for name in names]
    me = 0
    for name, size in zip(names, sizes):
        me = me * size + lax.axis_index(name)
    total = 1
    for size in sizes:
        total *= size

    def at(index):
        where = {}
        for name, size in reversed(list(zip(names, sizes))):
            where[name] = lax.rem(index, size)
            index = index // size
        return where

    return me, total, at


def kernel(state_in, cot_in, order_in, lanes_in, table_in, gains_in, w_qkv_in, w_proj_in, w_fc1_in, w_fc2_in,
           du_ref, qkv_ref, proj_ref, fc1_ref, fc2_ref, gain_ref, table_ref,
           state, cot, order, lanes, table, gains, w_qkv, w_proj, w_fc1, w_fc2,
           q_ref, k_ref, v_ref, o_ref, m_ref, g_ref, slope_ref, prob_first, prob_second, bias_ref, grad_ref, mine_ref,
           own_ref, out_lat, out_lon, out_both, in_lat, in_lon, in_both,
           back_lat, back_lon, back_both, home_lat, home_lon, home_both,
           chunk_first, chunk_second, gain_first, gain_second,
           got_a, sum_a, got_b, sum_b, got_c, sent_d, got_d,
           gain_s, gain_a, gain_b, gain_c, gain_d,
           load, send_h, recv_h, send_a, recv_a, send_b, recv_b, send_c, recv_c, send_d, recv_d):
    loads = [
        pltpu.make_async_copy(source, target, load.at[i])
        for i, (source, target) in enumerate(
            (
                (order_in, order),
                (state_in, state),
                (cot_in, cot),
                (table_in, table),
                (lanes_in, lanes),
                (gains_in, gains),
                (w_qkv_in, w_qkv),
                (w_proj_in, w_proj),
                (w_fc1_in, w_fc1),
                (w_fc2_in, w_fc2),
            )
        )
    ]
    for copy in loads:
        copy.start()
    core = lax.axis_index("lon_2")
    side = lax.axis_index("lon_1")
    y, y_count = lax.axis_index("lon_0"), lax.axis_size("lon_0")
    lat_me, lat_count, lat_at = ring(LAT)
    lon_me, lon_count, lon_at = ring(LON)
    core_peer = {"lon_2": 1 - core}
    side_peer = {"lon_1": 1 - side}

    def y_peer(o):
        return lax.rem(y + o, y_count)

    def lat_peer(o):
        return lax.rem(lat_me + o, lat_count)

    def neighbours(way):
        lat = lat_at(lax.rem(lat_me + way + lat_count, lat_count))
        lon = lon_at(lax.rem(lon_me + way + lon_count, lon_count))
        return lat, lon, {**lat, **lon}

    lower, upper = neighbours(-1), neighbours(1)
    peers = (
        [*lower, *upper, core_peer, side_peer]
        + [{"lon_0": y_peer(o)} for o in range(1, y_count)]
        + [lat_at(lat_peer(o)) for o in range(1, lat_count)]
    )
    barrier = pltpu.get_barrier_semaphore()
    for device in peers:
        pl.semaphore_signal(barrier, inc=1, device_id=device, device_id_type=MESH)

    def send(source, target, sems, i, device):
        copy = pltpu.make_async_remote_copy(
            src_ref=source, dst_ref=target, send_sem=sems[0].at[i], recv_sem=sems[1].at[i],
            device_id=device, device_id_type=MESH,
        )
        copy.start()
        return copy

    def table_of(block):
        return jnp.concatenate([table[block, h] for h in range(HEADS)] + [jnp.zeros((2, POS), F32)], axis=0)

    for copy in loads:
        copy.wait()
    perm = order[...]
    x = nn(perm, flat_rows(state).astype(BF))
    cot_rows = nn(perm, flat_rows(cot).astype(BF))
    expand_bias(table_of(0), lanes[...], False, bias_ref)
    first_weights = (w_qkv[0], w_proj[0], w_fc1[0], w_fc2[0])
    q, k, v, o, m, g, slope = forward(x, gains[0], *first_weights, bias_ref, None, prob_first)
    out = quarters(m + nt(g, w_fc2[0]))
    given = quarters(cot_rows)
    for ref, keys in ((own_ref, OWN), (out_lat, BY_LAT), (out_lon, BY_LON), (out_both, BY_BOTH)):
        ref[...] = padded([out[key] for key in keys] + [given[key] for key in keys], ref.shape[0])
    pl.semaphore_wait(barrier, len(peers))
    flights = [
        send(source, target, (send_h, recv_h), i, lower[i])
        for i, (source, target) in enumerate(((out_lat, in_lat), (out_lon, in_lon), (out_both, in_both)))
    ]
    for ref, value in ((q_ref, q), (k_ref, k), (v_ref, v), (o_ref, o), (m_ref, m), (g_ref, g), (slope_ref, slope)):
        ref[...] = value

    expand_bias(table_of(1), lanes[...], True, bias_ref)
    row = lax.broadcasted_iota(jnp.int32, (WIN, WIN), 0)
    lane = lax.broadcasted_iota(jnp.int32, (WIN, WIN), 1)
    same_z = (row % 6 // 3) == (lane % 6 // 3)
    same_h = (row // 72) == (lane // 72)
    allowed = same_z & (same_h | (jnp.full((WIN, WIN), lat_me, jnp.int32) < lat_count - 1))
    for flight in flights:
        flight.wait()
    out, given = {}, {}
    for ref, keys in ((own_ref, OWN), (in_lat, BY_LAT), (in_lon, BY_LON), (in_both, BY_BOTH)):
        rows = ref[...].astype(F32)
        for i, key in enumerate(keys):
            out[key] = rows[36 * i : 36 * i + 36]
            given[key] = rows[36 * (i + len(keys)) :][:36]
    u = shifted(out)
    weights = (w_qkv[1], w_proj[1], w_fc1[1], w_fc2[1])
    saved = forward(u, gains[1], *weights, bias_ref, allowed, prob_second)
    du = backward(
        u, *saved, shifted(given), gains[1], *weights, lanes[...], True, prob_second, grad_ref,
        gain_second, chunk_second,
    )
    have = unshifted(du)
    mine_ref[...] = jnp.concatenate([have[key] for key in OWN] + [jnp.zeros((4, DIM), F32)], axis=0)
    for ref, keys in ((back_lat, BY_LAT), (back_lon, BY_LON), (back_both, BY_BOTH)):
        ref[...] = padded([have[key] for key in keys], ref.shape[0])
    flights = [
        send(source, target, (send_h, recv_h), 3 + i, upper[i])
        for i, (source, target) in enumerate(((back_lat, home_lat), (back_lon, home_lon), (back_both, home_both)))
    ]

    parts = (chunk_second, chunk_first)
    flights_a, flights_b, flights_c = [None] * 3, [None] * 3, [None] * 3

    def start_a(i):
        flights_a[i] = send(parts[i].at[pl.ds((1 - core) * 8, 8)], got_a.at[i], (send_a, recv_a), i, core_peer)

    def start_b(i):
        flights_a[i].wait()
        sum_a[i] = (parts[i][pl.ds(core * 8, 8)].astype(F32) + got_a[i].astype(F32)).astype(BF)
        flights_b[i] = [
            send(sum_a.at[i, pl.ds(y_peer(o) * 2, 2)], got_b.at[i, y], (send_b, recv_b),
                 i * (y_count - 1) + o - 1, {"lon_0": y_peer(o)})
            for o in range(1, y_count)
        ]
        got_b[i, pl.ds(y, 1)] = sum_a[i, pl.ds(y * 2, 2)][None]

    def start_c(i):
        for flight in flights_b[i]:
            flight.wait()
        total = got_b[i, 0].astype(F32)
        for o in range(1, y_count):
            total = total + got_b[i, o].astype(F32)
        sum_b[i] = total.astype(BF)
        flights_c[i] = send(sum_b.at[i, 1 - side], got_c.at[i], (send_c, recv_c), i, side_peer)

    rows_of = [None, None]

    def finish_c(i):
        flights_c[i].wait()
        chunk = sum_b[i, pl.ds(side, 1)][0].astype(F32) + got_c[i].astype(F32)
        sums = jnp.concatenate((chunk[216:224], chunk[224:232]), axis=1)
        for h in range(HEADS):
            table_ref[1 - i, h] = sums[h : h + 1, :207]
        rows_of[1 - i] = unpack_chunk(chunk)

    start_a(0)

    for flight in flights:
        flight.wait()
    have = {}
    for ref, keys in ((mine_ref, OWN), (home_lat, BY_LAT), (home_lon, BY_LON), (home_both, BY_BOTH)):
        rows = ref[...].astype(F32)
        for i, key in enumerate(keys):
            have[key] = rows[36 * i : 36 * i + 36]
    x = nn(order[...], flat_rows(state).astype(BF))
    du = backward(
        x, q_ref[...], k_ref[...], v_ref[...], o_ref[...], m_ref[...], g_ref[...],
        slope_ref[...], whole_block(have), gains[0], *first_weights, lanes[...], False, prob_first, grad_ref,
        gain_first, chunk_first, meanwhile=lambda: start_b(0),
    )
    start_a(1)
    pad = jnp.zeros((2, 64), F32)
    gain_s[0] = jnp.concatenate(
        (
            jnp.concatenate((gain_first[...], pad), axis=1),
            jnp.concatenate((gain_second[...], pad), axis=1),
            jnp.zeros((4, 256), F32),
        ),
        axis=0,
    )
    flights_a[2] = send(gain_s.at[0], gain_a, (send_a, recv_a), 2, core_peer)
    start_c(0)
    start_b(1)
    flights_a[2].wait()
    gain_s[1] = gain_s[0] + gain_a[...]
    flights_b[2] = [
        send(gain_s.at[1], gain_b.at[y], (send_b, recv_b), 2 * (y_count - 1) + o - 1, {"lon_0": y_peer(o)})
        for o in range(1, y_count)
    ]
    gain_b[pl.ds(y, 1)] = gain_s[pl.ds(1, 1)]
    high, low = two_pieces(du)
    flat = tn(order[...], high) + tn(order[...], low)
    for z in range(2):
        for i in range(6):
            start = (z * 6 + i) * 24
            du_ref[z, i] = flat[start : start + 24]
    finish_c(0)
    for flight in flights_b[2]:
        flight.wait()
    total = gain_b[0]
    for o in range(1, y_count):
        total = total + gain_b[o]
    gain_s[2] = total
    flights_c[2] = send(gain_s.at[2], gain_c, (send_c, recv_c), 2, side_peer)
    start_c(1)
    flights_c[2].wait()
    gain_s[3] = gain_s[2] + gain_c[...]
    flights_d = [
        send(gain_s.at[3], gain_d.at[lat_me], (send_d, recv_d), o - 1, lat_at(lat_peer(o)))
        for o in range(1, lat_count)
    ]
    finish_c(1)
    across = jnp.concatenate([jnp.transpose(rows[:96]) for rows in rows_of], axis=1)
    for a in range(16):
        down, right = 96 + 12 * (a // 4), 48 * (a % 4)
        piece = jnp.concatenate(
            [across[12 * a : 12 * a + 12]]
            + [rows[down : down + 12, right : right + 48] for rows in rows_of]
            + [jnp.zeros((12, 96), F32)],
            axis=1,
        )
        sent_d[a] = jnp.concatenate((piece, jnp.zeros((4, 384), F32)), axis=0).astype(BF)
    flights_d += [
        send(sent_d.at[lat_peer(o)], got_d.at[lat_me], (send_d, recv_d), lat_count - 2 + o, lat_at(lat_peer(o)))
        for o in range(1, lat_count)
    ]
    got_d[pl.ds(lat_me, 1)] = sent_d[pl.ds(lat_me, 1)]
    gain_d[pl.ds(lat_me, 1)] = gain_s[pl.ds(3, 1)]
    for flight in flights_d:
        flight.wait()
    total = jnp.sum(got_d[...].astype(F32), axis=0)
    for i in range(2):
        qkv_ref[:, i, :] = total[:12, 96 * i : 96 * i + 36]
        proj_ref[:, i, :] = total[:12, 96 * i + 36 : 96 * i + 48]
        fc1_ref[:, i, :] = total[:12, 96 * i + 48 : 96 * i + 96]
        fc2_ref[:, i, :] = total[:12, 192 + 48 * i : 240 + 48 * i]
    sums = gain_d[0]
    for o in range(1, lat_count):
        sums = sums + gain_d[o]
    for i in range(2):
        gain_ref[i] = sums[2 * i : 2 * i + 2, :DIM]


def body(state, out_cot, qkv_weight, proj_weight, fc1_weight, fc2_weight, norm_gain, bias_table):
    vmem = pl.BlockSpec(memory_space=pltpu.VMEM)
    dma = pltpu.SemaphoreType.DMA
    args = (
        state, out_cot, token_order(), lane_order(), bias_table.reshape(2, HEADS, 1, POS), norm_gain,
        qkv_weight, proj_weight, fc1_weight, jnp.swapaxes(fc2_weight, 1, 2),
    )
    buffers = [(a.shape, a.dtype) for a in args] + [((TOK, DIM), BF)] * 4 + [
        ((TOK, DIM), F32),
        ((TOK, HID), BF),
        ((TOK, HID), BF),
        ((2, HEADS * WIN, WIN), BF),
        ((2, HEADS * WIN, WIN), BF),
        ((2, 8 * WIN, 128), F32),
        ((2, 8 * WIN, 128), F32),
        ((112, DIM), F32),
        ((224, DIM), BF),
        ((224, DIM), BF),
        ((80, DIM), BF),
        ((80, DIM), BF),
        ((224, DIM), BF),
        ((80, DIM), BF),
        ((80, DIM), BF),
        ((112, DIM), BF),
        ((48, DIM), BF),
        ((48, DIM), BF),
        ((112, DIM), BF),
        ((48, DIM), BF),
        ((48, DIM), BF),
        ((16, 240, 128), BF),
        ((16, 240, 128), BF),
        ((2, DIM), F32),
        ((2, DIM), F32),
        ((2, 8, 240, 128), BF),
        ((2, 8, 240, 128), BF),
        ((2, 4, 2, 240, 128), BF),
        ((2, 2, 240, 128), BF),
        ((2, 240, 128), BF),
        ((16, 16, 384), BF),
        ((16, 16, 384), BF),
        ((4, 8, 256), F32),
        ((8, 256), F32),
        ((4, 8, 256), F32),
        ((8, 256), F32),
        ((16, 8, 256), F32),
    ]
    shapes = (
        (2, 6, 24, DIM), (12, 2, 36), (12, 2, 12), (12, 2, 48), (12, 2, 48), (2, 2, DIM), (2, 6, 1, 207)
    )
    outs = pl.pallas_call(
        kernel,
        in_specs=[pl.BlockSpec(memory_space=pltpu.HBM)] * 10,
        out_specs=[vmem] * 7,
        out_shape=[jax.ShapeDtypeStruct(s, F32) for s in shapes],
        scratch_shapes=[pltpu.VMEM(s, d) for s, d in buffers]
        + [dma((10,)), dma((6,)), dma((6,)), dma((3,)), dma((3,)), dma((9,)), dma((9,)), dma((3,)), dma((3,)), dma((30,)), dma((30,))],
        compiler_params=pltpu.CompilerParams(
            collective_id=0, has_side_effects=True, vmem_limit_bytes=60 * 1024 * 1024
        ),
    )(*args)
    state_grad, qkv, proj, fc1, fc2, gain, table = outs
    return (
        state_grad,
        jnp.swapaxes(qkv, 0, 1),
        jnp.swapaxes(proj, 0, 1),
        jnp.swapaxes(fc1, 0, 1),
        jnp.transpose(fc2, (1, 2, 0)),
        gain,
        table.reshape(2, 1, 1, HEADS, 207),
    )


def solution(mesh):
    split = Mesh(mesh.devices.reshape(8, 2, 4, 2, 2), ("lat_0", "lat_1", "lon_0", "lon_1", "lon_2"))
    placed = (
        P(None, LAT, LON, None),
        P(None, LAT, LON, None),
        P(),
        P(),
        P(),
        P(),
        P(),
        P(None, LAT, None, None, None),
    )
    return jax.shard_map(
        body,
        mesh=split,
        in_specs=placed,
        out_specs=(
            P(None, LAT, LON, None),
            P(None, LAT, LON),
            P(None, LAT, LON),
            P(None, LAT, LON),
            P(None, LAT, LON),
            P(),
            P(None, LAT, None, None, LON),
        ),
        check_vma=False,
    )
```

time: 343 us -> 66.2 us (0.19)
  waiting for transfers between devices: 153 us -> 0 us
  blocking collectives: 79 us -> 0 us
  Pallas kernels: 15.5 us -> 59 us
  starting transfers between devices: 35.4 us -> 0 us
  local copies, waits for them, and re-layouts: 37.4 us -> 5.71 us
  between operations: 15.8 us -> 0.66 us
  other arithmetic: 5.89 us -> 0 us
    unnamed x3 -> x0, waiting for transfers between devices: 114 us -> none
    psum x1 -> x0, blocking collectives: 79 us -> none  [body(): gain_grad = lax.psum(jnp.stack((first_grads[4], second_grads[4])), LAT_LON)]
    pallas_call x3 -> x1, Pallas kernels: 15.5 us -> 59 us  [body(): pl.pallas_call(kernel, in_specs=[pl.BlockSpec(memory_space=pltpu.HBM)] *...]
    all_to_all x5 -> x0, starting transfers between devices: 27.9 us -> none  [sent_and_summed(): parts = lax.all_to_all(jnp.moveaxis(parts, dim, 0), axis, 0, 0, tiled=True)]
    all_to_all x5 -> x0, waiting for transfers between devices: 24.1 us -> none  [sent_and_summed(): parts = lax.all_to_all(jnp.moveaxis(parts, dim, 0), axis, 0, 0, tiled=True)]
    unnamed x111 -> x19, local copies, waits for them, and re-layouts: 27 us -> 5.71 us
    ppermute x4 -> x0, waiting for transfers between devices: 15.4 us -> none  [from_behind(): return lax.ppermute(value, axis, pairs)]
    ppermute x4 -> x0, starting transfers between devices: 7.37 us -> none  [from_behind(): return lax.ppermute(value, axis, pairs)]
  transfers between devices with their start and end apart: 11 -> 0, of which waited for: 9 -> 0; matrix products, arithmetic and copies ran while one was open for 4% -> 0% of each run, Pallas kernels for 0% -> 0%
where the time goes in v3:
time: 66.2 us; the launch traced here: 65.4 us
  Pallas kernels  59 us (89%)
  local copies, waits for them, and re-layouts  5.71 us (9%)
    pallas_call x1, Pallas kernels, body(): pl.pallas_call(kernel, in_specs=[pl.BlockSpec(memory_space=pltpu.HBM)] *...  59 us
    unnamed x19, local copies, waits for them, and re-layouts  5.71 us

profile of v3, /device:TPU:2, one launch (start us, length us, event | category | flops | bytes accessed | tf_op | source)
XLA Modules:
  0.0 65.4 jit_solution(13740489472464418547)
XLA Ops:
  0.6 59.0 %shard_map.153 = (f32[2,6,24,192]{3,2,1,0:T(8,128)}, f32[12,2,36]{2,1,0:T(2,128)}, f32[12,2,12]{2,1,0:T(2,128)}, f32[12,2,48]{2,1,0:T(2,128)}, f32[12,2,48]{2,1,...) custom-call(bf16[2,6,24,192]{3,2,1,0:T(8,128)(2,1)} %state_in.1, bf16[2,6,24,192]{3,2,1,0:T(8,128)(2,1)} %cot_in.1, ...), custom_call_target="tpu_custom_call" | custom-call | tf_op jit(solution)/shard_map/pallas_call | solution.py:653
  59.6 0.0 copy-start.4
  59.7 1.7 %copy.25 = f32[2,6,24,192]{3,2,1,0:T(8,128)} copy(f32[2,6,24,192]{3,2,1,0:T(8,128)} %get-tuple-element.35) | data formatting | bytes 442368
  61.4 0.0 copy-done.4
  61.4 0.0 copy-start.3
  61.4 0.6 copy.26
  62.0 0.1 copy-done.3
  62.1 0.0 copy-start.2
  62.1 0.6 copy.27
  62.7 0.1 copy-done.2
  62.8 0.0 copy-start.1
  62.8 0.6 copy.28
  63.4 0.1 copy-done.1
  63.5 0.0 copy-start.5
  63.5 0.0 copy-start
  63.5 0.6 copy.29
  64.1 0.1 copy-done.5
  64.2 0.6 copy.30
  64.8 0.0 copy-done
  64.8 0.6 copy.31
Async XLA Ops:
  59.6 1.7 %copy-start.4 = (f32[12,2,36]{2,1,0:T(2,128)S(1)}, f32[12,2,36]{2,1,0:T(2,128)}, u32[]{:S(2)}) copy-start(f32[12,2,36]{2,1,0:T(2,128)} %get-tuple-element.15) | copy-start | bytes 10372
  61.4 0.7 %copy-start.3 = (f32[12,2,12]{2,1,0:T(2,128)S(1)}, f32[12,2,12]{2,1,0:T(2,128)}, u32[]{:S(2)}) copy-start(f32[12,2,12]{2,1,0:T(2,128)} %get-tuple-element.16) | copy-start | bytes 3460
  62.1 0.7 %copy-start.2 = (f32[12,2,48]{2,1,0:T(2,128)S(1)}, f32[12,2,48]{2,1,0:T(2,128)}, u32[]{:S(2)}) copy-start(f32[12,2,48]{2,1,0:T(2,128)} %get-tuple-element.17) | copy-start | bytes 13828
  62.8 0.7 %copy-start.1 = (f32[12,2,48]{2,1,0:T(2,128)S(1)}, f32[12,2,48]{2,1,0:T(2,128)}, u32[]{:S(2)}) copy-start(f32[12,2,48]{2,1,0:T(2,128)} %get-tuple-element.18) | copy-start | bytes 13828
  63.5 0.7 %copy-start.5 = (f32[2,2,192]{2,1,0:T(2,128)S(1)}, f32[2,2,192]{2,1,0:T(2,128)}, u32[]{:S(2)}) copy-start(f32[2,2,192]{2,1,0:T(2,128)} %get-tuple-element.40) | copy-start | bytes 9220
  63.5 1.3 %copy-start = (f32[2,6,1,207]{3,2,1,0:T(1,128)S(1)}, f32[2,6,1,207]{3,2,1,0:T(1,128)}, u32[]{:S(2)}) copy-start(f32[2,6,1,207]{3,2,1,0:T(1,128)} %get-tuple-element.20) | copy-start | bytes 29812

commit v4 on v3

--- a/solution.py
+++ b/solution.py
@@ -136,34 +136,38 @@
     )
 
 
-def pack_chunks(qkv, proj, fc1, fc2, table, out_ref):
+def folded(rows):
+    half = rows.shape[0] // 2
+    right = rows[:, 128:]
+    return jnp.concatenate((rows[:, :128], jnp.concatenate((right[:half], right[half:]), axis=1)), axis=0)
+
+
+def unfolded(rows):
+    count = rows.shape[0] // 3 * 2
+    right = jnp.concatenate((rows[count:, :64], rows[count:, 64:]), axis=0)
+    return jnp.concatenate((rows[:count], right), axis=1)
+
+
+def place(b):
+    return b % 2 * 8 + b // 4 * 2 + b // 2 % 2
+
+
+def pack_mlp(fc1, fc2, out_ref):
+    for b in range(16):
+        rows = [fc1[48 * b : 48 * b + 48]] + [part[12 * b : 12 * b + 12] for part in fc2]
+        out_ref[place(b)] = folded(jnp.concatenate(rows, axis=0)).astype(BF)
+
+
+def pack_attention(qkv, proj, table, gains, out_ref):
     table = jnp.concatenate((table, jnp.zeros((8, 256), F32)), axis=1)
+    ends = jnp.concatenate((gains[0][:, 128:], gains[1][:, 128:]), axis=1)
+    tail = jnp.concatenate((gains[0][:, :128], gains[1][:, :128], ends, jnp.zeros((5, 128), F32)), axis=0)
     for b in range(16):
-        rows = jnp.concatenate(
-            [qkv[36 * b : 36 * b + 36], proj[12 * b : 12 * b + 12], fc1[48 * b : 48 * b + 48]]
-            + [part[12 * b : 12 * b + 12] for part in fc2],
-            axis=0,
-        )
-        right = rows[:, 128:]
+        rows = jnp.concatenate((qkv[36 * b : 36 * b + 36], proj[12 * b : 12 * b + 12]), axis=0)
         own = table[:, 207 * b : 207 * b + 207]
         own = jnp.concatenate((own, jnp.zeros((8, 49), F32)), axis=1)
-        chunk = jnp.concatenate(
-            (
-                rows[:, :128],
-                jnp.concatenate((right[:72], right[72:]), axis=1),
-                own[:, :128],
-                own[:, 128:],
-                jnp.zeros((8, 128), F32),
-            ),
-            axis=0,
-        )
-        y, x, core = b // 4, b // 2 % 2, b % 2
-        out_ref[core * 8 + y * 2 + x] = chunk.astype(BF)
-
-
-def unpack_chunk(chunk):
-    right = jnp.concatenate((chunk[144:216, :64], chunk[144:216, 64:]), axis=0)
-    return jnp.concatenate((chunk[:144], right), axis=1)
+        chunk = jnp.concatenate((folded(rows), own[:, :128], own[:, 128:], tail), axis=0)
+        out_ref[place(b)] = chunk.astype(BF)
 
 
 def normed(u):
@@ -195,7 +199,7 @@
     return total
 
 
-def forward(u, gains, w_qkv, w_proj, w_fc1, w_fc2, bias_ref, allowed, prob_ref):
+def forward(u, gains, w_qkv, w_proj, w_fc1, bias_ref, allowed, prob_ref, meanwhile=None):
     masks = head_masks()
     unit, _ = normed(u)
     n1 = (unit * gains[0:1]).astype(BF)
@@ -220,37 +224,37 @@
             out_t.append(nn(v_t[h * HEAD : h * HEAD + HEAD], p))
         joined.append(jnp.transpose(jnp.concatenate(out_t, axis=0)))
     o = jnp.concatenate(joined, axis=0).astype(BF)
-    m = u + nn(o, w_proj)
+    if meanwhile is not None:
+        meanwhile()
+    m = u + nn(o, w_proj[...])
     unit2, _ = normed(m)
     n2 = (unit2 * gains[1:2]).astype(BF)
-    e = nn(n2, w_fc1)
+    e = nn(n2, w_fc1[...])
     cdf = 0.5 * (1.0 + lax.erf(e * (0.5**0.5)))
     g = (e * cdf).astype(BF)
     slope = cdf + e * jnp.exp(e * e * -0.5) * 0.3989422804014327
     return q.astype(BF), k.astype(BF), v.astype(BF), o, m, g, slope.astype(BF)
 
 
-def backward(u, q, k, v, o, m, g, slope, cot, gains, w_qkv, w_proj, w_fc1, w_fc2, lanes, flip, prob_ref, grad_ref, gain_ref, chunk_ref,
-             meanwhile=None):
-    grad_ref[...] = jnp.zeros_like(grad_ref)
+def back_mlp(cot, m, slope, w_fc2):
+    unit, scale = normed(m)
+    y2 = cot.astype(BF)
+    dg = nn(y2, w_fc2).astype(BF).astype(F32)
+    return y2, (dg * slope.astype(F32)).astype(BF), unit, scale
+
+
+def back_middle(cot, y1, unit, scale, gain, w_fc1):
+    dn = nt(y1, w_fc1).astype(BF).astype(F32)
+    return cot + normed_back(dn * gain, unit, scale), jnp.sum(dn * unit, 0, keepdims=True)
+
+
+def mlp_grads(y2, y1, g, unit, gain):
+    n2 = (unit * gain).astype(BF)
+    return tn(y1, n2), [tn(y2, g[:, DIM * i : DIM * i + DIM]) for i in range(4)]
+
+
+def back_attention(do, q, k, v, prob_ref, grad_ref, meanwhile=None):
     masks = head_masks()
-    unit, scale = normed(u)
-    n1 = (unit * gains[0:1]).astype(BF)
-    unit2, scale2 = normed(m)
-    n2 = (unit2 * gains[1:2]).astype(BF)
-    y2 = cot.astype(BF)
-    fc2 = [tn(y2, g[:, DIM * i : DIM * i + DIM]) for i in range(4)]
-    dg = nn(y2, w_fc2).astype(BF).astype(F32)
-    y1 = (dg * slope.astype(F32)).astype(BF)
-    fc1 = tn(y1, n2)
-    dn2 = nt(y1, w_fc1).astype(BF).astype(F32)
-    gain_ref[1:2, :] = jnp.sum(dn2 * unit2, 0, keepdims=True)
-    dm = cot + normed_back(dn2 * gains[1:2], unit2, scale2)
-    yp = dm.astype(BF)
-    proj = tn(yp, o)
-    do = nt(yp, w_proj).astype(BF)
-    if meanwhile is not None:
-        meanwhile()
     dqs, dks, dvs = [], [], []
     for n in range(2):
         part = slice(n * WIN, n * WIN + WIN)
@@ -275,17 +279,22 @@
             dq_t.append(nn(k_t[h * HEAD : h * HEAD + HEAD], ds))
         dqs.append(jnp.transpose(jnp.concatenate(dq_t, axis=0)))
         dks.append(from_heads(nn(jnp.concatenate(ds_all, axis=0), q_n), masks))
-    dn1 = jnp.zeros((TOK, DIM), F32)
-    qkv = []
-    for i, parts in enumerate((dqs, dks, dvs)):
-        d = jnp.concatenate(parts, axis=0).astype(BF)
-        qkv.append(tn(d, n1))
-        dn1 = dn1 + nt(d, w_qkv[:, i * DIM : i * DIM + DIM])
-    dn1 = dn1.astype(BF).astype(F32)
-    gain_ref[0:1, :] = jnp.sum(dn1 * unit, 0, keepdims=True)
-    table = reduce_bias(grad_ref, lanes, flip)
-    pack_chunks(jnp.concatenate(qkv, axis=0), proj, fc1, fc2, table, chunk_ref)
-    return dm + normed_back(dn1 * gains[0:1], unit, scale)
+        if n == 0 and meanwhile is not None:
+            meanwhile()
+    return [jnp.concatenate(parts, axis=0).astype(BF) for parts in (dqs, dks, dvs)]
+
+
+def back_input(dm, d_qkv, unit, scale, gain, w_qkv):
+    dn = jnp.zeros((TOK, DIM), F32)
+    for i in range(3):
+        dn = dn + nt(d_qkv[i], w_qkv[:, i * DIM : i * DIM + DIM])
+    dn = dn.astype(BF).astype(F32)
+    return dm + normed_back(dn * gain, unit, scale), jnp.sum(dn * unit, 0, keepdims=True)
+
+
+def qkv_grads(d_qkv, unit, gain):
+    n1 = (unit * gain).astype(BF)
+    return jnp.concatenate([tn(d, n1) for d in d_qkv], axis=0)
 
 
 def quarters(x):
@@ -362,13 +371,11 @@
 def kernel(state_in, cot_in, order_in, lanes_in, table_in, gains_in, w_qkv_in, w_proj_in, w_fc1_in, w_fc2_in,
            du_ref, qkv_ref, proj_ref, fc1_ref, fc2_ref, gain_ref, table_ref,
            state, cot, order, lanes, table, gains, w_qkv, w_proj, w_fc1, w_fc2,
-           q_ref, k_ref, v_ref, o_ref, m_ref, g_ref, slope_ref, prob_first, prob_second, bias_ref, grad_ref, mine_ref,
-           own_ref, out_lat, out_lon, out_both, in_lat, in_lon, in_both,
-           back_lat, back_lon, back_both, home_lat, home_lon, home_both,
-           chunk_first, chunk_second, gain_first, gain_second,
-           got_a, sum_a, got_b, sum_b, got_c, sent_d, got_d,
-           gain_s, gain_a, gain_b, gain_c, gain_d,
-           load, send_h, recv_h, send_a, recv_a, send_b, recv_b, send_c, recv_c, send_d, recv_d):
+           q_ref, k_ref, v_ref, o_ref, m_ref, g_ref, slope_ref, prob_first, prob_second, bias_ref, grad_ref,
+           mine_ref, own_ref, *rest):
+    halos, rest = rest[:18], rest[18:]
+    parts, got_a, sum_a, got_b, sum_b, got_c = (rest[4 * i : 4 * i + 4] for i in range(6))
+    sent_d, got_d, load, send_h, recv_h, send_a, recv_a, send_b, recv_b, send_c, recv_c, send_d, recv_d = rest[24:]
     loads = [
         pltpu.make_async_copy(source, target, load.at[i])
         for i, (source, target) in enumerate(
@@ -428,23 +435,51 @@
     def table_of(block):
         return jnp.concatenate([table[block, h] for h in range(HEADS)] + [jnp.zeros((2, POS), F32)], axis=0)
 
-    for copy in loads:
+    def exchange(step, targets):
+        return [
+            send(halos[6 * step + i], halos[6 * step + 3 + i], (send_h, recv_h), 3 * step + i, targets[i])
+            for i in range(3)
+        ]
+
+    def fill(step, have):
+        for i, keys in enumerate((BY_LAT, BY_LON, BY_BOTH)):
+            ref = halos[6 * step + i]
+            ref[...] = padded([have[key] for key in keys], ref.shape[0])
+
+    def arrived(step, own):
+        have = {}
+        for ref, keys in zip((own, *halos[6 * step + 3 : 6 * step + 6]), (OWN, BY_LAT, BY_LON, BY_BOTH)):
+            rows = ref[...].astype(F32)
+            for i, key in enumerate(keys):
+                have[key] = rows[36 * i : 36 * i + 36]
+        return have
+
+    for copy in loads[:5]:
         copy.wait()
     perm = order[...]
     x = nn(perm, flat_rows(state).astype(BF))
-    cot_rows = nn(perm, flat_rows(cot).astype(BF))
+    given = quarters(nn(perm, flat_rows(cot).astype(BF)))
+    fill(0, given)
     expand_bias(table_of(0), lanes[...], False, bias_ref)
-    first_weights = (w_qkv[0], w_proj[0], w_fc1[0], w_fc2[0])
-    q, k, v, o, m, g, slope = forward(x, gains[0], *first_weights, bias_ref, None, prob_first)
+    for copy in loads[5:7]:
+        copy.wait()
+    first_gains, second_gains = gains[0], gains[1]
+    early = []
+
+    def open_halo():
+        for copy in loads[7:]:
+            copy.wait()
+        pl.semaphore_wait(barrier, len(peers))
+        early.extend(exchange(0, lower))
+
+    q, k, v, o, m, g, slope = forward(
+        x, first_gains, w_qkv[0], w_proj.at[0], w_fc1.at[0], bias_ref, None, prob_first, open_halo
+    )
     out = quarters(m + nt(g, w_fc2[0]))
-    given = quarters(cot_rows)
-    for ref, keys in ((own_ref, OWN), (out_lat, BY_LAT), (out_lon, BY_LON), (out_both, BY_BOTH)):
-        ref[...] = padded([out[key] for key in keys] + [given[key] for key in keys], ref.shape[0])
-    pl.semaphore_wait(barrier, len(peers))
-    flights = [
-        send(source, target, (send_h, recv_h), i, lower[i])
-        for i, (source, target) in enumerate(((out_lat, in_lat), (out_lon, in_lon), (out_both, in_both)))
-    ]
+    fill(1, out)
+    flights = early + exchange(1, lower)
+    own_ref[0] = padded([out[key] for key in OWN], 112)
+    own_ref[1] = padded([given[key] for key in OWN], 112)
     for ref, value in ((q_ref, q), (k_ref, k), (v_ref, v), (o_ref, o), (m_ref, m), (g_ref, g), (slope_ref, slope)):
         ref[...] = value
 
@@ -454,151 +489,150 @@
     same_z = (row % 6 // 3) == (lane % 6 // 3)
     same_h = (row // 72) == (lane // 72)
     allowed = same_z & (same_h | (jnp.full((WIN, WIN), lat_me, jnp.int32) < lat_count - 1))
+    grad_ref[...] = jnp.zeros_like(grad_ref)
     for flight in flights:
         flight.wait()
-    out, given = {}, {}
-    for ref, keys in ((own_ref, OWN), (in_lat, BY_LAT), (in_lon, BY_LON), (in_both, BY_BOTH)):
-        rows = ref[...].astype(F32)
-        for i, key in enumerate(keys):
-            out[key] = rows[36 * i : 36 * i + 36]
-            given[key] = rows[36 * (i + len(keys)) :][:36]
-    u = shifted(out)
-    weights = (w_qkv[1], w_proj[1], w_fc1[1], w_fc2[1])
-    saved = forward(u, gains[1], *weights, bias_ref, allowed, prob_second)
-    du = backward(
-        u, *saved, shifted(given), gains[1], *weights, lanes[...], True, prob_second, grad_ref,
-        gain_second, chunk_second,
-    )
+    u = shifted(arrived(1, own_ref.at[0]))
+    cot_u = shifted(arrived(0, own_ref.at[1]))
+    q, k, v, o, m, g, slope = forward(
+        u, second_gains, w_qkv[1], w_proj.at[1], w_fc1.at[1], bias_ref, allowed, prob_second
+    )
+    y2, y1, unit2, scale2 = back_mlp(cot_u, m, slope, w_fc2[1])
+    dm, gain2 = back_middle(cot_u, y1, unit2, scale2, second_gains[1:2], w_fc1[1])
+    yp = dm.astype(BF)
+    d_qkv = back_attention(nt(yp, w_proj[1]).astype(BF), q, k, v, prob_second, grad_ref)
+    unit1, scale1 = normed(u)
+    du, gain1 = back_input(dm, d_qkv, unit1, scale1, second_gains[0:1], w_qkv[1])
     have = unshifted(du)
+    fill(2, have)
+    flights = exchange(2, upper)
     mine_ref[...] = jnp.concatenate([have[key] for key in OWN] + [jnp.zeros((4, DIM), F32)], axis=0)
-    for ref, keys in ((back_lat, BY_LAT), (back_lon, BY_LON), (back_both, BY_BOTH)):
-        ref[...] = padded([have[key] for key in keys], ref.shape[0])
-    flights = [
-        send(source, target, (send_h, recv_h), 3 + i, upper[i])
-        for i, (source, target) in enumerate(((back_lat, home_lat), (back_lon, home_lon), (back_both, home_both)))
-    ]
-
-    parts = (chunk_second, chunk_first)
-    flights_a, flights_b, flights_c = [None] * 3, [None] * 3, [None] * 3
+
+    flights_a, flights_b, flights_c, done = [None] * 4, [None] * 4, [None] * 4, [None] * 4
 
     def start_a(i):
-        flights_a[i] = send(parts[i].at[pl.ds((1 - core) * 8, 8)], got_a.at[i], (send_a, recv_a), i, core_peer)
+        flights_a[i] = send(parts[i].at[pl.ds((1 - core) * 8, 8)], got_a[i], (send_a, recv_a), i, core_peer)
 
     def start_b(i):
         flights_a[i].wait()
-        sum_a[i] = (parts[i][pl.ds(core * 8, 8)].astype(F32) + got_a[i].astype(F32)).astype(BF)
+        sum_a[i][...] = (parts[i][pl.ds(core * 8, 8)].astype(F32) + got_a[i][...].astype(F32)).astype(BF)
         flights_b[i] = [
-            send(sum_a.at[i, pl.ds(y_peer(o) * 2, 2)], got_b.at[i, y], (send_b, recv_b),
+            send(sum_a[i].at[pl.ds(y_peer(o) * 2, 2)], got_b[i].at[y], (send_b, recv_b),
                  i * (y_count - 1) + o - 1, {"lon_0": y_peer(o)})
             for o in range(1, y_count)
         ]
-        got_b[i, pl.ds(y, 1)] = sum_a[i, pl.ds(y * 2, 2)][None]
+        got_b[i][pl.ds(y, 1)] = sum_a[i][pl.ds(y * 2, 2)][None]
 
     def start_c(i):
         for flight in flights_b[i]:
             flight.wait()
-        total = got_b[i, 0].astype(F32)
+        total = got_b[i][0].astype(F32)
         for o in range(1, y_count):
-            total = total + got_b[i, o].astype(F32)
-        sum_b[i] = total.astype(BF)
-        flights_c[i] = send(sum_b.at[i, 1 - side], got_c.at[i], (send_c, recv_c), i, side_peer)
-
-    rows_of = [None, None]
+            total = total + got_b[i][o].astype(F32)
+        sum_b[i][...] = total.astype(BF)
+        flights_c[i] = send(sum_b[i].at[1 - side], got_c[i], (send_c, recv_c), i, side_peer)
 
     def finish_c(i):
         flights_c[i].wait()
-        chunk = sum_b[i, pl.ds(side, 1)][0].astype(F32) + got_c[i].astype(F32)
-        sums = jnp.concatenate((chunk[216:224], chunk[224:232]), axis=1)
-        for h in range(HEADS):
-            table_ref[1 - i, h] = sums[h : h + 1, :207]
-        rows_of[1 - i] = unpack_chunk(chunk)
-
+        chunk = sum_b[i][pl.ds(side, 1)][0].astype(F32) + got_c[i][...].astype(F32)
+        if i % 2 == 0:
+            rows = unfolded(chunk)
+            done[i] = (jnp.transpose(rows[:48]), rows[48:])
+        else:
+            sums = jnp.concatenate((chunk[72:80], chunk[80:88]), axis=1)
+            for h in range(HEADS):
+                table_ref[1 - i // 2, h] = sums[h : h + 1, :207]
+            gain = jnp.concatenate(
+                (
+                    jnp.concatenate((chunk[88:89], chunk[90:91, :64]), axis=1),
+                    jnp.concatenate((chunk[89:90], chunk[90:91, 64:]), axis=1),
+                ),
+                axis=0,
+            )
+            done[i] = (jnp.transpose(unfolded(chunk[:72])), gain)
+
+    pack_mlp(*mlp_grads(y2, y1, g, unit2, second_gains[1:2]), parts[0])
     start_a(0)
+    pack_attention(
+        qkv_grads(d_qkv, unit1, second_gains[0:1]), tn(yp, o), reduce_bias(grad_ref, lanes[...], True),
+        (gain1, gain2), parts[1],
+    )
+    start_a(1)
 
     for flight in flights:
         flight.wait()
-    have = {}
-    for ref, keys in ((mine_ref, OWN), (home_lat, BY_LAT), (home_lon, BY_LON), (home_both, BY_BOTH)):
-        rows = ref[...].astype(F32)
-        for i, key in enumerate(keys):
-            have[key] = rows[36 * i : 36 * i + 36]
-    x = nn(order[...], flat_rows(state).astype(BF))
-    du = backward(
-        x, q_ref[...], k_ref[...], v_ref[...], o_ref[...], m_ref[...], g_ref[...],
-        slope_ref[...], whole_block(have), gains[0], *first_weights, lanes[...], False, prob_first, grad_ref,
-        gain_first, chunk_first, meanwhile=lambda: start_b(0),
-    )
-    start_a(1)
-    pad = jnp.zeros((2, 64), F32)
-    gain_s[0] = jnp.concatenate(
-        (
-            jnp.concatenate((gain_first[...], pad), axis=1),
-            jnp.concatenate((gain_second[...], pad), axis=1),
-            jnp.zeros((4, 256), F32),
-        ),
-        axis=0,
-    )
-    flights_a[2] = send(gain_s.at[0], gain_a, (send_a, recv_a), 2, core_peer)
+    cot_x = whole_block(arrived(2, mine_ref))
+    y2, y1, unit2, scale2 = back_mlp(cot_x, m_ref[...], slope_ref[...], w_fc2[0])
+    start_b(0)
+    pack_mlp(*mlp_grads(y2, y1, g_ref[...], unit2, first_gains[1:2]), parts[2])
+    start_a(2)
+    start_b(1)
+    dm, gain2 = back_middle(cot_x, y1, unit2, scale2, first_gains[1:2], w_fc1[0])
+    yp = dm.astype(BF)
+    do = nt(yp, w_proj[0]).astype(BF)
+    d_qkv = back_attention(
+        do, q_ref[...], k_ref[...], v_ref[...], prob_first, grad_ref, lambda: start_b(2)
+    )
     start_c(0)
-    start_b(1)
-    flights_a[2].wait()
-    gain_s[1] = gain_s[0] + gain_a[...]
-    flights_b[2] = [
-        send(gain_s.at[1], gain_b.at[y], (send_b, recv_b), 2 * (y_count - 1) + o - 1, {"lon_0": y_peer(o)})
-        for o in range(1, y_count)
-    ]
-    gain_b[pl.ds(y, 1)] = gain_s[pl.ds(1, 1)]
+    unit1, scale1 = normed(nn(order[...], flat_rows(state).astype(BF)))
+    du, gain1 = back_input(dm, d_qkv, unit1, scale1, first_gains[0:1], w_qkv[0])
+    pack_attention(
+        qkv_grads(d_qkv, unit1, first_gains[0:1]), tn(yp, o_ref[...]), reduce_bias(grad_ref, lanes[...], False),
+        (gain1, gain2), parts[3],
+    )
+    start_a(3)
+    start_c(1)
     high, low = two_pieces(du)
     flat = tn(order[...], high) + tn(order[...], low)
+    start_b(3)
     for z in range(2):
         for i in range(6):
             start = (z * 6 + i) * 24
             du_ref[z, i] = flat[start : start + 24]
     finish_c(0)
-    for flight in flights_b[2]:
-        flight.wait()
-    total = gain_b[0]
-    for o in range(1, y_count):
-        total = total + gain_b[o]
-    gain_s[2] = total
-    flights_c[2] = send(gain_s.at[2], gain_c, (send_c, recv_c), 2, side_peer)
-    start_c(1)
-    flights_c[2].wait()
-    gain_s[3] = gain_s[2] + gain_c[...]
-    flights_d = [
-        send(gain_s.at[3], gain_d.at[lat_me], (send_d, recv_d), o - 1, lat_at(lat_peer(o)))
-        for o in range(1, lat_count)
-    ]
+    start_c(2)
     finish_c(1)
-    across = jnp.concatenate([jnp.transpose(rows[:96]) for rows in rows_of], axis=1)
+    finish_c(2)
+    start_c(3)
+    finish_c(3)
+    across = jnp.concatenate([done[i][0] for i in (3, 1, 2, 0)], axis=1)
+    gain = jnp.concatenate((done[3][1], done[1][1]), axis=0)
+    gain = jnp.concatenate((gain, jnp.zeros((4, DIM), F32)), axis=1)
     for a in range(16):
-        down, right = 96 + 12 * (a // 4), 48 * (a % 4)
+        down, right = 12 * (a // 4), 48 * (a % 4)
         piece = jnp.concatenate(
             [across[12 * a : 12 * a + 12]]
-            + [rows[down : down + 12, right : right + 48] for rows in rows_of]
+            + [done[i][1][down : down + 12, right : right + 48] for i in (2, 0)]
             + [jnp.zeros((12, 96), F32)],
             axis=1,
         )
-        sent_d[a] = jnp.concatenate((piece, jnp.zeros((4, 384), F32)), axis=0).astype(BF)
-    flights_d += [
-        send(sent_d.at[lat_peer(o)], got_d.at[lat_me], (send_d, recv_d), lat_count - 2 + o, lat_at(lat_peer(o)))
+        sent_d[a] = jnp.concatenate((piece, gain), axis=0).astype(BF)
+    flights_d = [
+        send(sent_d.at[lat_peer(o)], got_d.at[lat_me], (send_d, recv_d), o - 1, lat_at(lat_peer(o)))
         for o in range(1, lat_count)
     ]
     got_d[pl.ds(lat_me, 1)] = sent_d[pl.ds(lat_me, 1)]
-    gain_d[pl.ds(lat_me, 1)] = gain_s[pl.ds(3, 1)]
     for flight in flights_d:
         flight.wait()
-    total = jnp.sum(got_d[...].astype(F32), axis=0)
+    total = got_d[0].astype(F32)
+    for o in range(1, lat_count):
+        total = total + got_d[o].astype(F32)
     for i in range(2):
-        qkv_ref[:, i, :] = total[:12, 96 * i : 96 * i + 36]
-        proj_ref[:, i, :] = total[:12, 96 * i + 36 : 96 * i + 48]
-        fc1_ref[:, i, :] = total[:12, 96 * i + 48 : 96 * i + 96]
+        qkv_ref[:, i, :] = total[:12, 48 * i : 48 * i + 36]
+        proj_ref[:, i, :] = total[:12, 48 * i + 36 : 48 * i + 48]
+        fc1_ref[:, i, :] = total[:12, 96 + 48 * i : 144 + 48 * i]
         fc2_ref[:, i, :] = total[:12, 192 + 48 * i : 240 + 48 * i]
-    sums = gain_d[0]
-    for o in range(1, lat_count):
-        sums = sums + gain_d[o]
-    for i in range(2):
-        gain_ref[i] = sums[2 * i : 2 * i + 2, :DIM]
+        gain_ref[i] = total[12 + 2 * i : 14 + 2 * i, :DIM]
+
+
+def hand_over(*refs):
+    count = len(refs) // 2
+    sems = refs[-1]
+    copies = [pltpu.make_async_copy(refs[i], refs[count + i], sems.at[i]) for i in range(count)]
+    for copy in copies:
+        copy.start()
+    for copy in copies:
+        copy.wait()
 
 
 def body(state, out_cot, qkv_weight, proj_weight, fc1_weight, fc2_weight, norm_gain, bias_table):
@@ -617,36 +651,13 @@
         ((2, 8 * WIN, 128), F32),
         ((2, 8 * WIN, 128), F32),
         ((112, DIM), F32),
-        ((224, DIM), BF),
-        ((224, DIM), BF),
-        ((80, DIM), BF),
-        ((80, DIM), BF),
-        ((224, DIM), BF),
-        ((80, DIM), BF),
-        ((80, DIM), BF),
-        ((112, DIM), BF),
-        ((48, DIM), BF),
-        ((48, DIM), BF),
-        ((112, DIM), BF),
-        ((48, DIM), BF),
-        ((48, DIM), BF),
-        ((16, 240, 128), BF),
-        ((16, 240, 128), BF),
-        ((2, DIM), F32),
-        ((2, DIM), F32),
-        ((2, 8, 240, 128), BF),
-        ((2, 8, 240, 128), BF),
-        ((2, 4, 2, 240, 128), BF),
-        ((2, 2, 240, 128), BF),
-        ((2, 240, 128), BF),
-        ((16, 16, 384), BF),
-        ((16, 16, 384), BF),
-        ((4, 8, 256), F32),
-        ((8, 256), F32),
-        ((4, 8, 256), F32),
-        ((8, 256), F32),
-        ((16, 8, 256), F32),
+        ((2, 112, DIM), BF),
     ]
+    buffers += [((112, DIM), BF), ((48, DIM), BF), ((48, DIM), BF)] * 6
+    rows = (144, 96, 144, 96)
+    for lead in ((16,), (8,), (8,), (4, 2), (2,), ()):
+        buffers += [(lead + (r, 128), BF) for r in rows]
+    buffers += [((16, 16, 384), BF), ((16, 16, 384), BF)]
     shapes = (
         (2, 6, 24, DIM), (12, 2, 36), (12, 2, 12), (12, 2, 48), (12, 2, 48), (2, 2, DIM), (2, 6, 1, 207)
     )
@@ -656,11 +667,20 @@
         out_specs=[vmem] * 7,
         out_shape=[jax.ShapeDtypeStruct(s, F32) for s in shapes],
         scratch_shapes=[pltpu.VMEM(s, d) for s, d in buffers]
-        + [dma((10,)), dma((6,)), dma((6,)), dma((3,)), dma((3,)), dma((9,)), dma((9,)), dma((3,)), dma((3,)), dma((30,)), dma((30,))],
+        + [dma((n,)) for n in (10, 9, 9, 4, 4, 12, 12, 4, 4, 15, 15)],
         compiler_params=pltpu.CompilerParams(
             collective_id=0, has_side_effects=True, vmem_limit_bytes=60 * 1024 * 1024
         ),
     )(*args)
+    hbm = pl.BlockSpec(memory_space=pltpu.HBM)
+    outs = pl.pallas_call(
+        hand_over,
+        in_specs=[hbm] * 7,
+        out_specs=[hbm] * 7,
+        out_shape=[jax.ShapeDtypeStruct(s, F32) for s in shapes],
+        scratch_shapes=[dma((7,))],
+        compiler_params=pltpu.CompilerParams(vmem_limit_bytes=60 * 1024 * 1024),
+    )(*outs)
     state_grad, qkv, proj, fc1, fc2, gain, table = outs
     return (
         state_grad,

time: 66.2 us -> 66.5 us (level); the launches traced: 65.4 us -> 66.4 us
  Pallas kernels: 59 us -> 65.6 us
  local copies, waits for them, and re-layouts: 5.71 us -> 0 us
    pallas_call x0 -> x1, Pallas kernels: none -> 12.1 us  [body(): pl.pallas_call(hand_over, in_specs=[hbm] * 7, out_specs=[hbm] * 7, out_sh...]
    unnamed x19 -> x0, local copies, waits for them, and re-layouts: 5.71 us -> none
    pallas_call x1, Pallas kernels: 59 us -> 53.5 us  [body(): pl.pallas_call(kernel, in_specs=[pl.BlockSpec(memory_space=pltpu.HBM)] *...]
where the time goes in v4:
time: 66.5 us; the launch traced here: 66.4 us
  Pallas kernels  65.6 us (99%)
  between operations  0.8 us (1%)
    pallas_call x1, Pallas kernels, body(): pl.pallas_call(kernel, in_specs=[pl.BlockSpec(memory_space=pltpu.HBM)] *...  53.5 us
    pallas_call x1, Pallas kernels, body(): pl.pallas_call(hand_over, in_specs=[hbm] * 7, out_specs=[hbm] * 7, out_sh...  12.1 us

profile of v4, /device:TPU:2, one launch (start us, length us, event | category | flops | bytes accessed | tf_op | source)
XLA Modules:
  0.0 66.4 jit_solution(9405862914494099651)
XLA Ops:
  0.6 53.5 %shard_map.153 = (f32[2,6,24,192]{3,2,1,0:T(8,128)}, f32[12,2,36]{2,1,0:T(2,128)}, f32[12,2,12]{2,1,0:T(2,128)}, f32[12,2,48]{2,1,0:T(2,128)}, f32[12,2,48]{2,1,...) custom-call(bf16[2,6,24,192]{3,2,1,0:T(8,128)(2,1)} %state_in.1, bf16[2,6,24,192]{3,2,1,0:T(8,128)(2,1)} %cot_in.1, ...), custom_call_target="tpu_custom_call" | custom-call | tf_op jit(solution)/shard_map/pallas_call | solution.py:664
  54.1 12.1 %shard_map.154 = (f32[2,6,24,192]{3,2,1,0:T(8,128)}, f32[12,2,36]{2,1,0:T(2,128)}, f32[12,2,12]{2,1,0:T(2,128)}, f32[12,2,48]{2,1,0:T(2,128)}, f32[12,2,48]{2,1,...) custom-call(f32[2,6,24,192]{3,2,1,0:T(8,128)} %get-tuple-element.21.refs_0_, ...), custom_call_target="tpu_custom_call" | custom-call | tf_op jit(solution)/shard_map/pallas_call | solution.py:676

commit v5 on v4

--- a/solution.py
+++ b/solution.py
@@ -158,10 +158,9 @@
         out_ref[place(b)] = folded(jnp.concatenate(rows, axis=0)).astype(BF)
 
 
-def pack_attention(qkv, proj, table, gains, out_ref):
+def pack_attention(qkv, proj, table, out_ref):
     table = jnp.concatenate((table, jnp.zeros((8, 256), F32)), axis=1)
-    ends = jnp.concatenate((gains[0][:, 128:], gains[1][:, 128:]), axis=1)
-    tail = jnp.concatenate((gains[0][:, :128], gains[1][:, :128], ends, jnp.zeros((5, 128), F32)), axis=0)
+    tail = jnp.zeros((8, 128), F32)
     for b in range(16):
         rows = jnp.concatenate((qkv[36 * b : 36 * b + 36], proj[12 * b : 12 * b + 12]), axis=0)
         own = table[:, 207 * b : 207 * b + 207]
@@ -374,8 +373,10 @@
            q_ref, k_ref, v_ref, o_ref, m_ref, g_ref, slope_ref, prob_first, prob_second, bias_ref, grad_ref,
            mine_ref, own_ref, *rest):
     halos, rest = rest[:18], rest[18:]
-    parts, got_a, sum_a, got_b, sum_b, got_c = (rest[4 * i : 4 * i + 4] for i in range(6))
-    sent_d, got_d, load, send_h, recv_h, send_a, recv_a, send_b, recv_b, send_c, recv_c, send_d, recv_d = rest[24:]
+    parts, got_a, sum_a, relay, passed, got_b, sum_b, got_c = (rest[4 * i : 4 * i + 4] for i in range(8))
+    rest = rest[32:]
+    sent_d, got_d, sent_e, got_e, gain_s, gain_a, gain_b, gain_c = rest[:8]
+    load, send_h, recv_h, send_a, recv_a, send_b, recv_b, send_c, recv_c, send_d, recv_d = rest[8:]
     loads = [
         pltpu.make_async_copy(source, target, load.at[i])
         for i, (source, target) in enumerate(
@@ -508,27 +509,41 @@
     flights = exchange(2, upper)
     mine_ref[...] = jnp.concatenate([have[key] for key in OWN] + [jnp.zeros((4, DIM), F32)], axis=0)
 
-    flights_a, flights_b, flights_c, done = [None] * 4, [None] * 4, [None] * 4, [None] * 4
+    flights_a, flights_r, flights_b, flights_c, done = ([None] * 4 for _ in range(5))
+    up, down, far = y_peer(1), y_peer(y_count - 1), y_peer(2)
 
     def start_a(i):
         flights_a[i] = send(parts[i].at[pl.ds((1 - core) * 8, 8)], got_a[i], (send_a, recv_a), i, core_peer)
+
+    def send_y(i, j, source, target, peer):
+        return send(source, target, (send_b, recv_b), 6 * i + j, {"lon_0": peer})
 
     def start_b(i):
         flights_a[i].wait()
         sum_a[i][...] = (parts[i][pl.ds(core * 8, 8)].astype(F32) + got_a[i][...].astype(F32)).astype(BF)
+        flights_r[i] = [
+            send_y(i, 0, sum_a[i].at[far * 2], relay[i].at[0], up),
+            send_y(i, 1, sum_a[i].at[far * 2 + 1], relay[i].at[1], down),
+        ]
         flights_b[i] = [
-            send(sum_a[i].at[pl.ds(y_peer(o) * 2, 2)], got_b[i].at[y], (send_b, recv_b),
-                 i * (y_count - 1) + o - 1, {"lon_0": y_peer(o)})
-            for o in range(1, y_count)
+            send_y(i, 2, sum_a[i].at[up * 2 + 1], got_b[i].at[0, 1], up),
+            send_y(i, 3, sum_a[i].at[down * 2], got_b[i].at[1, 0], down),
         ]
-        got_b[i][pl.ds(y, 1)] = sum_a[i][pl.ds(y * 2, 2)][None]
+
+    def pass_b(i):
+        for flight in flights_r[i]:
+            flight.wait()
+        passed[i][0] = (sum_a[i][pl.ds(up * 2, 1)][0].astype(F32) + relay[i][0].astype(F32)).astype(BF)
+        passed[i][1] = (sum_a[i][pl.ds(down * 2 + 1, 1)][0].astype(F32) + relay[i][1].astype(F32)).astype(BF)
+        flights_b[i] += [
+            send_y(i, 4, passed[i].at[0], got_b[i].at[0, 0], up),
+            send_y(i, 5, passed[i].at[1], got_b[i].at[1, 1], down),
+        ]
 
     def start_c(i):
         for flight in flights_b[i]:
             flight.wait()
-        total = got_b[i][0].astype(F32)
-        for o in range(1, y_count):
-            total = total + got_b[i][o].astype(F32)
+        total = sum_a[i][pl.ds(y * 2, 2)].astype(F32) + got_b[i][0].astype(F32) + got_b[i][1].astype(F32)
         sum_b[i][...] = total.astype(BF)
         flights_c[i] = send(sum_b[i].at[1 - side], got_c[i], (send_c, recv_c), i, side_peer)
 
@@ -542,20 +557,13 @@
             sums = jnp.concatenate((chunk[72:80], chunk[80:88]), axis=1)
             for h in range(HEADS):
                 table_ref[1 - i // 2, h] = sums[h : h + 1, :207]
-            gain = jnp.concatenate(
-                (
-                    jnp.concatenate((chunk[88:89], chunk[90:91, :64]), axis=1),
-                    jnp.concatenate((chunk[89:90], chunk[90:91, 64:]), axis=1),
-                ),
-                axis=0,
-            )
-            done[i] = (jnp.transpose(unfolded(chunk[:72])), gain)
-
+            done[i] = jnp.transpose(unfolded(chunk[:72]))
+
+    first_of_gains = (gain1, gain2)
     pack_mlp(*mlp_grads(y2, y1, g, unit2, second_gains[1:2]), parts[0])
     start_a(0)
     pack_attention(
-        qkv_grads(d_qkv, unit1, second_gains[0:1]), tn(yp, o), reduce_bias(grad_ref, lanes[...], True),
-        (gain1, gain2), parts[1],
+        qkv_grads(d_qkv, unit1, second_gains[0:1]), tn(yp, o), reduce_bias(grad_ref, lanes[...], True), parts[1]
     )
     start_a(1)
 
@@ -570,69 +578,113 @@
     dm, gain2 = back_middle(cot_x, y1, unit2, scale2, first_gains[1:2], w_fc1[0])
     yp = dm.astype(BF)
     do = nt(yp, w_proj[0]).astype(BF)
-    d_qkv = back_attention(
-        do, q_ref[...], k_ref[...], v_ref[...], prob_first, grad_ref, lambda: start_b(2)
-    )
+    pass_b(0)
+
+    def halfway():
+        start_b(2)
+        pass_b(1)
+
+    d_qkv = back_attention(do, q_ref[...], k_ref[...], v_ref[...], prob_first, grad_ref, halfway)
     start_c(0)
+    pass_b(2)
     unit1, scale1 = normed(nn(order[...], flat_rows(state).astype(BF)))
-    du, gain1 = back_input(dm, d_qkv, unit1, scale1, first_gains[0:1], w_qkv[0])
     pack_attention(
         qkv_grads(d_qkv, unit1, first_gains[0:1]), tn(yp, o_ref[...]), reduce_bias(grad_ref, lanes[...], False),
-        (gain1, gain2), parts[3],
+        parts[3],
     )
     start_a(3)
+    du, gain1 = back_input(dm, d_qkv, unit1, scale1, first_gains[0:1], w_qkv[0])
+    gain_s[0] = jnp.concatenate(
+        [jnp.concatenate((row, jnp.zeros((1, 64), F32)), axis=1) for row in (gain1, gain2, *first_of_gains)]
+        + [jnp.zeros((4, 256), F32)],
+        axis=0,
+    )
+    gain_flight = send(gain_s.at[0], gain_a, (send_a, recv_a), 4, core_peer)
     start_c(1)
+    start_b(3)
+    gain_flight.wait()
+    gain_s[1] = gain_s[0] + gain_a[...]
+    gain_flights = [
+        send(gain_s.at[1], gain_b.at[y], (send_b, recv_b), 23 + o, {"lon_0": y_peer(o)})
+        for o in range(1, y_count)
+    ]
+    gain_b[pl.ds(y, 1)] = gain_s[pl.ds(1, 1)]
+    start_c(2)
+    finish_c(0)
+    finish_c(1)
+    pass_b(3)
     high, low = two_pieces(du)
     flat = tn(order[...], high) + tn(order[...], low)
-    start_b(3)
     for z in range(2):
         for i in range(6):
             start = (z * 6 + i) * 24
             du_ref[z, i] = flat[start : start + 24]
-    finish_c(0)
-    start_c(2)
-    finish_c(1)
     finish_c(2)
-    start_c(3)
-    finish_c(3)
-    across = jnp.concatenate([done[i][0] for i in (3, 1, 2, 0)], axis=1)
-    gain = jnp.concatenate((done[3][1], done[1][1]), axis=0)
-    gain = jnp.concatenate((gain, jnp.zeros((4, DIM), F32)), axis=1)
+    across = jnp.concatenate([done[1], done[2][0], done[0][0]], axis=1)
     for a in range(16):
-        down, right = 12 * (a // 4), 48 * (a % 4)
+        low_row, right = 12 * (a // 4), 48 * (a % 4)
         piece = jnp.concatenate(
             [across[12 * a : 12 * a + 12]]
-            + [done[i][1][down : down + 12, right : right + 48] for i in (2, 0)]
-            + [jnp.zeros((12, 96), F32)],
+            + [done[i][1][low_row : low_row + 12, right : right + 48] for i in (2, 0)]
+            + [jnp.zeros((12, 16), F32)],
             axis=1,
         )
-        sent_d[a] = jnp.concatenate((piece, gain), axis=0).astype(BF)
-    flights_d = [
-        send(sent_d.at[lat_peer(o)], got_d.at[lat_me], (send_d, recv_d), o - 1, lat_at(lat_peer(o)))
-        for o in range(1, lat_count)
-    ]
+        sent_d[a] = jnp.concatenate((piece, jnp.zeros((4, 256), F32)), axis=0).astype(BF)
+
+    def to_latitudes(source, target, first_sem):
+        return [
+            send(source.at[lat_peer(o)], target.at[lat_me], (send_d, recv_d), first_sem + o - 1, lat_at(lat_peer(o)))
+            for o in range(1, lat_count)
+        ]
+
+    start_c(3)
+    flights_d = to_latitudes(sent_d, got_d, 0)
     got_d[pl.ds(lat_me, 1)] = sent_d[pl.ds(lat_me, 1)]
+    for flight in gain_flights:
+        flight.wait()
+    total = gain_b[0]
+    for o in range(1, y_count):
+        total = total + gain_b[o]
+    gain_s[2] = total
+    gain_flight = send(gain_s.at[2], gain_c, (send_c, recv_c), 4, side_peer)
+    finish_c(3)
+    gain_flight.wait()
+    total = gain_s[2] + gain_c[...]
+    gain = jnp.concatenate([total[r : r + 1, 64 * c : 64 * c + 64] for r in range(4) for c in range(3)], axis=0)
+    for a in range(16):
+        piece = jnp.concatenate((done[3][12 * a : 12 * a + 12], gain, jnp.zeros((12, 16), F32)), axis=1)
+        sent_e[a] = jnp.concatenate((piece, jnp.zeros((4, 128), F32)), axis=0).astype(BF)
+    flights_e = to_latitudes(sent_e, got_e, lat_count - 1)
+    got_e[pl.ds(lat_me, 1)] = sent_e[pl.ds(lat_me, 1)]
     for flight in flights_d:
         flight.wait()
-    total = got_d[0].astype(F32)
-    for o in range(1, lat_count):
-        total = total + got_d[o].astype(F32)
+
+    def summed(ref):
+        total = ref[0].astype(F32)
+        for o in range(1, lat_count):
+            total = total + ref[o].astype(F32)
+        return total
+
+    total = summed(got_d)
+    qkv_ref[:, 1, :] = total[:12, :36]
+    proj_ref[:, 1, :] = total[:12, 36:48]
     for i in range(2):
-        qkv_ref[:, i, :] = total[:12, 48 * i : 48 * i + 36]
-        proj_ref[:, i, :] = total[:12, 48 * i + 36 : 48 * i + 48]
-        fc1_ref[:, i, :] = total[:12, 96 + 48 * i : 144 + 48 * i]
-        fc2_ref[:, i, :] = total[:12, 192 + 48 * i : 240 + 48 * i]
-        gain_ref[i] = total[12 + 2 * i : 14 + 2 * i, :DIM]
+        fc1_ref[:, i, :] = total[:12, 48 + 48 * i : 96 + 48 * i]
+        fc2_ref[:, i, :] = total[:12, 144 + 48 * i : 192 + 48 * i]
+    for flight in flights_e:
+        flight.wait()
+    total = summed(got_e)
+    qkv_ref[:, 0, :] = total[:12, :36]
+    proj_ref[:, 0, :] = total[:12, 36:48]
+    for r in range(4):
+        gain_ref[r // 2, r % 2 : r % 2 + 1] = jnp.concatenate(
+            [total[3 * r + c : 3 * r + c + 1, 48:112] for c in range(3)], axis=1
+        )
 
 
 def hand_over(*refs):
-    count = len(refs) // 2
-    sems = refs[-1]
-    copies = [pltpu.make_async_copy(refs[i], refs[count + i], sems.at[i]) for i in range(count)]
-    for copy in copies:
-        copy.start()
-    for copy in copies:
-        copy.wait()
+    for source, target in zip(refs[:7], refs[7:]):
+        target[...] = source[...]
 
 
 def body(state, out_cot, qkv_weight, proj_weight, fc1_weight, fc2_weight, norm_gain, bias_table):
@@ -655,9 +707,10 @@
     ]
     buffers += [((112, DIM), BF), ((48, DIM), BF), ((48, DIM), BF)] * 6
     rows = (144, 96, 144, 96)
-    for lead in ((16,), (8,), (8,), (4, 2), (2,), ()):
+    for lead in ((16,), (8,), (8,), (2,), (2,), (2, 2), (2,), ()):
         buffers += [(lead + (r, 128), BF) for r in rows]
-    buffers += [((16, 16, 384), BF), ((16, 16, 384), BF)]
+    buffers += [((16, 16, 256), BF), ((16, 16, 256), BF), ((16, 16, 128), BF), ((16, 16, 128), BF)]
+    buffers += [((3, 8, 256), F32), ((8, 256), F32), ((4, 8, 256), F32), ((8, 256), F32)]
     shapes = (
         (2, 6, 24, DIM), (12, 2, 36), (12, 2, 12), (12, 2, 48), (12, 2, 48), (2, 2, DIM), (2, 6, 1, 207)
     )
@@ -667,18 +720,16 @@
         out_specs=[vmem] * 7,
         out_shape=[jax.ShapeDtypeStruct(s, F32) for s in shapes],
         scratch_shapes=[pltpu.VMEM(s, d) for s, d in buffers]
-        + [dma((n,)) for n in (10, 9, 9, 4, 4, 12, 12, 4, 4, 15, 15)],
+        + [dma((n,)) for n in (10, 9, 9, 5, 5, 27, 27, 5, 5, 30, 30)],
         compiler_params=pltpu.CompilerParams(
             collective_id=0, has_side_effects=True, vmem_limit_bytes=60 * 1024 * 1024
         ),
     )(*args)
-    hbm = pl.BlockSpec(memory_space=pltpu.HBM)
     outs = pl.pallas_call(
         hand_over,
-        in_specs=[hbm] * 7,
-        out_specs=[hbm] * 7,
+        in_specs=[vmem] * 7,
+        out_specs=[vmem] * 7,
         out_shape=[jax.ShapeDtypeStruct(s, F32) for s in shapes],
-        scratch_shapes=[dma((7,))],
         compiler_params=pltpu.CompilerParams(vmem_limit_bytes=60 * 1024 * 1024),
     )(*outs)
     state_grad, qkv, proj, fc1, fc2, gain, table = outs

time: 66.5 us -> 59.8 us (0.90)
  Pallas kernels: 65.6 us -> 59 us
    pallas_call x1, Pallas kernels: 12.1 us -> 1.77 us  [body(): pl.pallas_call(hand_over, in_specs=[vmem] * 7, out_specs=[vmem] * 7, out_...]
    pallas_call x1, Pallas kernels: 53.5 us -> 57.3 us  [body(): pl.pallas_call(kernel, in_specs=[pl.BlockSpec(memory_space=pltpu.HBM)] *...]
where the time goes in v5:
time: 59.8 us; the launch traced here: 59.7 us
  Pallas kernels  59 us (99%)
  between operations  0.64 us (1%)
    pallas_call x1, Pallas kernels, body(): pl.pallas_call(kernel, in_specs=[pl.BlockSpec(memory_space=pltpu.HBM)] *...  57.3 us
    pallas_call x1, Pallas kernels, body(): pl.pallas_call(hand_over, in_specs=[vmem] * 7, out_specs=[vmem] * 7, out_...  1.77 us

profile of v5, /device:TPU:2, one launch (start us, length us, event | category | flops | bytes accessed | tf_op | source)
XLA Modules:
  0.0 59.7 jit_solution(644104950770295682)
XLA Ops:
  0.6 57.3 %shard_map.153 = (f32[2,6,24,192]{3,2,1,0:T(8,128)}, f32[12,2,36]{2,1,0:T(2,128)}, f32[12,2,12]{2,1,0:T(2,128)}, f32[12,2,48]{2,1,0:T(2,128)}, f32[12,2,48]{2,1,...) custom-call(bf16[2,6,24,192]{3,2,1,0:T(8,128)(2,1)} %state_in.1, bf16[2,6,24,192]{3,2,1,0:T(8,128)(2,1)} %cot_in.1, ...), custom_call_target="tpu_custom_call" | custom-call | tf_op jit(solution)/shard_map/pallas_call | solution.py:717
  57.9 1.8 %shard_map.154 = (f32[2,6,24,192]{3,2,1,0:T(8,128)}, f32[12,2,36]{2,1,0:T(2,128)}, f32[12,2,12]{2,1,0:T(2,128)}, f32[12,2,48]{2,1,0:T(2,128)}, f32[12,2,48]{2,1,...) custom-call(f32[2,6,24,192]{3,2,1,0:T(8,128)} %get-tuple-element.21.refs_0_, ...), custom_call_target="tpu_custom_call" | custom-call | tf_op jit(solution)/shard_map/pallas_call | solution.py:728

commit v6 on v5

--- a/solution.py
+++ b/solution.py
@@ -158,9 +158,10 @@
         out_ref[place(b)] = folded(jnp.concatenate(rows, axis=0)).astype(BF)
 
 
-def pack_attention(qkv, proj, table, out_ref):
+def pack_attention(qkv, proj, table, gains, out_ref):
     table = jnp.concatenate((table, jnp.zeros((8, 256), F32)), axis=1)
-    tail = jnp.zeros((8, 128), F32)
+    ends = jnp.concatenate((gains[0][:, 128:], gains[1][:, 128:]), axis=1)
+    tail = jnp.concatenate((gains[0][:, :128], gains[1][:, :128], ends, jnp.zeros((5, 128), F32)), axis=0)
     for b in range(16):
         rows = jnp.concatenate((qkv[36 * b : 36 * b + 36], proj[12 * b : 12 * b + 12]), axis=0)
         own = table[:, 207 * b : 207 * b + 207]
@@ -373,10 +374,9 @@
            q_ref, k_ref, v_ref, o_ref, m_ref, g_ref, slope_ref, prob_first, prob_second, bias_ref, grad_ref,
            mine_ref, own_ref, *rest):
     halos, rest = rest[:18], rest[18:]
-    parts, got_a, sum_a, relay, passed, got_b, sum_b, got_c = (rest[4 * i : 4 * i + 4] for i in range(8))
-    rest = rest[32:]
-    sent_d, got_d, sent_e, got_e, gain_s, gain_a, gain_b, gain_c = rest[:8]
-    load, send_h, recv_h, send_a, recv_a, send_b, recv_b, send_c, recv_c, send_d, recv_d = rest[8:]
+    parts, got_a, sum_a, got_b = (rest[4 * i : 4 * i + 4] for i in range(4))
+    rest = rest[16:]
+    sent_d, got_d, sent_e, got_e, load, send_h, recv_h, send_a, recv_a, send_b, recv_b, send_d, recv_d = rest
     loads = [
         pltpu.make_async_copy(source, target, load.at[i])
         for i, (source, target) in enumerate(
@@ -397,15 +397,13 @@
     for copy in loads:
         copy.start()
     core = lax.axis_index("lon_2")
-    side = lax.axis_index("lon_1")
-    y, y_count = lax.axis_index("lon_0"), lax.axis_size("lon_0")
+    chip, chip_count, chip_at = ring(LON[:2])
     lat_me, lat_count, lat_at = ring(LAT)
     lon_me, lon_count, lon_at = ring(LON)
     core_peer = {"lon_2": 1 - core}
-    side_peer = {"lon_1": 1 - side}
-
-    def y_peer(o):
-        return lax.rem(y + o, y_count)
+
+    def chip_peer(o):
+        return lax.rem(chip + o, chip_count)
 
     def lat_peer(o):
         return lax.rem(lat_me + o, lat_count)
@@ -417,8 +415,8 @@
 
     lower, upper = neighbours(-1), neighbours(1)
     peers = (
-        [*lower, *upper, core_peer, side_peer]
-        + [{"lon_0": y_peer(o)} for o in range(1, y_count)]
+        [*lower, *upper, core_peer]
+        + [chip_at(chip_peer(o)) for o in range(1, chip_count)]
         + [lat_at(lat_peer(o)) for o in range(1, lat_count)]
     )
     barrier = pltpu.get_barrier_semaphore()
@@ -509,47 +507,27 @@
     flights = exchange(2, upper)
     mine_ref[...] = jnp.concatenate([have[key] for key in OWN] + [jnp.zeros((4, DIM), F32)], axis=0)
 
-    flights_a, flights_r, flights_b, flights_c, done = ([None] * 4 for _ in range(5))
-    up, down, far = y_peer(1), y_peer(y_count - 1), y_peer(2)
+    flights_a, flights_b, done = [None] * 4, [None] * 4, [None] * 4
 
     def start_a(i):
         flights_a[i] = send(parts[i].at[pl.ds((1 - core) * 8, 8)], got_a[i], (send_a, recv_a), i, core_peer)
-
-    def send_y(i, j, source, target, peer):
-        return send(source, target, (send_b, recv_b), 6 * i + j, {"lon_0": peer})
 
     def start_b(i):
         flights_a[i].wait()
         sum_a[i][...] = (parts[i][pl.ds(core * 8, 8)].astype(F32) + got_a[i][...].astype(F32)).astype(BF)
-        flights_r[i] = [
-            send_y(i, 0, sum_a[i].at[far * 2], relay[i].at[0], up),
-            send_y(i, 1, sum_a[i].at[far * 2 + 1], relay[i].at[1], down),
+        flights_b[i] = [
+            send(sum_a[i].at[chip_peer(o)], got_b[i].at[chip], (send_b, recv_b),
+                 i * (chip_count - 1) + o - 1, chip_at(chip_peer(o)))
+            for o in range(1, chip_count)
         ]
-        flights_b[i] = [
-            send_y(i, 2, sum_a[i].at[up * 2 + 1], got_b[i].at[0, 1], up),
-            send_y(i, 3, sum_a[i].at[down * 2], got_b[i].at[1, 0], down),
-        ]
-
-    def pass_b(i):
-        for flight in flights_r[i]:
-            flight.wait()
-        passed[i][0] = (sum_a[i][pl.ds(up * 2, 1)][0].astype(F32) + relay[i][0].astype(F32)).astype(BF)
-        passed[i][1] = (sum_a[i][pl.ds(down * 2 + 1, 1)][0].astype(F32) + relay[i][1].astype(F32)).astype(BF)
-        flights_b[i] += [
-            send_y(i, 4, passed[i].at[0], got_b[i].at[0, 0], up),
-            send_y(i, 5, passed[i].at[1], got_b[i].at[1, 1], down),
-        ]
-
-    def start_c(i):
+        got_b[i][pl.ds(chip, 1)] = sum_a[i][pl.ds(chip, 1)]
+
+    def finish_b(i):
         for flight in flights_b[i]:
             flight.wait()
-        total = sum_a[i][pl.ds(y * 2, 2)].astype(F32) + got_b[i][0].astype(F32) + got_b[i][1].astype(F32)
-        sum_b[i][...] = total.astype(BF)
-        flights_c[i] = send(sum_b[i].at[1 - side], got_c[i], (send_c, recv_c), i, side_peer)
-
-    def finish_c(i):
-        flights_c[i].wait()
-        chunk = sum_b[i][pl.ds(side, 1)][0].astype(F32) + got_c[i][...].astype(F32)
+        chunk = got_b[i][0].astype(F32)
+        for o in range(1, chip_count):
+            chunk = chunk + got_b[i][o].astype(F32)
         if i % 2 == 0:
             rows = unfolded(chunk)
             done[i] = (jnp.transpose(rows[:48]), rows[48:])
@@ -557,13 +535,16 @@
             sums = jnp.concatenate((chunk[72:80], chunk[80:88]), axis=1)
             for h in range(HEADS):
                 table_ref[1 - i // 2, h] = sums[h : h + 1, :207]
-            done[i] = jnp.transpose(unfolded(chunk[:72]))
-
-    first_of_gains = (gain1, gain2)
+            pieces = [chunk[88 + r : 89 + r, 64 * c : 64 * c + 64] for r in range(2) for c in range(2)]
+            ends = [chunk[90:91, :64], chunk[90:91, 64:]]
+            gain = jnp.concatenate(pieces[:2] + ends[:1] + pieces[2:] + ends[1:], axis=0)
+            done[i] = (jnp.transpose(unfolded(chunk[:72])), gain)
+
     pack_mlp(*mlp_grads(y2, y1, g, unit2, second_gains[1:2]), parts[0])
     start_a(0)
     pack_attention(
-        qkv_grads(d_qkv, unit1, second_gains[0:1]), tn(yp, o), reduce_bias(grad_ref, lanes[...], True), parts[1]
+        qkv_grads(d_qkv, unit1, second_gains[0:1]), tn(yp, o), reduce_bias(grad_ref, lanes[...], True),
+        (gain1, gain2), parts[1],
     )
     start_a(1)
 
@@ -578,49 +559,19 @@
     dm, gain2 = back_middle(cot_x, y1, unit2, scale2, first_gains[1:2], w_fc1[0])
     yp = dm.astype(BF)
     do = nt(yp, w_proj[0]).astype(BF)
-    pass_b(0)
-
-    def halfway():
-        start_b(2)
-        pass_b(1)
-
-    d_qkv = back_attention(do, q_ref[...], k_ref[...], v_ref[...], prob_first, grad_ref, halfway)
-    start_c(0)
-    pass_b(2)
+    d_qkv = back_attention(do, q_ref[...], k_ref[...], v_ref[...], prob_first, grad_ref, lambda: start_b(2))
     unit1, scale1 = normed(nn(order[...], flat_rows(state).astype(BF)))
+    du, gain1 = back_input(dm, d_qkv, unit1, scale1, first_gains[0:1], w_qkv[0])
     pack_attention(
         qkv_grads(d_qkv, unit1, first_gains[0:1]), tn(yp, o_ref[...]), reduce_bias(grad_ref, lanes[...], False),
-        parts[3],
+        (gain1, gain2), parts[3],
     )
     start_a(3)
-    du, gain1 = back_input(dm, d_qkv, unit1, scale1, first_gains[0:1], w_qkv[0])
-    gain_s[0] = jnp.concatenate(
-        [jnp.concatenate((row, jnp.zeros((1, 64), F32)), axis=1) for row in (gain1, gain2, *first_of_gains)]
-        + [jnp.zeros((4, 256), F32)],
-        axis=0,
-    )
-    gain_flight = send(gain_s.at[0], gain_a, (send_a, recv_a), 4, core_peer)
-    start_c(1)
+    finish_b(0)
+    finish_b(1)
     start_b(3)
-    gain_flight.wait()
-    gain_s[1] = gain_s[0] + gain_a[...]
-    gain_flights = [
-        send(gain_s.at[1], gain_b.at[y], (send_b, recv_b), 23 + o, {"lon_0": y_peer(o)})
-        for o in range(1, y_count)
-    ]
-    gain_b[pl.ds(y, 1)] = gain_s[pl.ds(1, 1)]
-    start_c(2)
-    finish_c(0)
-    finish_c(1)
-    pass_b(3)
-    high, low = two_pieces(du)
-    flat = tn(order[...], high) + tn(order[...], low)
-    for z in range(2):
-        for i in range(6):
-            start = (z * 6 + i) * 24
-            du_ref[z, i] = flat[start : start + 24]
-    finish_c(2)
-    across = jnp.concatenate([done[1], done[2][0], done[0][0]], axis=1)
+    finish_b(2)
+    across = jnp.concatenate([done[1][0], done[2][0], done[0][0]], axis=1)
     for a in range(16):
         low_row, right = 12 * (a // 4), 48 * (a % 4)
         piece = jnp.concatenate(
@@ -637,22 +588,18 @@
             for o in range(1, lat_count)
         ]
 
-    start_c(3)
     flights_d = to_latitudes(sent_d, got_d, 0)
     got_d[pl.ds(lat_me, 1)] = sent_d[pl.ds(lat_me, 1)]
-    for flight in gain_flights:
-        flight.wait()
-    total = gain_b[0]
-    for o in range(1, y_count):
-        total = total + gain_b[o]
-    gain_s[2] = total
-    gain_flight = send(gain_s.at[2], gain_c, (send_c, recv_c), 4, side_peer)
-    finish_c(3)
-    gain_flight.wait()
-    total = gain_s[2] + gain_c[...]
-    gain = jnp.concatenate([total[r : r + 1, 64 * c : 64 * c + 64] for r in range(4) for c in range(3)], axis=0)
+    high, low = two_pieces(du)
+    flat = tn(order[...], high) + tn(order[...], low)
+    for z in range(2):
+        for i in range(6):
+            start = (z * 6 + i) * 24
+            du_ref[z, i] = flat[start : start + 24]
+    finish_b(3)
+    gain = jnp.concatenate((done[3][1], done[1][1]), axis=0)
     for a in range(16):
-        piece = jnp.concatenate((done[3][12 * a : 12 * a + 12], gain, jnp.zeros((12, 16), F32)), axis=1)
+        piece = jnp.concatenate((done[3][0][12 * a : 12 * a + 12], gain, jnp.zeros((12, 16), F32)), axis=1)
         sent_e[a] = jnp.concatenate((piece, jnp.zeros((4, 128), F32)), axis=0).astype(BF)
     flights_e = to_latitudes(sent_e, got_e, lat_count - 1)
     got_e[pl.ds(lat_me, 1)] = sent_e[pl.ds(lat_me, 1)]
@@ -707,10 +654,9 @@
     ]
     buffers += [((112, DIM), BF), ((48, DIM), BF), ((48, DIM), BF)] * 6
     rows = (144, 96, 144, 96)
-    for lead in ((16,), (8,), (8,), (2,), (2,), (2, 2), (2,), ()):
-        buffers += [(lead + (r, 128), BF) for r in rows]
+    for lead in (16, 8, 8, 8):
+        buffers += [((lead, r, 128), BF) for r in rows]
     buffers += [((16, 16, 256), BF), ((16, 16, 256), BF), ((16, 16, 128), BF), ((16, 16, 128), BF)]
-    buffers += [((3, 8, 256), F32), ((8, 256), F32), ((4, 8, 256), F32), ((8, 256), F32)]
     shapes = (
         (2, 6, 24, DIM), (12, 2, 36), (12, 2, 12), (12, 2, 48), (12, 2, 48), (2, 2, DIM), (2, 6, 1, 207)
     )
@@ -720,7 +666,7 @@
         out_specs=[vmem] * 7,
         out_shape=[jax.ShapeDtypeStruct(s, F32) for s in shapes],
         scratch_shapes=[pltpu.VMEM(s, d) for s, d in buffers]
-        + [dma((n,)) for n in (10, 9, 9, 5, 5, 27, 27, 5, 5, 30, 30)],
+        + [dma((n,)) for n in (10, 9, 9, 4, 4, 28, 28, 30, 30)],
         compiler_params=pltpu.CompilerParams(
             collective_id=0, has_side_effects=True, vmem_limit_bytes=60 * 1024 * 1024
         ),

time: 59.8 us -> 52.4 us (0.88)
  Pallas kernels: 59 us -> 51.7 us
    pallas_call x1, Pallas kernels: 57.3 us -> 49.9 us  [body(): pl.pallas_call(kernel, in_specs=[pl.BlockSpec(memory_space=pltpu.HBM)] *...]
where the time goes in v6:
time: 52.4 us; the launch traced here: 52.3 us
  Pallas kernels  51.7 us (99%)
  between operations  0.64 us (1%)
    pallas_call x1, Pallas kernels, body(): pl.pallas_call(kernel, in_specs=[pl.BlockSpec(memory_space=pltpu.HBM)] *...  49.9 us
    pallas_call x1, Pallas kernels, body(): pl.pallas_call(hand_over, in_specs=[vmem] * 7, out_specs=[vmem] * 7, out_...  1.77 us

profile of v6, /device:TPU:2, one launch (start us, length us, event | category | flops | bytes accessed | tf_op | source)
XLA Modules:
  0.0 52.3 jit_solution(16619930102728017990)
XLA Ops:
  0.6 49.9 %shard_map.153 = (f32[2,6,24,192]{3,2,1,0:T(8,128)}, f32[12,2,36]{2,1,0:T(2,128)}, f32[12,2,12]{2,1,0:T(2,128)}, f32[12,2,48]{2,1,0:T(2,128)}, f32[12,2,48]{2,1,...) custom-call(bf16[2,6,24,192]{3,2,1,0:T(8,128)(2,1)} %state_in.1, bf16[2,6,24,192]{3,2,1,0:T(8,128)(2,1)} %cot_in.1, ...), custom_call_target="tpu_custom_call" | custom-call | tf_op jit(solution)/shard_map/pallas_call | solution.py:663
  50.5 1.8 %shard_map.154 = (f32[2,6,24,192]{3,2,1,0:T(8,128)}, f32[12,2,36]{2,1,0:T(2,128)}, f32[12,2,12]{2,1,0:T(2,128)}, f32[12,2,48]{2,1,0:T(2,128)}, f32[12,2,48]{2,1,...) custom-call(f32[2,6,24,192]{3,2,1,0:T(8,128)} %get-tuple-element.21.refs_0_, ...), custom_call_target="tpu_custom_call" | custom-call | tf_op jit(solution)/shard_map/pallas_call | solution.py:674

commit v7 on v6

--- a/solution.py
+++ b/solution.py
@@ -232,8 +232,11 @@
     e = nn(n2, w_fc1[...])
     cdf = 0.5 * (1.0 + lax.erf(e * (0.5**0.5)))
     g = (e * cdf).astype(BF)
-    slope = cdf + e * jnp.exp(e * e * -0.5) * 0.3989422804014327
-    return q.astype(BF), k.astype(BF), v.astype(BF), o, m, g, slope.astype(BF)
+
+    def slope():
+        return (cdf + e * jnp.exp(e * e * -0.5) * 0.3989422804014327).astype(BF)
+
+    return q.astype(BF), k.astype(BF), v.astype(BF), o, m, g, slope
 
 
 def back_mlp(cot, m, slope, w_fc2):
@@ -277,10 +280,10 @@
             ds = (ds * SCALE).astype(BF)
             ds_all.append(ds)
             dq_t.append(nn(k_t[h * HEAD : h * HEAD + HEAD], ds))
+            if n == 0 and h == 2 and meanwhile is not None:
+                meanwhile()
         dqs.append(jnp.transpose(jnp.concatenate(dq_t, axis=0)))
         dks.append(from_heads(nn(jnp.concatenate(ds_all, axis=0), q_n), masks))
-        if n == 0 and meanwhile is not None:
-            meanwhile()
     return [jnp.concatenate(parts, axis=0).astype(BF) for parts in (dqs, dks, dvs)]
 
 
@@ -366,6 +369,10 @@
         return where
 
     return me, total, at
+
+
+def farthest_first(count):
+    return sorted(range(1, count), key=lambda o: -min(o, count - o))
 
 
 def kernel(state_in, cot_in, order_in, lanes_in, table_in, gains_in, w_qkv_in, w_proj_in, w_fc1_in, w_fc2_in,
@@ -437,7 +444,7 @@
     def exchange(step, targets):
         return [
             send(halos[6 * step + i], halos[6 * step + 3 + i], (send_h, recv_h), 3 * step + i, targets[i])
-            for i in range(3)
+            for i in (2, 1, 0)
         ]
 
     def fill(step, have):
@@ -453,12 +460,15 @@
                 have[key] = rows[36 * i : 36 * i + 36]
         return have
 
-    for copy in loads[:5]:
+    for copy in loads[:2]:
         copy.wait()
     perm = order[...]
     x = nn(perm, flat_rows(state).astype(BF))
+    loads[2].wait()
     given = quarters(nn(perm, flat_rows(cot).astype(BF)))
     fill(0, given)
+    for copy in loads[3:5]:
+        copy.wait()
     expand_bias(table_of(0), lanes[...], False, bias_ref)
     for copy in loads[5:7]:
         copy.wait()
@@ -479,7 +489,7 @@
     flights = early + exchange(1, lower)
     own_ref[0] = padded([out[key] for key in OWN], 112)
     own_ref[1] = padded([given[key] for key in OWN], 112)
-    for ref, value in ((q_ref, q), (k_ref, k), (v_ref, v), (o_ref, o), (m_ref, m), (g_ref, g), (slope_ref, slope)):
+    for ref, value in ((q_ref, q), (k_ref, k), (v_ref, v), (o_ref, o), (m_ref, m), (g_ref, g), (slope_ref, slope())):
         ref[...] = value
 
     expand_bias(table_of(1), lanes[...], True, bias_ref)
@@ -496,7 +506,7 @@
     q, k, v, o, m, g, slope = forward(
         u, second_gains, w_qkv[1], w_proj.at[1], w_fc1.at[1], bias_ref, allowed, prob_second
     )
-    y2, y1, unit2, scale2 = back_mlp(cot_u, m, slope, w_fc2[1])
+    y2, y1, unit2, scale2 = back_mlp(cot_u, m, slope(), w_fc2[1])
     dm, gain2 = back_middle(cot_u, y1, unit2, scale2, second_gains[1:2], w_fc1[1])
     yp = dm.astype(BF)
     d_qkv = back_attention(nt(yp, w_proj[1]).astype(BF), q, k, v, prob_second, grad_ref)
@@ -518,7 +528,7 @@
         flights_b[i] = [
             send(sum_a[i].at[chip_peer(o)], got_b[i].at[chip], (send_b, recv_b),
                  i * (chip_count - 1) + o - 1, chip_at(chip_peer(o)))
-            for o in range(1, chip_count)
+            for o in farthest_first(chip_count)
         ]
         got_b[i][pl.ds(chip, 1)] = sum_a[i][pl.ds(chip, 1)]
 
@@ -548,14 +558,14 @@
     )
     start_a(1)
 
+    start_b(0)
     for flight in flights:
         flight.wait()
+    start_b(1)
     cot_x = whole_block(arrived(2, mine_ref))
     y2, y1, unit2, scale2 = back_mlp(cot_x, m_ref[...], slope_ref[...], w_fc2[0])
-    start_b(0)
     pack_mlp(*mlp_grads(y2, y1, g_ref[...], unit2, first_gains[1:2]), parts[2])
     start_a(2)
-    start_b(1)
     dm, gain2 = back_middle(cot_x, y1, unit2, scale2, first_gains[1:2], w_fc1[0])
     yp = dm.astype(BF)
     do = nt(yp, w_proj[0]).astype(BF)
@@ -585,7 +595,7 @@
     def to_latitudes(source, target, first_sem):
         return [
             send(source.at[lat_peer(o)], target.at[lat_me], (send_d, recv_d), first_sem + o - 1, lat_at(lat_peer(o)))
-            for o in range(1, lat_count)
+            for o in farthest_first(lat_count)
         ]
 
     flights_d = to_latitudes(sent_d, got_d, 0)

time: 52.4 us -> 48.5 us (0.926)
  Pallas kernels: 51.7 us -> 47.8 us
    pallas_call x1, Pallas kernels: 49.9 us -> 46 us  [body(): pl.pallas_call(kernel, in_specs=[pl.BlockSpec(memory_space=pltpu.HBM)] *...]
where the time goes in v7:
time: 48.5 us; the launch traced here: 48.4 us
  Pallas kernels  47.8 us (99%)
  between operations  0.64 us (1%)
    pallas_call x1, Pallas kernels, body(): pl.pallas_call(kernel, in_specs=[pl.BlockSpec(memory_space=pltpu.HBM)] *...  46 us
    pallas_call x1, Pallas kernels, body(): pl.pallas_call(hand_over, in_specs=[vmem] * 7, out_specs=[vmem] * 7, out_...  1.77 us

profile of v7, /device:TPU:2, one launch (start us, length us, event | category | flops | bytes accessed | tf_op | source)
XLA Modules:
  0.0 48.4 jit_solution(16687363991634263184)
XLA Ops:
  0.6 46.0 %shard_map.153 = (f32[2,6,24,192]{3,2,1,0:T(8,128)}, f32[12,2,36]{2,1,0:T(2,128)}, f32[12,2,12]{2,1,0:T(2,128)}, f32[12,2,48]{2,1,0:T(2,128)}, f32[12,2,48]{2,1,...) custom-call(bf16[2,6,24,192]{3,2,1,0:T(8,128)(2,1)} %state_in.1, bf16[2,6,24,192]{3,2,1,0:T(8,128)(2,1)} %cot_in.1, ...), custom_call_target="tpu_custom_call" | custom-call | tf_op jit(solution)/shard_map/pallas_call | solution.py:673
  46.6 1.8 %shard_map.154 = (f32[2,6,24,192]{3,2,1,0:T(8,128)}, f32[12,2,36]{2,1,0:T(2,128)}, f32[12,2,12]{2,1,0:T(2,128)}, f32[12,2,48]{2,1,0:T(2,128)}, f32[12,2,48]{2,1,...) custom-call(f32[2,6,24,192]{3,2,1,0:T(8,128)} %get-tuple-element.21.refs_0_, ...), custom_call_target="tpu_custom_call" | custom-call | tf_op jit(solution)/shard_map/pallas_call | solution.py:684

commit v8 on v7

--- a/solution.py
+++ b/solution.py
@@ -384,6 +384,32 @@
     parts, got_a, sum_a, got_b = (rest[4 * i : 4 * i + 4] for i in range(4))
     rest = rest[16:]
     sent_d, got_d, sent_e, got_e, load, send_h, recv_h, send_a, recv_a, send_b, recv_b, send_d, recv_d = rest
+    core = lax.axis_index("lon_2")
+    chip, chip_count, chip_at = ring(LON[:2])
+    lat_me, lat_count, lat_at = ring(LAT)
+    lon_me, lon_count, lon_at = ring(LON)
+    core_peer = {"lon_2": 1 - core}
+
+    def chip_peer(o):
+        return lax.rem(chip + o, chip_count)
+
+    def lat_peer(o):
+        return lax.rem(lat_me + o, lat_count)
+
+    def neighbours(way):
+        lat = lat_at(lax.rem(lat_me + way + lat_count, lat_count))
+        lon = lon_at(lax.rem(lon_me + way + lon_count, lon_count))
+        return lat, lon, {**lat, **lon}
+
+    lower, upper = neighbours(-1), neighbours(1)
+    peers = (
+        [lat_at(lat_peer(o)) for o in farthest_first(lat_count)]
+        + [chip_at(chip_peer(o)) for o in farthest_first(chip_count)]
+        + [*reversed(lower), *reversed(upper), core_peer]
+    )
+    barrier = pltpu.get_barrier_semaphore()
+    for device in peers:
+        pl.semaphore_signal(barrier, inc=1, device_id=device, device_id_type=MESH)
     loads = [
         pltpu.make_async_copy(source, target, load.at[i])
         for i, (source, target) in enumerate(
@@ -403,32 +429,6 @@
     ]
     for copy in loads:
         copy.start()
-    core = lax.axis_index("lon_2")
-    chip, chip_count, chip_at = ring(LON[:2])
-    lat_me, lat_count, lat_at = ring(LAT)
-    lon_me, lon_count, lon_at = ring(LON)
-    core_peer = {"lon_2": 1 - core}
-
-    def chip_peer(o):
-        return lax.rem(chip + o, chip_count)
-
-    def lat_peer(o):
-        return lax.rem(lat_me + o, lat_count)
-
-    def neighbours(way):
-        lat = lat_at(lax.rem(lat_me + way + lat_count, lat_count))
-        lon = lon_at(lax.rem(lon_me + way + lon_count, lon_count))
-        return lat, lon, {**lat, **lon}
-
-    lower, upper = neighbours(-1), neighbours(1)
-    peers = (
-        [*lower, *upper, core_peer]
-        + [chip_at(chip_peer(o)) for o in range(1, chip_count)]
-        + [lat_at(lat_peer(o)) for o in range(1, lat_count)]
-    )
-    barrier = pltpu.get_barrier_semaphore()
-    for device in peers:
-        pl.semaphore_signal(barrier, inc=1, device_id=device, device_id_type=MESH)
 
     def send(source, target, sems, i, device):
         copy = pltpu.make_async_remote_copy(
@@ -473,20 +473,19 @@
     for copy in loads[5:7]:
         copy.wait()
     first_gains, second_gains = gains[0], gains[1]
-    early = []
-
-    def open_halo():
+
+    def rest_of_loads():
         for copy in loads[7:]:
             copy.wait()
-        pl.semaphore_wait(barrier, len(peers))
-        early.extend(exchange(0, lower))
 
     q, k, v, o, m, g, slope = forward(
-        x, first_gains, w_qkv[0], w_proj.at[0], w_fc1.at[0], bias_ref, None, prob_first, open_halo
+        x, first_gains, w_qkv[0], w_proj.at[0], w_fc1.at[0], bias_ref, None, prob_first, rest_of_loads
     )
     out = quarters(m + nt(g, w_fc2[0]))
     fill(1, out)
-    flights = early + exchange(1, lower)
+    pl.semaphore_wait(barrier, len(peers))
+    flights = exchange(1, lower)
+    later_flights = exchange(0, lower)
     own_ref[0] = padded([out[key] for key in OWN], 112)
     own_ref[1] = padded([given[key] for key in OWN], 112)
     for ref, value in ((q_ref, q), (k_ref, k), (v_ref, v), (o_ref, o), (m_ref, m), (g_ref, g), (slope_ref, slope())):
@@ -502,10 +501,12 @@
     for flight in flights:
         flight.wait()
     u = shifted(arrived(1, own_ref.at[0]))
-    cot_u = shifted(arrived(0, own_ref.at[1]))
     q, k, v, o, m, g, slope = forward(
         u, second_gains, w_qkv[1], w_proj.at[1], w_fc1.at[1], bias_ref, allowed, prob_second
     )
+    for flight in later_flights:
+        flight.wait()
+    cot_u = shifted(arrived(0, own_ref.at[1]))
     y2, y1, unit2, scale2 = back_mlp(cot_u, m, slope(), w_fc2[1])
     dm, gain2 = back_middle(cot_u, y1, unit2, scale2, second_gains[1:2], w_fc1[1])
     yp = dm.astype(BF)

time: 48.5 us -> 49.3 us (1.016)
  Pallas kernels: 47.8 us -> 48.6 us
    pallas_call x1, Pallas kernels: 46 us -> 46.8 us  [body(): pl.pallas_call(kernel, in_specs=[pl.BlockSpec(memory_space=pltpu.HBM)] *...]
where the time goes in v8:
time: 49.3 us; the launch traced here: 49.2 us
  Pallas kernels  48.6 us (99%)
  between operations  0.64 us (1%)
    pallas_call x1, Pallas kernels, body(): pl.pallas_call(kernel, in_specs=[pl.BlockSpec(memory_space=pltpu.HBM)] *...  46.8 us
    pallas_call x1, Pallas kernels, body(): pl.pallas_call(hand_over, in_specs=[vmem] * 7, out_specs=[vmem] * 7, out_...  1.77 us

profile of v8, /device:TPU:2, one launch (start us, length us, event | category | flops | bytes accessed | tf_op | source)
XLA Modules:
  0.0 49.2 jit_solution(372927950487233386)
XLA Ops:
  0.6 46.8 %shard_map.153 = (f32[2,6,24,192]{3,2,1,0:T(8,128)}, f32[12,2,36]{2,1,0:T(2,128)}, f32[12,2,12]{2,1,0:T(2,128)}, f32[12,2,48]{2,1,0:T(2,128)}, f32[12,2,48]{2,1,...) custom-call(bf16[2,6,24,192]{3,2,1,0:T(8,128)(2,1)} %state_in.1, bf16[2,6,24,192]{3,2,1,0:T(8,128)(2,1)} %cot_in.1, ...), custom_call_target="tpu_custom_call" | custom-call | tf_op jit(solution)/shard_map/pallas_call | solution.py:674
  47.4 1.8 %shard_map.154 = (f32[2,6,24,192]{3,2,1,0:T(8,128)}, f32[12,2,36]{2,1,0:T(2,128)}, f32[12,2,12]{2,1,0:T(2,128)}, f32[12,2,48]{2,1,0:T(2,128)}, f32[12,2,48]{2,1,...) custom-call(f32[2,6,24,192]{3,2,1,0:T(8,128)} %get-tuple-element.21.refs_0_, ...), custom_call_target="tpu_custom_call" | custom-call | tf_op jit(solution)/shard_map/pallas_call | solution.py:685

commit v9 on v8

--- a/solution.py
+++ b/solution.py
@@ -239,11 +239,10 @@
     return q.astype(BF), k.astype(BF), v.astype(BF), o, m, g, slope
 
 
-def back_mlp(cot, m, slope, w_fc2):
-    unit, scale = normed(m)
+def back_mlp(cot, slope, w_fc2):
     y2 = cot.astype(BF)
     dg = nn(y2, w_fc2).astype(BF).astype(F32)
-    return y2, (dg * slope.astype(F32)).astype(BF), unit, scale
+    return y2, (dg * slope.astype(F32)).astype(BF)
 
 
 def back_middle(cot, y1, unit, scale, gain, w_fc1):
@@ -378,8 +377,8 @@
 def kernel(state_in, cot_in, order_in, lanes_in, table_in, gains_in, w_qkv_in, w_proj_in, w_fc1_in, w_fc2_in,
            du_ref, qkv_ref, proj_ref, fc1_ref, fc2_ref, gain_ref, table_ref,
            state, cot, order, lanes, table, gains, w_qkv, w_proj, w_fc1, w_fc2,
-           q_ref, k_ref, v_ref, o_ref, m_ref, g_ref, slope_ref, prob_first, prob_second, bias_ref, grad_ref,
-           mine_ref, own_ref, *rest):
+           q_ref, k_ref, v_ref, o_ref, g_ref, slope_ref, prob_first, prob_second, bias_ref, grad_ref,
+           mine_ref, own_ref, unit_ref, scale_ref, *rest):
     halos, rest = rest[:18], rest[18:]
     parts, got_a, sum_a, got_b = (rest[4 * i : 4 * i + 4] for i in range(4))
     rest = rest[16:]
@@ -488,8 +487,11 @@
     later_flights = exchange(0, lower)
     own_ref[0] = padded([out[key] for key in OWN], 112)
     own_ref[1] = padded([given[key] for key in OWN], 112)
-    for ref, value in ((q_ref, q), (k_ref, k), (v_ref, v), (o_ref, o), (m_ref, m), (g_ref, g), (slope_ref, slope())):
+    for ref, value in ((q_ref, q), (k_ref, k), (v_ref, v), (o_ref, o), (g_ref, g), (slope_ref, slope())):
         ref[...] = value
+
+    for i, value in enumerate((x, m)):
+        unit_ref[i], scale_ref[i] = normed(value)
 
     expand_bias(table_of(1), lanes[...], True, bias_ref)
     row = lax.broadcasted_iota(jnp.int32, (WIN, WIN), 0)
@@ -507,7 +509,8 @@
     for flight in later_flights:
         flight.wait()
     cot_u = shifted(arrived(0, own_ref.at[1]))
-    y2, y1, unit2, scale2 = back_mlp(cot_u, m, slope(), w_fc2[1])
+    y2, y1 = back_mlp(cot_u, slope(), w_fc2[1])
+    unit2, scale2 = normed(m)
     dm, gain2 = back_middle(cot_u, y1, unit2, scale2, second_gains[1:2], w_fc1[1])
     yp = dm.astype(BF)
     d_qkv = back_attention(nt(yp, w_proj[1]).astype(BF), q, k, v, prob_second, grad_ref)
@@ -564,14 +567,15 @@
         flight.wait()
     start_b(1)
     cot_x = whole_block(arrived(2, mine_ref))
-    y2, y1, unit2, scale2 = back_mlp(cot_x, m_ref[...], slope_ref[...], w_fc2[0])
+    y2, y1 = back_mlp(cot_x, slope_ref[...], w_fc2[0])
+    unit2, scale2 = unit_ref[1], scale_ref[1]
     pack_mlp(*mlp_grads(y2, y1, g_ref[...], unit2, first_gains[1:2]), parts[2])
     start_a(2)
     dm, gain2 = back_middle(cot_x, y1, unit2, scale2, first_gains[1:2], w_fc1[0])
     yp = dm.astype(BF)
     do = nt(yp, w_proj[0]).astype(BF)
     d_qkv = back_attention(do, q_ref[...], k_ref[...], v_ref[...], prob_first, grad_ref, lambda: start_b(2))
-    unit1, scale1 = normed(nn(order[...], flat_rows(state).astype(BF)))
+    unit1, scale1 = unit_ref[0], scale_ref[0]
     du, gain1 = back_input(dm, d_qkv, unit1, scale1, first_gains[0:1], w_qkv[0])
     pack_attention(
         qkv_grads(d_qkv, unit1, first_gains[0:1]), tn(yp, o_ref[...]), reduce_bias(grad_ref, lanes[...], False),
@@ -653,7 +657,6 @@
         qkv_weight, proj_weight, fc1_weight, jnp.swapaxes(fc2_weight, 1, 2),
     )
     buffers = [(a.shape, a.dtype) for a in args] + [((TOK, DIM), BF)] * 4 + [
-        ((TOK, DIM), F32),
         ((TOK, HID), BF),
         ((TOK, HID), BF),
         ((2, HEADS * WIN, WIN), BF),
@@ -662,6 +665,8 @@
         ((2, 8 * WIN, 128), F32),
         ((112, DIM), F32),
         ((2, 112, DIM), BF),
+        ((2, TOK, DIM), F32),
+        ((2, TOK, 1), F32),
     ]
     buffers += [((112, DIM), BF), ((48, DIM), BF), ((48, DIM), BF)] * 6
     rows = (144, 96, 144, 96)

time: 49.3 us -> 49 us (level)
  no operation moved by 1% of the time
where the time goes in v9:
time: 49 us; the launch traced here: 48.8 us
  Pallas kernels  48.2 us (98%)
  between operations  0.64 us (1%)
    pallas_call x1, Pallas kernels, body(): pl.pallas_call(kernel, in_specs=[pl.BlockSpec(memory_space=pltpu.HBM)] *...  46.4 us
    pallas_call x1, Pallas kernels, body(): pl.pallas_call(hand_over, in_specs=[vmem] * 7, out_specs=[vmem] * 7, out_...  1.77 us

profile of v9, /device:TPU:2, one launch (start us, length us, event | category | flops | bytes accessed | tf_op | source)
XLA Modules:
  0.0 48.8 jit_solution(4764530839642353636)
XLA Ops:
  0.6 46.4 %shard_map.153 = (f32[2,6,24,192]{3,2,1,0:T(8,128)}, f32[12,2,36]{2,1,0:T(2,128)}, f32[12,2,12]{2,1,0:T(2,128)}, f32[12,2,48]{2,1,0:T(2,128)}, f32[12,2,48]{2,1,...) custom-call(bf16[2,6,24,192]{3,2,1,0:T(8,128)(2,1)} %state_in.1, bf16[2,6,24,192]{3,2,1,0:T(8,128)(2,1)} %cot_in.1, ...), custom_call_target="tpu_custom_call" | custom-call | tf_op jit(solution)/shard_map/pallas_call | solution.py:679
  47.1 1.8 %shard_map.154 = (f32[2,6,24,192]{3,2,1,0:T(8,128)}, f32[12,2,36]{2,1,0:T(2,128)}, f32[12,2,12]{2,1,0:T(2,128)}, f32[12,2,48]{2,1,0:T(2,128)}, f32[12,2,48]{2,1,...) custom-call(f32[2,6,24,192]{3,2,1,0:T(8,128)} %get-tuple-element.21.refs_0_, ...), custom_call_target="tpu_custom_call" | custom-call | tf_op jit(solution)/shard_map/pallas_call | solution.py:690
